TPU v7x, 32 devices: a whole 2x2x4 slice. The times are simulated.
32 devices in a mesh: ctx: 8 (over z, x), tp: 4 (over y, core).
Axes of the slice: x: 2, y: 2, z: 4, core: 2. Of those that a mesh axis runs over, the one named last changes fastest.
Arguments:
- gate_q: bfloat16 [1024, 2048], P('tp', 'ctx'), may hold values from -6 to 6
- key_k: bfloat16 [1024, 2048], P('tp', 'ctx'), may hold values from -6 to 6
- value_v: bfloat16 [1024, 2048], P('tp', 'ctx'), may hold values from -6 to 6
- filter_taps: float32 [1024, 2048], P('tp', 'ctx'), may hold values from -1 to 1
- skip_bias: float32 [1024], P('tp'), may hold values from 0.5 to 1.5
- w_out: bfloat16 [1024, 4096], P('tp'), may hold values from -0.25 to 0.25
Outputs:
- mixed: bfloat16 [4096, 2048], P('tp', 'ctx')
All inputs are finite; a program needn't handle non-finite values.
Results may differ from a plain program's by a relative error of at most 0.018.
Values may be sent and summed in bfloat16 or wider, within the bound.
No kernel may reach another device: no remote copies, remote signals or barrier semaphores. Data moves between devices by JAX's collectives and lax.ppermute only.
A program may use at most 64 MiB of HBM per device.

v0:
```python
import math

import jax
import jax.numpy as jnp
from jax import lax
from jax.sharding import PartitionSpec as P

TOP_ACCURACY = lax.Precision.HIGHEST


def unit_circle(phase_num, period):
    radians = (phase_num % period).astype(jnp.float32) * (2.0 * math.pi / period)
    return (jnp.cos(radians), jnp.sin(radians))


def device_table(shards):
    freq_idx = lax.broadcasted_iota(jnp.int32, (2 * shards, shards), 0)
    pos_idx = lax.broadcasted_iota(jnp.int32, (2 * shards, shards), 1)
    return unit_circle(freq_idx * pos_idx, 2 * shards)


def device_forward(segment_list, shards):
    cosine_factor, sine_factor = device_table(shards)
    real_output = jnp.einsum("yo,hoq->hyq", cosine_factor, segment_list, precision=TOP_ACCURACY)
    imaginary_output = -jnp.einsum("yo,hoq->hyq", sine_factor, segment_list, precision=TOP_ACCURACY)
    return (real_output, imaginary_output)


def device_inverse(real_input, imaginary_input, shards, length):
    cosine_factor, sine_factor = device_table(shards)
    real_output = jnp.einsum("lg,ilr->igr", cosine_factor, real_input, precision=TOP_ACCURACY)
    real_output = real_output - jnp.einsum(
        "lg,ilr->igr", sine_factor, imaginary_input, precision=TOP_ACCURACY
    )
    return real_output / length


def complex_mul(left_re, left_im, right_re, right_im):
    return (left_re * right_re - left_im * right_im, left_re * right_im + left_im * right_re)


def spectral(sig_re, sig_im, tap_re, tap_im, freq_rows, length):
    seq_dev = sig_re.shape[2]
    positions = lax.iota(jnp.int32, seq_dev)
    twist_re, twist_sin = unit_circle(freq_rows[:, None] * positions[None, :], length)
    grid_k = lax.broadcasted_iota(jnp.int32, (seq_dev, seq_dev), 0)
    grid_n = lax.broadcasted_iota(jnp.int32, (seq_dev, seq_dev), 1)
    dft_re, dft_sin = unit_circle(grid_k * grid_n, seq_dev)

    def forward(part_re, part_im):
        part_re, part_im = complex_mul(part_re, part_im, twist_re, -twist_sin)
        out_re = jnp.einsum("kn,cjn->cjk", dft_re, part_re, precision=TOP_ACCURACY)
        out_re = out_re + jnp.einsum("kn,cjn->cjk", dft_sin, part_im, precision=TOP_ACCURACY)
        out_im = jnp.einsum("kn,cjn->cjk", dft_re, part_im, precision=TOP_ACCURACY)
        out_im = out_im - jnp.einsum("kn,cjn->cjk", dft_sin, part_re, precision=TOP_ACCURACY)
        return (out_re, out_im)

    sig_re, sig_im = forward(sig_re, sig_im)
    tap_re, tap_im = forward(tap_re, tap_im)
    prod_re, prod_im = complex_mul(sig_re, sig_im, tap_re, tap_im)
    back_re = jnp.einsum("kn,cjk->cjn", dft_re, prod_re, precision=TOP_ACCURACY)
    back_re = back_re - jnp.einsum("kn,cjk->cjn", dft_sin, prod_im, precision=TOP_ACCURACY)
    back_im = jnp.einsum("kn,cjk->cjn", dft_re, prod_im, precision=TOP_ACCURACY)
    back_im = back_im + jnp.einsum("kn,cjk->cjn", dft_sin, prod_re, precision=TOP_ACCURACY)
    return complex_mul(back_re, back_im, twist_re, twist_sin)


def body(gate_q, key_k, value_v, filter_taps, skip_bias, w_out):
    channels, seq_dev = key_k.shape
    shards = lax.axis_size("ctx")
    length = 2 * shards * seq_dev
    signal = key_k.astype(jnp.float32) * value_v.astype(jnp.float32)
    signal_cube = signal.reshape(channels, 1, seq_dev)
    taps_cube = filter_taps.reshape(channels, 1, seq_dev)
    segment_list = (
        lax.all_to_all(signal_cube, "ctx", split_axis=2, concat_axis=1, tiled=True),
        lax.all_to_all(taps_cube, "ctx", split_axis=2, concat_axis=1, tiled=True),
    )
    sig_re, sig_im = device_forward(segment_list[0], shards)
    tap_re, tap_im = device_forward(segment_list[1], shards)
    sig_re, sig_im, tap_re, tap_im = (
        lax.all_to_all(sig_re, "ctx", split_axis=1, concat_axis=2, tiled=True),
        lax.all_to_all(sig_im, "ctx", split_axis=1, concat_axis=2, tiled=True),
        lax.all_to_all(tap_re, "ctx", split_axis=1, concat_axis=2, tiled=True),
        lax.all_to_all(tap_im, "ctx", split_axis=1, concat_axis=2, tiled=True),
    )
    freq_rows = 2 * lax.axis_index("ctx") + lax.iota(jnp.int32, 2)
    prod_re, prod_im = spectral(sig_re, sig_im, tap_re, tap_im, freq_rows, length)
    segment_list = (
        lax.all_to_all(prod_re, "ctx", split_axis=2, concat_axis=1, tiled=True),
        lax.all_to_all(prod_im, "ctx", split_axis=2, concat_axis=1, tiled=True),
    )
    values = device_inverse(segment_list[0], segment_list[1], shards, length)
    convolved = lax.all_to_all(values, "ctx", split_axis=1, concat_axis=2, tiled=True)
    convolved = convolved.reshape(channels, seq_dev)
    gated_vals = (gate_q.astype(jnp.float32) * (convolved + skip_bias[:, None] * signal)).astype(
        jnp.bfloat16
    )
    return lax.psum_scatter(
        lax.dot_general(
            w_out, gated_vals, (((0,), (0,)), ((), ())), preferred_element_type=jnp.float32
        ).astype(jnp.bfloat16),
        "tp",
        scatter_dimension=0,
        tiled=True,
    )


def solution(mesh):
    return jax.shard_map(
        body,
        mesh=mesh,
        in_specs=(
            P("tp", "ctx"),
            P("tp", "ctx"),
            P("tp", "ctx"),
            P("tp", "ctx"),
            P("tp"),
            P("tp", None),
        ),
        out_specs=P("tp", "ctx"),
        check_vma=False,
    )
```

profile of v0, /device:TPU:0, one launch (start us, length us, event | category | flops | bytes accessed | tf_op | source)
XLA Modules:
  0.0 228.4 jit_solution(5767262555015712715)
XLA Ops:
  6.5 1.9 copy.102
  8.5 7.3 %all-to-all-start.3 = ((f32[256,1,256]{0,1,2:T(1,128)}), f32[256,1,256]{0,1,2:T(1,128)S(1)}, u32[]{:S(2)}, u32[]{:S(2)}) async-start(f32[256,1,256]{0,1,2:T(1,128)} %copy.102), calls=%async_computation.3 | async-start | bytes 524288 | tf_op jit(solution)/shard_map/all_to_all | solution.py:77
  15.7 1.0 copy.70
  16.7 1.0 copy.71
  17.8 1.0 copy.72
  18.8 5.9 %all-to-all-done.3 = f32[256,1,256]{0,1,2:T(1,128)S(1)} async-done(((f32[256,1,256]{0,1,2:T(1,128)}), f32[256,1,256]{0,1,2:T(1,128)S(1)}, u32[]{:S(2)}, u32[]{:S(2)}) %all-to-all-start.3) | async-done | bytes 262176 | tf_op jit(solution)/shard_map/all_to_all | solution.py:77
  24.6 3.6 %all-to-all-start = ((f32[256,1,256]{0,1,2:T(1,128)}), f32[256,1,256]{0,1,2:T(1,128)S(1)}, u32[]{:S(2)}, u32[]{:S(2)}) async-start(f32[256,1,256]{0,1,2:T(1,128)} %copy.72), calls=%async_computation | async-start | bytes 524288 | tf_op jit(solution)/shard_map/all_to_all | solution.py:76
  28.3 0.7 fusion.1
  29.0 1.1 copy.89
  30.1 6.7 %all-to-all-done = f32[256,1,256]{0,1,2:T(1,128)S(1)} async-done(((f32[256,1,256]{0,1,2:T(1,128)}), f32[256,1,256]{0,1,2:T(1,128)S(1)}, u32[]{:S(2)}, u32[]{:S(2)}) %all-to-all-start) | async-done | bytes 262176 | tf_op jit(solution)/shard_map/all_to_all | solution.py:76
  36.8 0.7 copy-done.7
  37.5 3.6 %all-to-all-start.5 = ((f32[256,16,32]{0,2,1:T(8,128)}), f32[256,16,32]{0,2,1:T(8,128)S(1)}, u32[]{:S(2)}, u32[]{:S(2)}) async-start(f32[256,16,32]{0,2,1:T(8,128)} %copy.89), calls=%async_computation.5 | async-start | bytes 1048576 | tf_op jit(solution)/shard_map/all_to_all | solution.py:85
  41.1 0.7 convolution_bitcast_fusion
  41.8 1.1 copy.85
  42.9 12.2 %all-to-all-done.5 = f32[256,16,32]{0,2,1:T(8,128)S(1)} async-done(((f32[256,16,32]{0,2,1:T(8,128)}), f32[256,16,32]{0,2,1:T(8,128)S(1)}, u32[]{:S(2)}, u32[]{:S(2)}) %all-to-all-start.5) | async-done | bytes 524320 | tf_op jit(solution)/shard_map/all_to_all | solution.py:85
  55.2 3.6 %all-to-all-start.4 = ((f32[256,16,32]{0,2,1:T(8,128)}), f32[256,16,32]{0,2,1:T(8,128)S(1)}, u32[]{:S(2)}, u32[]{:S(2)}) async-start(f32[256,16,32]{0,2,1:T(8,128)} %copy.85), calls=%async_computation.4 | async-start | bytes 1048576 | tf_op jit(solution)/shard_map/all_to_all | solution.py:84
  58.8 1.0 copy.103
  59.8 0.7 fusion.2
  60.5 1.1 copy.78
  61.6 11.5 %all-to-all-done.4 = f32[256,16,32]{0,2,1:T(8,128)S(1)} async-done(((f32[256,16,32]{0,2,1:T(8,128)}), f32[256,16,32]{0,2,1:T(8,128)S(1)}, u32[]{:S(2)}, u32[]{:S(2)}) %all-to-all-start.4) | async-done | bytes 524320 | tf_op jit(solution)/shard_map/all_to_all | solution.py:84
  73.1 4.1 %all-to-all-start.2 = ((f32[256,16,32]{0,2,1:T(8,128)}), f32[256,16,32]{0,2,1:T(8,128)}, u32[]{:S(2)}, u32[]{:S(2)}) async-start(f32[256,16,32]{0,2,1:T(8,128)} %copy.78), calls=%async_computation.2 | async-start | bytes 1048576 | tf_op jit(solution)/shard_map/all_to_all | solution.py:83
  77.2 0.7 convolution_bitcast_fusion.1
  78.0 1.1 copy.74
  79.1 12.3 %all-to-all-done.2 = f32[256,16,32]{0,2,1:T(8,128)} async-done(((f32[256,16,32]{0,2,1:T(8,128)}), f32[256,16,32]{0,2,1:T(8,128)}, u32[]{:S(2)}, u32[]{:S(2)}) %all-to-all-start.2) | async-done | bytes 524320 | tf_op jit(solution)/shard_map/all_to_all | solution.py:83
  91.3 4.3 %all-to-all-start.1 = ((f32[256,16,32]{0,2,1:T(8,128)}), f32[256,16,32]{0,2,1:T(8,128)}, u32[]{:S(2)}, u32[]{:S(2)}) async-start(f32[256,16,32]{0,2,1:T(8,128)} %copy.74), calls=%async_computation.1 | async-start | bytes 1048576 | tf_op jit(solution)/shard_map/all_to_all | solution.py:82
  95.7 0.1 fusion.74
  95.8 0.8 copy.90
  96.7 1.2 copy.91
  97.9 0.8 copy.86
  98.7 2.1 copy.87
  100.8 1.9 copy.79
  102.7 1.2 copy.80
  103.9 3.4 %fusion.20 = f32[256,2,256]{2,0,1:T(8,128)} fusion(f32[256,2,256]{2,0,1:T(8,128)S(1)} %copy.91, f32[256,2,256]{2,0,1:T(8,128)} %copy.87, f32[2,256]{1,0:T(2,128)S(1)} %get-tuple-element.10, f32[2,256]{1,0:T(2,128)S(1)} %get-tuple-element.11), kind=kOutput, calls=%fused_computation.44 | convolution fusion | flops 403963904 | bytes 1576960 | tf_op jit(solution)/shard_map/kn,cjn->cjk/dot_general | solution.py:54
  107.3 3.4 %fusion.24 = f32[256,2,256]{2,0,1:T(8,128)} fusion(f32[256,2,256]{2,0,1:T(8,128)S(1)} %copy.91, f32[256,2,256]{2,0,1:T(8,128)} %copy.87, f32[2,256]{1,0:T(2,128)S(1)} %get-tuple-element.10, f32[2,256]{1,0:T(2,128)S(1)} %get-tuple-element.11), kind=kOutput, calls=%fused_computation.48 | convolution fusion | flops 403963904 | bytes 1576960 | tf_op jit(solution)/shard_map/kn,cjn->cjk/dot_general | solution.py:52
  110.8 1.9 copy.75
  112.6 2.1 copy.76
  114.7 2.7 %fusion.22 = f32[256,2,256]{2,0,1:T(8,128)S(1)} fusion(f32[256,2,256]{2,0,1:T(8,128)S(1)} %copy.80, f32[256,2,256]{2,0,1:T(8,128)} %copy.76, f32[2,256]{1,0:T(2,128)S(1)} %get-tuple-element.10, f32[2,256]{1,0:T(2,128)S(1)} %get-tuple-element.11), kind=kOutput, calls=%fused_computation.46 | convolution fusion | flops 403963904 | bytes 1576960 | tf_op jit(solution)/shard_map/kn,cjn->cjk/dot_general | solution.py:54
  117.4 2.7 %fusion.26 = f32[256,2,256]{2,0,1:T(8,128)S(1)} fusion(f32[256,2,256]{2,0,1:T(8,128)S(1)} %copy.80, f32[256,2,256]{2,0,1:T(8,128)} %copy.76, f32[2,256]{1,0:T(2,128)S(1)} %get-tuple-element.10, f32[2,256]{1,0:T(2,128)S(1)} %get-tuple-element.11), kind=kOutput, calls=%fused_computation.50 | convolution fusion | flops 403963904 | bytes 1576960 | tf_op jit(solution)/shard_map/kn,cjn->cjk/dot_general | solution.py:52
  120.1 1.6 convolution_subtract_fusion.1
  121.7 1.6 convolution_add_fusion.1
  123.3 1.8 convolution_add_fusion.2
  125.2 1.6 multiply_subtract_fusion.1
  126.8 1.6 fusion.18
  128.3 1.6 fusion.16
  129.9 1.6 convolution_subtract_fusion
  131.5 1.6 multiply_add_fusion
  133.1 1.0 copy.97
  134.1 5.7 %all-to-all-start.7 = ((f32[256,2,256]{0,1,2:T(2,128)}), f32[256,2,256]{0,1,2:T(2,128)S(1)}, u32[]{:S(2)}, u32[]{:S(2)}) async-start(f32[256,2,256]{0,1,2:T(2,128)} %copy.97), calls=%async_computation.7 | async-start | bytes 1048576 | tf_op jit(solution)/shard_map/all_to_all | solution.py:91
  139.8 1.0 copy.94
  140.8 12.3 %all-to-all-done.7 = f32[256,2,256]{0,1,2:T(2,128)S(1)} async-done(((f32[256,2,256]{0,1,2:T(2,128)}), f32[256,2,256]{0,1,2:T(2,128)S(1)}, u32[]{:S(2)}, u32[]{:S(2)}) %all-to-all-start.7) | async-done | bytes 524320 | tf_op jit(solution)/shard_map/all_to_all | solution.py:91
  153.2 3.7 %all-to-all-start.6 = ((f32[256,2,256]{0,1,2:T(2,128)}), f32[256,2,256]{0,1,2:T(2,128)S(1)}, u32[]{:S(2)}, u32[]{:S(2)}) async-start(f32[256,2,256]{0,1,2:T(2,128)} %copy.94), calls=%async_computation.6 | async-start | bytes 1048576 | tf_op jit(solution)/shard_map/all_to_all | solution.py:90
  156.9 1.2 copy.99
  158.1 1.4 all_to_all.130
  159.5 11.1 %all-to-all-done.6 = f32[256,2,256]{0,1,2:T(2,128)S(1)} async-done(((f32[256,2,256]{0,1,2:T(2,128)}), f32[256,2,256]{0,1,2:T(2,128)S(1)}, u32[]{:S(2)}, u32[]{:S(2)}) %all-to-all-start.6) | async-done | bytes 524320 | tf_op jit(solution)/shard_map/all_to_all | solution.py:90
  170.7 0.4 copy.96
  171.1 1.2 all_to_all.126
  172.3 1.5 fusion.56
  173.7 0.4 fusion.4
  174.2 0.8 copy.100
  175.0 3.6 %all-to-all-start.8 = ((f32[256,8,32]{0,2,1:T(8,128)}), f32[256,8,32]{0,2,1:T(8,128)S(1)}, u32[]{:S(2)}, u32[]{:S(2)}) async-start(f32[256,8,32]{0,2,1:T(8,128)} %copy.100), calls=%async_computation.8 | async-start | bytes 524288 | tf_op jit(solution)/shard_map/all_to_all | solution.py:94
  178.8 8.2 %all-to-all-done.8 = f32[256,8,32]{0,2,1:T(8,128)S(1)} async-done(((f32[256,8,32]{0,2,1:T(8,128)}), f32[256,8,32]{0,2,1:T(8,128)S(1)}, u32[]{:S(2)}, u32[]{:S(2)}) %all-to-all-start.8) | async-done | bytes 262176 | tf_op jit(solution)/shard_map/all_to_all | solution.py:94
  187.0 2.1 fusion
  189.1 30.5 %reduce-scatter.2.cloned.1.call-done = bf16[1024,256]{0,1:T(8,128)(2,1)} async-done(((bf16[4096,256]{0,1:T(8,128)(2,1)}), bf16[1024,256]{0,1:T(8,128)(2,1)}) %reduce-scatter.2.cloned.1.call-update) | async-done | bytes 524304 | tf_op jit(solution)/shard_map/reduce_scatter | solution.py:99
  219.6 2.0 copy.101
  (29 shorter events, 0.4 us)
Async XLA Ops:
  6.5 180.5 %copy-start = (bf16[256,4096]{1,0:T(8,128)(2,1)S(1)}, bf16[256,4096]{1,0:T(8,128)(2,1)}, u32[]{:S(2)}) copy-start(bf16[256,4096]{1,0:T(8,128)(2,1)} %param.11) | copy-start | bytes 6291460
  8.5 16.2 %all-to-all-start.3 = ((f32[256,1,256]{0,1,2:T(1,128)}), f32[256,1,256]{0,1,2:T(1,128)S(1)}, u32[]{:S(2)}, u32[]{:S(2)}) async-start(f32[256,1,256]{0,1,2:T(1,128)} %copy.102), calls=%async_computation.3 | async-start | bytes 524288 | tf_op jit(solution)/shard_map/all_to_all | solution.py:77
  17.7 19.1 %copy-start.5 = (bf16[256,256]{0,1:T(8,128)(2,1)}, bf16[256,256]{0,1:T(8,128)(2,1)S(1)}, u32[]{:S(2)}) copy-start(bf16[256,256]{0,1:T(8,128)(2,1)S(1)} %copy.71) | copy-start | bytes 393220
  24.6 12.2 %all-to-all-start = ((f32[256,1,256]{0,1,2:T(1,128)}), f32[256,1,256]{0,1,2:T(1,128)S(1)}, u32[]{:S(2)}, u32[]{:S(2)}) async-start(f32[256,1,256]{0,1,2:T(1,128)} %copy.72), calls=%async_computation | async-start | bytes 524288 | tf_op jit(solution)/shard_map/all_to_all | solution.py:76
  36.8 0.7 copy-start.7
  37.5 17.6 %all-to-all-start.5 = ((f32[256,16,32]{0,2,1:T(8,128)}), f32[256,16,32]{0,2,1:T(8,128)S(1)}, u32[]{:S(2)}, u32[]{:S(2)}) async-start(f32[256,16,32]{0,2,1:T(8,128)} %copy.89), calls=%async_computation.5 | async-start | bytes 1048576 | tf_op jit(solution)/shard_map/all_to_all | solution.py:85
  55.2 17.9 %all-to-all-start.4 = ((f32[256,16,32]{0,2,1:T(8,128)}), f32[256,16,32]{0,2,1:T(8,128)S(1)}, u32[]{:S(2)}, u32[]{:S(2)}) async-start(f32[256,16,32]{0,2,1:T(8,128)} %copy.85), calls=%async_computation.4 | async-start | bytes 1048576 | tf_op jit(solution)/shard_map/all_to_all | solution.py:84
  73.1 18.3 %all-to-all-start.2 = ((f32[256,16,32]{0,2,1:T(8,128)}), f32[256,16,32]{0,2,1:T(8,128)}, u32[]{:S(2)}, u32[]{:S(2)}) async-start(f32[256,16,32]{0,2,1:T(8,128)} %copy.78), calls=%async_computation.2 | async-start | bytes 1048576 | tf_op jit(solution)/shard_map/all_to_all | solution.py:83
  91.3 19.4 %all-to-all-start.1 = ((f32[256,16,32]{0,2,1:T(8,128)}), f32[256,16,32]{0,2,1:T(8,128)}, u32[]{:S(2)}, u32[]{:S(2)}) async-start(f32[256,16,32]{0,2,1:T(8,128)} %copy.74), calls=%async_computation.1 | async-start | bytes 1048576 | tf_op jit(solution)/shard_map/all_to_all | solution.py:82
  114.7 5.4 %copy-start.1 = (f32[256,2,256]{2,0,1:T(8,128)S(1)}, f32[256,2,256]{2,0,1:T(8,128)}, u32[]{:S(2)}) copy-start(f32[256,2,256]{2,0,1:T(8,128)} %copy.87) | copy-start | bytes 1572868
  114.7 5.4 %copy-start.4 = (f32[256,2,256]{2,0,1:T(8,128)S(1)}, f32[256,2,256]{2,0,1:T(8,128)}, u32[]{:S(2)}) copy-start(f32[256,2,256]{2,0,1:T(8,128)} %fusion.20) | copy-start | bytes 1572868
  117.4 4.3 %copy-start.3 = (f32[256,2,256]{2,0,1:T(8,128)S(1)}, f32[256,2,256]{2,0,1:T(8,128)}, u32[]{:S(2)}) copy-start(f32[256,2,256]{2,0,1:T(8,128)} %fusion.24) | copy-start | bytes 1572868
  120.1 3.2 %copy-start.2 = (f32[256,2,256]{2,0,1:T(8,128)S(1)}, f32[256,2,256]{2,0,1:T(8,128)}, u32[]{:S(2)}) copy-start(f32[256,2,256]{2,0,1:T(8,128)} %copy.76) | copy-start | bytes 1572868
  134.1 19.1 %all-to-all-start.7 = ((f32[256,2,256]{0,1,2:T(2,128)}), f32[256,2,256]{0,1,2:T(2,128)S(1)}, u32[]{:S(2)}, u32[]{:S(2)}) async-start(f32[256,2,256]{0,1,2:T(2,128)} %copy.97), calls=%async_computation.7 | async-start | bytes 1048576 | tf_op jit(solution)/shard_map/all_to_all | solution.py:91
  153.2 17.5 %all-to-all-start.6 = ((f32[256,2,256]{0,1,2:T(2,128)}), f32[256,2,256]{0,1,2:T(2,128)S(1)}, u32[]{:S(2)}, u32[]{:S(2)}) async-start(f32[256,2,256]{0,1,2:T(2,128)} %copy.94), calls=%async_computation.6 | async-start | bytes 1048576 | tf_op jit(solution)/shard_map/all_to_all | solution.py:90
  171.1 7.6 %copy-start.8 = (bf16[256,256]{1,0:T(8,128)(2,1)S(1)}, bf16[256,256]{1,0:T(8,128)(2,1)}, u32[]{:S(2)}) copy-start(bf16[256,256]{1,0:T(8,128)(2,1)} %param.6) | copy-start | bytes 393220
  171.1 15.8 %copy-start.6 = (bf16[256,256]{0,1:T(8,128)(2,1)S(1)}, bf16[256,256]{0,1:T(8,128)(2,1)}, u32[]{:S(2)}) copy-start(bf16[256,256]{0,1:T(8,128)(2,1)} %copy-done.5) | copy-start | bytes 393220
  171.1 15.8 %copy-start.9 = (f32[256]{0:T(256)S(1)}, f32[256]{0:T(256)}, u32[]{:S(2)}) copy-start(f32[256]{0:T(256)} %param.10) | copy-start | bytes 3076
  175.0 12.0 %all-to-all-start.8 = ((f32[256,8,32]{0,2,1:T(8,128)}), f32[256,8,32]{0,2,1:T(8,128)S(1)}, u32[]{:S(2)}, u32[]{:S(2)}) async-start(f32[256,8,32]{0,2,1:T(8,128)} %copy.100), calls=%async_computation.8 | async-start | bytes 524288 | tf_op jit(solution)/shard_map/all_to_all | solution.py:94
  178.6 41.0 %reduce-scatter.2.cloned.1.call-start = ((), (), s32[]{:S(2)}) async-start(), calls=%async_computation.10 | async-start | bytes 2621440 | tf_op jit(solution)/shard_map/reduce_scatter | solution.py:99
Sparse Core Ops, SparseCore 0:
  189.2 30.2 reduce-scatter.1
where the time goes:
time: 230 us; the launch traced here: 228 us
  waiting for transfers between devices  111 us (48%)
  starting transfers between devices  39.6 us (17%)
  local copies, waits for them, and re-layouts  32.3 us (14%)
  matrix products  31.9 us (14%)
  between operations  13.7 us (6%)
    reduce_scatter x1, waiting for transfers between devices, body(): lax.psum_scatter(lax.dot_general(w_out, gated_vals, (((0,), (0,)), ((), (...  30.5 us
    all_to_all x1, waiting for transfers between devices, body(): lax.all_to_all(prod_im, 'ctx', split_axis=2, concat_axis=1, tiled=True)  12.3 us
    all_to_all x1, waiting for transfers between devices, body(): lax.all_to_all(sig_im, 'ctx', split_axis=1, concat_axis=2, tiled=True)  12.3 us
    all_to_all x1, waiting for transfers between devices, body(): lax.all_to_all(tap_im, 'ctx', split_axis=1, concat_axis=2, tiled=True)  12.2 us
    all_to_all x1, waiting for transfers between devices, body(): lax.all_to_all(tap_re, 'ctx', split_axis=1, concat_axis=2, tiled=True)  11.5 us
    all_to_all x1, waiting for transfers between devices, body(): lax.all_to_all(prod_re, 'ctx', split_axis=2, concat_axis=1, tiled=True)  11.1 us
    all_to_all x1, waiting for transfers between devices, body(): lax.all_to_all(values, 'ctx', split_axis=1, concat_axis=2, tiled=True)  8.16 us
    all_to_all x1, starting transfers between devices, body(): lax.all_to_all(taps_cube, 'ctx', split_axis=2, concat_axis=1, tiled=True)  7.25 us
  transfers between devices with their start and end apart: 10, of which 9 were waited for; matrix products, arithmetic and copies ran while one was open for 13% of the time, Pallas kernels for 0%

commit v1 on v0

v1 whole, which is shorter than its diff:
```python
import jax
import jax.numpy as jnp
from jax import lax
from jax.experimental import pallas as pl
from jax.experimental.pallas import tpu as pltpu
from jax.sharding import PartitionSpec as P

LANES = 128
PACK = 16
SUB = 64
PHASES = LANES // SUB


def conv_kernel(x_ref, y_ref, taps, rows, sums):
    blocks, _, chans, seq_dev = x_ref.shape
    halves = seq_dev // LANES
    lines = blocks * halves
    length = lines * LANES
    lane = lax.broadcasted_iota(jnp.int32, (chans, LANES), 1)

    taps[:, pl.ds(0, LANES)] = jnp.zeros((chans, LANES), jnp.float32)
    zero = jnp.zeros((chans * lines, LANES), jnp.float32)
    for phase in range(PHASES):
        for chan in range(chans):
            rows[phase, pl.ds(chan * 2 * lines, lines), :] = jnp.zeros((lines, LANES), jnp.float32)
    del zero
    older = [jnp.zeros((chans, LANES), jnp.float32)] * (PHASES - 1)
    for line in range(lines):
        block, half = divmod(line, halves)
        cut = pl.ds(half * LANES, LANES)
        taps[:, pl.ds(LANES + line * LANES, LANES)] = x_ref[block, 1, :, cut].astype(jnp.float32)
        now = [x_ref[block, 0, :, cut].astype(jnp.float32)] + older
        older = now[: PHASES - 1]
        for phase in range(PHASES):
            made = None
            for step in range(PHASES):
                turn = (SUB * (step - phase)) % LANES
                piece = pltpu.roll(now[step], turn, axis=1) if turn else now[step]
                made = piece if made is None else jnp.where(lane >= SUB * step, piece, made)
            rows[phase, pl.ds(lines + line, chans, stride=2 * lines), :] = made

    def channel(chan, _):
        wide = jnp.broadcast_to(taps[pl.ds(chan, 1), :], (PACK, LANES + length))
        skew = pltpu.roll(wide, 0, 1, stride=1, stride_axis=0).astype(jnp.bfloat16)
        parts = []
        for part in range(SUB // PACK):
            parts.append(pltpu.roll(skew, part * PACK, 1) if part else skew)
        toeplitz = jnp.concatenate(
            [part[:, (line + 1) * LANES : (line + 2) * LANES] for line in range(lines) for part in parts], 0
        )
        base = chan * 2 * lines + lines
        left = jnp.concatenate(
            [
                jnp.concatenate(
                    [
                        rows[phase, pl.ds(base - PHASES * step, lines), :].astype(jnp.bfloat16)
                        for step in range(lines // PHASES)
                    ],
                    1,
                )
                for phase in range(PHASES)
            ],
            0,
        )
        total = jnp.dot(left, toeplitz, preferred_element_type=jnp.float32)
        for phase in range(PHASES):
            sums[phase, pl.ds(chan * lines, lines), :] = total[phase * lines : (phase + 1) * lines]
        return 0

    lax.fori_loop(0, chans, channel, 0)

    older = [jnp.zeros((chans, LANES), jnp.float32)] * PHASES
    for line in range(lines):
        block, half = divmod(line, halves)
        now = [sums[phase, pl.ds(line, chans, stride=lines), :] for phase in range(PHASES)]
        value = now[0]
        for phase in range(1, PHASES):
            mixed = jnp.where(lane < LANES - SUB * phase, now[phase], older[phase])
            value = value + pltpu.roll(mixed, SUB * phase, axis=1)
        older = now
        y_ref[block, :, pl.ds(half * LANES, LANES)] = value.astype(jnp.bfloat16)


def convolve(pieces):
    blocks, _, chans, seq_dev = pieces.shape
    lines = blocks * seq_dev // LANES
    return pl.pallas_call(
        conv_kernel,
        out_shape=jax.ShapeDtypeStruct((blocks, chans, seq_dev), jnp.bfloat16),
        in_specs=[pl.BlockSpec(memory_space=pltpu.VMEM)],
        out_specs=pl.BlockSpec(memory_space=pltpu.VMEM),
        scratch_shapes=[
            pltpu.VMEM((chans, LANES + lines * LANES), jnp.float32),
            pltpu.VMEM((PHASES, chans * 2 * lines, LANES), jnp.float32),
            pltpu.VMEM((PHASES, chans * lines, LANES), jnp.float32),
        ],
        compiler_params=pltpu.CompilerParams(vmem_limit_bytes=40 * 2**20),
        cost_estimate=pl.CostEstimate(
            flops=2 * chans * lines * LANES * lines * LANES,
            bytes_accessed=6 * chans * lines * LANES,
            transcendentals=0,
        ),
        name="toeplitz_conv",
    )(pieces)


def body(gate_q, key_k, value_v, filter_taps, skip_bias, w_out):
    channels, seq_dev = key_k.shape
    shards = lax.axis_size("ctx")
    tp = lax.axis_size("tp")
    me = lax.axis_index("tp")
    share = channels // shards
    feats = w_out.shape[1] // tp
    signal = key_k.astype(jnp.float32) * value_v.astype(jnp.float32)
    pieces = jnp.stack(
        [
            signal.astype(jnp.bfloat16).reshape(shards, share, seq_dev),
            filter_taps.astype(jnp.bfloat16).reshape(shards, share, seq_dev),
        ],
        1,
    )

    def own_feats(owner):
        return lax.dynamic_slice_in_dim(w_out, owner * feats, feats, 1)

    weights = [own_feats(me)]
    for step in range(1, tp):
        weights.append(lax.ppermute(own_feats((me + step) % tp), "tp", [(i, (i + step) % tp) for i in range(tp)]))

    pieces = lax.all_to_all(pieces, "ctx", split_axis=0, concat_axis=0, tiled=True)
    convolved = convolve(pieces)
    convolved = lax.all_to_all(convolved, "ctx", split_axis=0, concat_axis=0, tiled=True)
    convolved, *weights = lax.optimization_barrier((convolved, *weights))
    convolved = convolved.reshape(channels, seq_dev).astype(jnp.float32)
    gated_vals = (gate_q.astype(jnp.float32) * (convolved + skip_bias[:, None] * signal)).astype(jnp.bfloat16)
    gathered = lax.all_gather(gated_vals, "tp", axis=0, tiled=True)
    total = None
    for step in range(tp):
        rows = lax.dynamic_slice_in_dim(gathered, ((me - step) % tp) * channels, channels, 0)
        term = lax.dot_general(weights[step], rows, (((0,), (0,)), ((), ())), preferred_element_type=jnp.float32)
        total = term if total is None else total + term
    return total.astype(jnp.bfloat16)


def solution(mesh):
    return jax.shard_map(
        body,
        mesh=mesh,
        in_specs=(P("tp", "ctx"), P("tp", "ctx"), P("tp", "ctx"), P("tp", "ctx"), P("tp"), P("tp", None)),
        out_specs=P("tp", "ctx"),
        check_vma=False,
    )
```

time: 230 us -> 51.8 us (0.23)
  waiting for transfers between devices: 111 us -> 11.4 us
  matrix products: 31.9 us -> 2.21 us
  local copies, waits for them, and re-layouts: 32.3 us -> 2.84 us
  starting transfers between devices: 39.6 us -> 12.9 us
  between operations: 13.7 us -> 0.08 us
  Pallas kernels: 0 us -> 12 us
  blocking collectives: 0 us -> 7.2 us
  other arithmetic: 0.23 us -> 2.82 us
    all_to_all x9 -> x2, waiting for transfers between devices: 80.2 us -> 7.86 us  [the longest x1 4.02 us: body(): lax.all_to_all(pieces, 'ctx', split_axis=0, concat_axis=0, tiled=True)]
    reduce_scatter x1 -> x0, waiting for transfers between devices: 30.5 us -> none  [body(): lax.psum_scatter(lax.dot_general(w_out, gated_vals, (((0,), (0,)), ((), (...]
    dot_general x19 -> x4, matrix products: 31.9 us -> 2.21 us  [body(): lax.dot_general(weights[step], rows, (((0,), (0,)), ((), ())), preferred_...]
    all_to_all x9 -> x2, starting transfers between devices: 39.6 us -> 10.8 us  [the longest x1 7.25 us: body(): lax.all_to_all(pieces, 'ctx', split_axis=0, concat_axis=0, tiled=True)]
    all_to_all x14 -> x0, local copies, waits for them, and re-layouts: 16.3 us -> none  [the longest x2 3.94 us: body(): lax.all_to_all(sig_re, 'ctx', split_axis=1, concat_axis=2, tiled=True)]
    pallas_call x0 -> x1, Pallas kernels: none -> 12 us  [convolve(): pl.pallas_call(conv_kernel, out_shape=jax.ShapeDtypeStruct((blocks, chans...]
    all_gather x0 -> x1, blocking collectives: none -> 7.2 us  [body(): gathered = lax.all_gather(gated_vals, 'tp', axis=0, tiled=True)]
    unnamed x25 -> x8, local copies, waits for them, and re-layouts: 3.84 us -> 0.02 us
  transfers between devices with their start and end apart: 10 -> 5, of which waited for: 9 -> 3; matrix products, arithmetic and copies ran while one was open for 13% -> 5% of each run, Pallas kernels for 0% -> 23%
where the time goes in v1:
time: 51.8 us; the launch traced here: 51.4 us
  starting transfers between devices  12.9 us (25%)
  Pallas kernels  12 us (23%)
  waiting for transfers between devices  11.4 us (22%)
  blocking collectives  7.2 us (14%)
  local copies, waits for them, and re-layouts  2.84 us (5%)
  other arithmetic  2.82 us (5%)
  matrix products  2.21 us (4%)
    pallas_call x1, Pallas kernels, convolve(): pl.pallas_call(conv_kernel, out_shape=jax.ShapeDtypeStruct((blocks, chans...  12 us
    all_to_all x1, starting transfers between devices, body(): lax.all_to_all(pieces, 'ctx', split_axis=0, concat_axis=0, tiled=True)  7.25 us
    all_gather x1, blocking collectives, body(): gathered = lax.all_gather(gated_vals, 'tp', axis=0, tiled=True)  7.2 us
    all_to_all x1, waiting for transfers between devices, body(): lax.all_to_all(pieces, 'ctx', split_axis=0, concat_axis=0, tiled=True)  4.02 us
    all_to_all x1, waiting for transfers between devices, body(): lax.all_to_all(convolved, 'ctx', split_axis=0, concat_axis=0, tiled=True)  3.83 us
    all_to_all x1, starting transfers between devices, body(): lax.all_to_all(convolved, 'ctx', split_axis=0, concat_axis=0, tiled=True)  3.59 us
    ppermute x3, waiting for transfers between devices, body(): lax.ppermute(own_feats((me + step) % tp), 'tp', [(i, (i + step) % tp) for...  3.5 us
    dynamic_slice x1, local copies, waits for them, and re-layouts, own_feats(): return lax.dynamic_slice_in_dim(w_out, owner * feats, feats, 1)  2.82 us
  transfers between devices with their start and end apart: 5, of which 3 were waited for; matrix products, arithmetic and copies ran while one was open for 5% of the time, Pallas kernels for 23%

profile of v1, /device:TPU:0, one launch (start us, length us, event | category | flops | bytes accessed | tf_op | source)
XLA Modules:
  0.0 51.4 jit_solution(17259506455275655755)
XLA Ops:
  0.0 1.0 %convert_element_type.30 = bf16[256,256]{1,0:T(8,128)(2,1)S(1)} convert(f32[256,256]{1,0:T(8,128)} %param.9) | non-fusion elementwise | flops 65536 | bytes 393216 | tf_op jit(solution)/shard_map/convert_element_type | solution.py:118
  1.0 1.0 %fusion.5 = bf16[256,256]{1,0:T(8,128)(2,1)S(1)} fusion(bf16[256,256]{1,0:T(8,128)(2,1)} %param.8, bf16[256,256]{1,0:T(8,128)(2,1)} %param.7), kind=kLoop, calls=%fused_computation.9 | loop fusion | flops 262144 | bytes 393216 | tf_op jit(solution)/shard_map/convert_element_type | solution.py:117
  2.0 0.7 %pad_maximum_fusion = bf16[8,2,32,256]{3,2,1,0:T(8,128)(2,1)} fusion(bf16[8,1,32,256]{3,2,1,0:T(8,128)(2,1)S(1)} %bitcast.9, bf16[8,1,32,256]{3,2,1,0:T(8,128)(2,1)S(1)} %bitcast.10), kind=kLoop, calls=%fused_computation.4 | loop fusion | flops 131072 | bytes 524288 | tf_op jit(solution)/shard_map/stack | solution.py:115
  2.7 7.3 %all-to-all-start = ((bf16[8,2,32,256]{3,2,1,0:T(8,128)(2,1)}), bf16[8,2,32,256]{3,2,1,0:T(8,128)(2,1)S(1)}, u32[]{:S(2)}, u32[]{:S(2)}) async-start(bf16[8,2,32,256]{3,2,1,0:T(8,128)(2,1)} %pad_maximum_fusion), calls=%async_computation | async-start | bytes 524288 | tf_op jit(solution)/shard_map/all_to_all | solution.py:130
  10.0 0.0 copy-start
  10.0 0.0 copy-start.1
  10.0 0.0 copy-start.2
  10.0 0.0 copy-start.3
  10.0 2.8 %constant_dynamic-slice_fusion = (bf16[256,1024]{1,0:T(8,128)(2,1)}, bf16[256,1024]{1,0:T(8,128)(2,1)}, bf16[256,1024]{1,0:T(8,128)(2,1)S(1)}, bf16[256,1024]{1,0:T(8,128)(2,1)S(1)}) fusion(bf16[256,4096]{1,0:T(8,128)(2,1)} %param.11, s32[]{:T(128)S(6)} %select_n.61, s32[]{:T(128)S(6)} %select_n.57, s32[]{:T(128)S(6)} %select_n.55, s32[]{:T(128)S(6)} %select_n.59), kind=kLoop, calls=%fused_computation.21 | loop fusion | bytes 4194320 | tf_op jit(solution)/shard_map/dynamic_slice | solution.py:124
  12.8 0.7 %collective-permute-start.2 = (bf16[256,1024]{1,0:T(8,128)(2,1)}, bf16[256,1024]{1,0:T(8,128)(2,1)S(1)}, u32[]{:S(2)}, u32[]{:S(2)}) collective-permute-start(bf16[256,1024]{1,0:T(8,128)(2,1)} %get-tuple-element.15), channel_id=1, source_target_pairs={{0,3},{1,0},{2,1},{3,2},{4,7},{5,4},{6,5},{7,6},{8,11},{9,8},{10,9... | collective-permute-start | bytes 1572872 | tf_op jit(solution)/shard_map/ppermute | solution.py:128
  13.5 0.0 collective-permute-start
  13.5 1.3 %collective-permute-start.1 = (bf16[256,1024]{1,0:T(8,128)(2,1)S(1)}, bf16[256,1024]{1,0:T(8,128)(2,1)S(1)}, u32[]{:S(2)}, u32[]{:S(2)}) collective-permute-start(bf16[256,1024]{1,0:T(8,128)(2,1)S(1)} %get-tuple-element.18), channel_id=1, source_target_pairs={{0,2},{1,3},{2,0},{3,1},{4,6},{5,7},{6,4},{7,5},{8,10},{9,11},{10,... | collective-permute-start | bytes 1572872 | tf_op jit(solution)/shard_map/ppermute | solution.py:128
  14.8 4.0 %all-to-all-done.x_ref = bf16[8,2,32,256]{3,2,1,0:T(8,128)(2,1)S(1)} async-done(((bf16[8,2,32,256]{3,2,1,0:T(8,128)(2,1)}), bf16[8,2,32,256]{3,2,1,0:T(8,128)(2,1)S(1)}, u32[]{:S(2)}, u32[]{:S(2)}) %all-to-all-start) | async-done | bytes 262176 | tf_op jit(solution)/shard_map/all_to_all | solution.py:130
  18.9 12.0 %toeplitz_conv.1 = bf16[8,32,256]{2,1,0:T(8,128)(2,1)} custom-call(bf16[8,2,32,256]{3,2,1,0:T(8,128)(2,1)S(1)} %all-to-all-done.x_ref), custom_call_target="tpu_custom_call" | custom-call | flops 268435456 | bytes 393216 | tf_op jit(solution)/shard_map/toeplitz_conv/pallas_call | solution.py:87
  30.9 3.6 %all-to-all-start.1 = ((bf16[8,32,256]{2,1,0:T(8,128)(2,1)}), bf16[8,32,256]{2,1,0:T(8,128)(2,1)S(1)}, u32[]{:S(2)}, u32[]{:S(2)}) async-start(bf16[8,32,256]{2,1,0:T(8,128)(2,1)} %toeplitz_conv.1), calls=%async_computation.1 | async-start | bytes 262144 | tf_op jit(solution)/shard_map/all_to_all | solution.py:132
  34.5 0.0 collective-permute-done.2
  34.5 0.0 collective-permute-done
  34.5 3.5 %collective-permute-done.1 = bf16[256,1024]{1,0:T(8,128)(2,1)S(1)} collective-permute-done((bf16[256,1024]{1,0:T(8,128)(2,1)S(1)}, bf16[256,1024]{1,0:T(8,128)(2,1)S(1)}, u32[]{:S(2)}, u32[]{:S(2)}) %collective-permute-start.1) | collective-permute-done | bytes 524320 | tf_op jit(solution)/shard_map/ppermute | solution.py:128
  38.0 3.8 %all-to-all-done.1 = bf16[8,32,256]{2,1,0:T(8,128)(2,1)S(1)} async-done(((bf16[8,32,256]{2,1,0:T(8,128)(2,1)}), bf16[8,32,256]{2,1,0:T(8,128)(2,1)S(1)}, u32[]{:S(2)}, u32[]{:S(2)}) %all-to-all-start.1) | async-done | bytes 131104 | tf_op jit(solution)/shard_map/all_to_all | solution.py:132
  41.8 0.0 copy-done
  41.8 0.0 copy-done.1
  41.8 0.0 copy-done.2
  41.9 0.0 copy-done.3
  41.9 0.1 fusion.4
  42.0 7.2 %all_gather.3 = bf16[1024,256]{1,0:T(8,128)(2,1)S(1)} all-gather(bf16[256,256]{1,0:T(8,128)(2,1)S(1)} %fusion.4), channel_id=1, replica_groups=mesh['ctx'=8,'tp'=4] {'tp'}, dimensions={0}, use_global_device_ids=true | all-gather | bytes 655360 | tf_op jit(solution)/shard_map/all_gather | solution.py:136
  49.2 0.3 fusion.6
  49.5 0.4 fusion.8
  49.9 0.4 fusion.10
  50.3 1.2 %fusion.2 = bf16[1024,256]{1,0:T(8,128)(2,1)} fusion(f32[1024,256]{1,0:T(8,128)S(1)} %fusion.6, f32[1024,256]{1,0:T(8,128)S(1)} %fusion.8, f32[1024,256]{1,0:T(8,128)S(1)} %fusion.10, bf16[256,1024]{1,0:T(8,128)(2,1)S(1)} %get-tuple-element.10, bf16[1024,256]{1,0:T(8,128)(2,1)S(1)} %all_gather.3, s32[]{:T(128)S(6)} %select_n.63), kind=kOutput, calls=%fused_computation.3 | convolution fusion | flops 135266304 | bytes 4325380 | tf_op jit(solution)/shard_map/dot_general | solution.py:140
Async XLA Ops:
  2.7 16.2 %all-to-all-start = ((bf16[8,2,32,256]{3,2,1,0:T(8,128)(2,1)}), bf16[8,2,32,256]{3,2,1,0:T(8,128)(2,1)S(1)}, u32[]{:S(2)}, u32[]{:S(2)}) async-start(bf16[8,2,32,256]{3,2,1,0:T(8,128)(2,1)} %pad_maximum_fusion), calls=%async_computation | async-start | bytes 524288 | tf_op jit(solution)/shard_map/all_to_all | solution.py:130
  10.0 31.9 %copy-start = (bf16[256,256]{1,0:T(8,128)(2,1)S(1)}, bf16[256,256]{1,0:T(8,128)(2,1)}, u32[]{:S(2)}) copy-start(bf16[256,256]{1,0:T(8,128)(2,1)} %param.8) | copy-start | bytes 393220
  10.0 31.9 %copy-start.1 = (bf16[256,256]{1,0:T(8,128)(2,1)S(1)}, bf16[256,256]{1,0:T(8,128)(2,1)}, u32[]{:S(2)}) copy-start(bf16[256,256]{1,0:T(8,128)(2,1)} %param.7) | copy-start | bytes 393220
  10.0 31.9 %copy-start.2 = (bf16[256,256]{1,0:T(8,128)(2,1)S(1)}, bf16[256,256]{1,0:T(8,128)(2,1)}, u32[]{:S(2)}) copy-start(bf16[256,256]{1,0:T(8,128)(2,1)} %param.6) | copy-start | bytes 393220
  10.0 31.9 %copy-start.3 = (f32[256]{0:T(256)S(1)}, f32[256]{0:T(256)}, u32[]{:S(2)}) copy-start(f32[256]{0:T(256)} %param.10) | copy-start | bytes 3076
  12.8 21.7 %collective-permute-start.2 = (bf16[256,1024]{1,0:T(8,128)(2,1)}, bf16[256,1024]{1,0:T(8,128)(2,1)S(1)}, u32[]{:S(2)}, u32[]{:S(2)}) collective-permute-start(bf16[256,1024]{1,0:T(8,128)(2,1)} %get-tuple-element.15), channel_id=1, source_target_pairs={{0,3},{1,0},{2,1},{3,2},{4,7},{5,4},{6,5},{7,6},{8,11},{9,8},{10,9... | collective-permute-start | bytes 1572872 | tf_op jit(solution)/shard_map/ppermute | solution.py:128
  13.5 21.0 %collective-permute-start = (bf16[256,1024]{1,0:T(8,128)(2,1)}, bf16[256,1024]{1,0:T(8,128)(2,1)S(1)}, u32[]{:S(2)}, u32[]{:S(2)}) collective-permute-start(bf16[256,1024]{1,0:T(8,128)(2,1)} %get-tuple-element.16), channel_id=1, source_target_pairs={{0,1},{1,2},{2,3},{3,0},{4,5},{5,6},{6,7},{7,4},{8,9},{9,10},{10,1... | collective-permute-start | bytes 1572872 | tf_op jit(solution)/shard_map/ppermute | solution.py:128
  13.5 24.5 %collective-permute-start.1 = (bf16[256,1024]{1,0:T(8,128)(2,1)S(1)}, bf16[256,1024]{1,0:T(8,128)(2,1)S(1)}, u32[]{:S(2)}, u32[]{:S(2)}) collective-permute-start(bf16[256,1024]{1,0:T(8,128)(2,1)S(1)} %get-tuple-element.18), channel_id=1, source_target_pairs={{0,2},{1,3},{2,0},{3,1},{4,6},{5,7},{6,4},{7,5},{8,10},{9,11},{10,... | collective-permute-start | bytes 1572872 | tf_op jit(solution)/shard_map/ppermute | solution.py:128
  30.9 10.9 %all-to-all-start.1 = ((bf16[8,32,256]{2,1,0:T(8,128)(2,1)}), bf16[8,32,256]{2,1,0:T(8,128)(2,1)S(1)}, u32[]{:S(2)}, u32[]{:S(2)}) async-start(bf16[8,32,256]{2,1,0:T(8,128)(2,1)} %toeplitz_conv.1), calls=%async_computation.1 | async-start | bytes 262144 | tf_op jit(solution)/shard_map/all_to_all | solution.py:132

commit v2 on v1

--- a/solution.py
+++ b/solution.py
@@ -7,7 +7,7 @@
 
 LANES = 128
 PACK = 16
-SUB = 64
+SUB = 32
 PHASES = LANES // SUB
 
 
@@ -67,7 +67,7 @@
             sums[phase, pl.ds(chan * lines, lines), :] = total[phase * lines : (phase + 1) * lines]
         return 0
 
-    lax.fori_loop(0, chans, channel, 0)
+    lax.fori_loop(0, chans, channel, 0, unroll=8 if chans % 8 == 0 else 1)
 
     older = [jnp.zeros((chans, LANES), jnp.float32)] * PHASES
     for line in range(lines):
@@ -95,13 +95,115 @@
             pltpu.VMEM((PHASES, chans * lines, LANES), jnp.float32),
         ],
         compiler_params=pltpu.CompilerParams(vmem_limit_bytes=40 * 2**20),
-        cost_estimate=pl.CostEstimate(
-            flops=2 * chans * lines * LANES * lines * LANES,
-            bytes_accessed=6 * chans * lines * LANES,
-            transcendentals=0,
-        ),
+        cost_estimate=pl.CostEstimate(flops=1, bytes_accessed=1, transcendentals=0),
         name="toeplitz_conv",
     )(pieces)
+
+
+def partner(me, step, tp):
+    if tp & (tp - 1) == 0:
+        return me ^ step
+    return (me + step) % tp
+
+
+def source(me, step, tp):
+    if tp & (tp - 1) == 0:
+        return me ^ step
+    return (me + tp - step) % tp
+
+
+def exchanges(tp, channels):
+    early = tp // 2
+    return [(step, 0, channels) for step in [early] + [step for step in range(tp - 1, 0, -1) if step != early]]
+
+
+def prepare_kernel(key_ref, value_ref, taps_ref, w_ref, pieces_ref, *refs):
+    shards, _, share, _ = pieces_ref.shape
+    tp = lax.axis_size("tp")
+    feats = w_ref.shape[1] // tp
+    me = lax.axis_index("tp")
+    plan = exchanges(tp, w_ref.shape[0])
+    cuts, (key, value, taps, in_sems, sems) = refs[: len(plan)], refs[len(plan) :]
+    loads = []
+    for place, (ref, held) in enumerate(((key_ref, key), (value_ref, value), (taps_ref, taps))):
+        loads.append(pltpu.make_async_copy(ref, held, in_sems.at[place]))
+        loads[-1].start()
+    copies = []
+    for place, (step, first, count) in enumerate(plan):
+        column = pl.multiple_of(partner(me, step, tp) * feats, LANES)
+        cut = w_ref.at[pl.ds(first, count), pl.ds(column, feats)]
+        copies.append(pltpu.make_async_copy(cut, cuts[place], sems.at[place]))
+        copies[-1].start()
+    for load in loads:
+        load.wait()
+    for shard in range(shards):
+        rows = pl.ds(shard * share, share)
+        signal = key[rows, :].astype(jnp.float32) * value[rows, :].astype(jnp.float32)
+        pieces_ref[shard, 0] = signal.astype(jnp.bfloat16)
+        pieces_ref[shard, 1] = taps[rows, :].astype(jnp.bfloat16)
+    for copy in copies:
+        copy.wait()
+
+
+def prepare(key_k, value_v, filter_taps, w_out, shards, tp):
+    channels, seq_dev = key_k.shape
+    feats = w_out.shape[1] // tp
+    plan = exchanges(tp, channels)
+    vmem, hbm = pl.BlockSpec(memory_space=pltpu.VMEM), pl.BlockSpec(memory_space=pltpu.HBM)
+    return pl.pallas_call(
+        prepare_kernel,
+        out_shape=[jax.ShapeDtypeStruct((shards, 2, channels // shards, seq_dev), jnp.bfloat16)]
+        + [jax.ShapeDtypeStruct((count, feats), jnp.bfloat16) for _, _, count in plan],
+        in_specs=[hbm, hbm, hbm, hbm],
+        out_specs=[vmem] * (1 + len(plan)),
+        scratch_shapes=[
+            pltpu.VMEM(key_k.shape, key_k.dtype),
+            pltpu.VMEM(value_v.shape, value_v.dtype),
+            pltpu.VMEM(filter_taps.shape, filter_taps.dtype),
+            pltpu.SemaphoreType.DMA((3,)),
+            pltpu.SemaphoreType.DMA((len(plan),)),
+        ],
+        compiler_params=pltpu.CompilerParams(vmem_limit_bytes=60 * 2**20),
+        cost_estimate=pl.CostEstimate(flops=channels * seq_dev, bytes_accessed=4 * w_out.size, transcendentals=0),
+        name="prepare",
+    )(key_k, value_v, filter_taps, w_out)
+
+
+def project_kernel(gated_ref, own_ref, *refs):
+    weights, out_ref = refs[:-1], refs[-1]
+    tp = lax.axis_size("tp")
+    channels = own_ref.shape[0]
+    me = lax.axis_index("tp")
+
+    def term(weight_ref, step, first, count):
+        row = pl.multiple_of(source(me, step, tp) * channels + first, PACK)
+        return lax.dot_general(
+            weight_ref[...],
+            gated_ref[pl.ds(row, count), :],
+            (((0,), (0,)), ((), ())),
+            preferred_element_type=jnp.float32,
+        )
+
+    total = term(own_ref, 0, 0, channels)
+    for weight_ref, (step, first, count) in zip(weights, exchanges(tp, channels)):
+        total = total + term(weight_ref, step, first, count)
+    out_ref[...] = total.astype(jnp.bfloat16)
+
+
+def project(gathered, own, weights):
+    channels, feats = own.shape
+    rows, seq_dev = gathered.shape
+    return pl.pallas_call(
+        project_kernel,
+        out_shape=jax.ShapeDtypeStruct((feats, seq_dev), jnp.bfloat16),
+        in_specs=[pl.BlockSpec(memory_space=pltpu.VMEM)] * (2 + len(weights)),
+        out_specs=pl.BlockSpec(memory_space=pltpu.VMEM),
+        compiler_params=pltpu.CompilerParams(vmem_limit_bytes=24 * 2**20),
+        cost_estimate=pl.CostEstimate(
+            flops=2 * rows * feats * seq_dev, bytes_accessed=2 * rows * (feats + seq_dev), transcendentals=0
+        ),
+        name="project",
+    )(gathered, own, *weights)
 
 
 def body(gate_q, key_k, value_v, filter_taps, skip_bias, w_out):
@@ -109,37 +211,23 @@
     shards = lax.axis_size("ctx")
     tp = lax.axis_size("tp")
     me = lax.axis_index("tp")
-    share = channels // shards
     feats = w_out.shape[1] // tp
-    signal = key_k.astype(jnp.float32) * value_v.astype(jnp.float32)
-    pieces = jnp.stack(
-        [
-            signal.astype(jnp.bfloat16).reshape(shards, share, seq_dev),
-            filter_taps.astype(jnp.bfloat16).reshape(shards, share, seq_dev),
-        ],
-        1,
-    )
-
-    def own_feats(owner):
-        return lax.dynamic_slice_in_dim(w_out, owner * feats, feats, 1)
-
-    weights = [own_feats(me)]
-    for step in range(1, tp):
-        weights.append(lax.ppermute(own_feats((me + step) % tp), "tp", [(i, (i + step) % tp) for i in range(tp)]))
-
+    pieces, *cuts = prepare(key_k, value_v, filter_taps, w_out, shards, tp)
+    weights = [
+        lax.ppermute(cut, "tp", [(i, partner(i, step, tp)) for i in range(tp)])
+        for cut, (step, _, _) in zip(cuts, exchanges(tp, channels))
+    ]
     pieces = lax.all_to_all(pieces, "ctx", split_axis=0, concat_axis=0, tiled=True)
     convolved = convolve(pieces)
+    convolved, weights[0] = lax.optimization_barrier((convolved, weights[0]))
     convolved = lax.all_to_all(convolved, "ctx", split_axis=0, concat_axis=0, tiled=True)
-    convolved, *weights = lax.optimization_barrier((convolved, *weights))
+    own = lax.dynamic_slice_in_dim(w_out, me * feats, feats, 1)
+    convolved, own, *weights = lax.optimization_barrier((convolved, own, *weights))
     convolved = convolved.reshape(channels, seq_dev).astype(jnp.float32)
+    signal = key_k.astype(jnp.float32) * value_v.astype(jnp.float32)
     gated_vals = (gate_q.astype(jnp.float32) * (convolved + skip_bias[:, None] * signal)).astype(jnp.bfloat16)
     gathered = lax.all_gather(gated_vals, "tp", axis=0, tiled=True)
-    total = None
-    for step in range(tp):
-        rows = lax.dynamic_slice_in_dim(gathered, ((me - step) % tp) * channels, channels, 0)
-        term = lax.dot_general(weights[step], rows, (((0,), (0,)), ((), ())), preferred_element_type=jnp.float32)
-        total = term if total is None else total + term
-    return total.astype(jnp.bfloat16)
+    return project(gathered, own, weights)
 
 
 def solution(mesh):

time: 51.8 us -> 44.9 us (0.87)
  waiting for transfers between devices: 11.4 us -> 14.3 us
  other arithmetic: 2.82 us -> 0.12 us
  Pallas kernels: 12 us -> 9.43 us
  matrix products: 2.21 us -> 0 us
  local copies, waits for them, and re-layouts: 2.84 us -> 1.09 us
  blocking collectives: 7.2 us -> 6.51 us
    pallas_call x1, Pallas kernels: 12 us -> 4.96 us  [convolve(): pl.pallas_call(conv_kernel, out_shape=jax.ShapeDtypeStruct((blocks, chans...]
    pallas_call x0 -> x2, Pallas kernels: none -> 4.48 us  [the longest x1 2.88 us: prepare(): pl.pallas_call(prepare_kernel, out_shape=[jax.ShapeDtypeStruct((shards, 2...]
    all_to_all x1, waiting for transfers between devices: 4.02 us -> 8.02 us  [body(): lax.all_to_all(pieces, 'ctx', split_axis=0, concat_axis=0, tiled=True)]
    ppermute x3, waiting for transfers between devices: 3.5 us -> 0.01 us  [body(): lax.ppermute(cut, 'tp', [(i, partner(i, step, tp)) for i in range(tp)])]
    all_to_all x1, waiting for transfers between devices: 3.83 us -> 6.24 us  [body(): lax.all_to_all(convolved, 'ctx', split_axis=0, concat_axis=0, tiled=True)]
    dot_general x4 -> x0, matrix products: 2.21 us -> none  [body(): lax.dot_general(weights[step], rows, (((0,), (0,)), ((), ())), preferred_...]
    convert_element_type x2 -> x0, other arithmetic: 1.97 us -> none  [the longest x1 1 us: body(): signal.astype(jnp.bfloat16).reshape(shards, share, seq_dev)]
    dynamic_slice x1, local copies, waits for them, and re-layouts: 2.82 us -> 1.08 us  [body(): own = lax.dynamic_slice_in_dim(w_out, me * feats, feats, 1)]
  transfers between devices with their start and end apart: 5 -> 5, of which waited for: 3 -> 2; matrix products, arithmetic and copies ran while one was open for 5% -> 2% of each run, Pallas kernels for 23% -> 11%
where the time goes in v2:
time: 44.9 us; the launch traced here: 44.5 us
  waiting for transfers between devices  14.3 us (32%)
  starting transfers between devices  13.1 us (29%)
  Pallas kernels  9.43 us (21%)
  blocking collectives  6.51 us (14%)
  local copies, waits for them, and re-layouts  1.09 us (2%)
    all_to_all x1, waiting for transfers between devices, body(): lax.all_to_all(pieces, 'ctx', split_axis=0, concat_axis=0, tiled=True)  8.02 us
    all_gather x1, blocking collectives, body(): gathered = lax.all_gather(gated_vals, 'tp', axis=0, tiled=True)  6.51 us
    all_to_all x1, waiting for transfers between devices, body(): lax.all_to_all(convolved, 'ctx', split_axis=0, concat_axis=0, tiled=True)  6.24 us
    all_to_all x1, starting transfers between devices, body(): lax.all_to_all(pieces, 'ctx', split_axis=0, concat_axis=0, tiled=True)  5.81 us
    pallas_call x1, Pallas kernels, convolve(): pl.pallas_call(conv_kernel, out_shape=jax.ShapeDtypeStruct((blocks, chans...  4.96 us
    ppermute x3, starting transfers between devices, body(): lax.ppermute(cut, 'tp', [(i, partner(i, step, tp)) for i in range(tp)])  3.66 us
    all_to_all x1, starting transfers between devices, body(): lax.all_to_all(convolved, 'ctx', split_axis=0, concat_axis=0, tiled=True)  3.59 us
    pallas_call x1, Pallas kernels, prepare(): pl.pallas_call(prepare_kernel, out_shape=[jax.ShapeDtypeStruct((shards, 2...  2.88 us
  transfers between devices with their start and end apart: 5, of which 2 were waited for; matrix products, arithmetic and copies ran while one was open for 2% of the time, Pallas kernels for 11%

profile of v2, /device:TPU:0, one launch (start us, length us, event | category | flops | bytes accessed | tf_op | source)
XLA Modules:
  0.0 44.5 jit_solution(8645832587125685645)
XLA Ops:
  0.0 0.0 copy-start
  0.0 0.0 copy-start.1
  0.0 0.0 copy-start.3
  0.0 0.0 copy-start.2
  0.0 2.9 %prepare.1 = (bf16[8,2,32,256]{3,2,1,0:T(8,128)(2,1)}, bf16[256,1024]{1,0:T(8,128)(2,1)}, bf16[256,1024]{1,0:T(8,128)(2,1)}, bf16[256,1024]{1,0:T(8,128)(2,1)}) custom-call(bf16[256,256]{1,0:T(8,128)(2,1)} %key_ref.1, bf16[256,256]{1,0:T(8,128)(2,1)} %value_ref.1, f32[256,256]{1,0:T(8,128)} %taps_ref.1, bf16[256,4096]{1,0:T(8,128)(2,1)} %w_ref.1), custom_call_target="tpu_custom_call" | custom-call | flops 65536 | bytes 4194304 | tf_op jit(solution)/shard_map/prepare/pallas_call | solution.py:153
  2.9 3.0 %collective-permute-start = (bf16[256,1024]{1,0:T(8,128)(2,1)}, bf16[256,1024]{1,0:T(8,128)(2,1)S(1)}, u32[]{:S(2)}, u32[]{:S(2)}) collective-permute-start(bf16[256,1024]{1,0:T(8,128)(2,1)} %get-tuple-element.17), channel_id=1, source_target_pairs={{0,2},{1,3},{2,0},{3,1},{4,6},{5,7},{6,4},{7,5},{8,10},{9,11},{10,... | collective-permute-start | bytes 1572872 | tf_op jit(solution)/shard_map/ppermute | solution.py:217
  5.9 5.8 %all-to-all-start = ((bf16[8,2,32,256]{3,2,1,0:T(8,128)(2,1)}), bf16[8,2,32,256]{3,2,1,0:T(8,128)(2,1)S(1)}, u32[]{:S(2)}, u32[]{:S(2)}) async-start(bf16[8,2,32,256]{3,2,1,0:T(8,128)(2,1)} %get-tuple-element.16), calls=%async_computation | async-start | bytes 524288 | tf_op jit(solution)/shard_map/all_to_all | solution.py:220
  11.7 0.0 collective-permute-start.1
  11.8 0.6 %collective-permute-start.2 = (bf16[256,1024]{1,0:T(8,128)(2,1)}, bf16[256,1024]{1,0:T(8,128)(2,1)S(1)}, u32[]{:S(2)}, u32[]{:S(2)}) collective-permute-start(bf16[256,1024]{1,0:T(8,128)(2,1)} %get-tuple-element.21), channel_id=1, source_target_pairs={{0,1},{1,0},{2,3},{3,2},{4,5},{5,4},{6,7},{7,6},{8,9},{9,8},{10,11... | collective-permute-start | bytes 1572872 | tf_op jit(solution)/shard_map/ppermute | solution.py:217
  12.4 8.0 %all-to-all-done.x_ref = bf16[8,2,32,256]{3,2,1,0:T(8,128)(2,1)S(1)} async-done(((bf16[8,2,32,256]{3,2,1,0:T(8,128)(2,1)}), bf16[8,2,32,256]{3,2,1,0:T(8,128)(2,1)S(1)}, u32[]{:S(2)}, u32[]{:S(2)}) %all-to-all-start) | async-done | bytes 262176 | tf_op jit(solution)/shard_map/all_to_all | solution.py:220
  20.4 5.0 %toeplitz_conv.1 = bf16[8,32,256]{2,1,0:T(8,128)(2,1)} custom-call(bf16[8,2,32,256]{3,2,1,0:T(8,128)(2,1)S(1)} %all-to-all-done.x_ref), custom_call_target="tpu_custom_call" | custom-call | flops 1 | bytes 1 | tf_op jit(solution)/shard_map/toeplitz_conv/pallas_call | solution.py:87
  25.3 0.0 collective-permute-done.refs_0_
  25.3 3.6 %all-to-all-start.1 = ((bf16[8,32,256]{2,1,0:T(8,128)(2,1)}), bf16[8,32,256]{2,1,0:T(8,128)(2,1)S(1)}, u32[]{:S(2)}, u32[]{:S(2)}) async-start(bf16[8,32,256]{2,1,0:T(8,128)(2,1)} %toeplitz_conv.1), calls=%async_computation.1 | async-start | bytes 262144 | tf_op jit(solution)/shard_map/all_to_all | solution.py:223
  28.9 1.1 %constant_dynamic-slice_fusion.own_ref = bf16[256,1024]{1,0:T(8,128)(2,1)S(1)} fusion(bf16[256,4096]{1,0:T(8,128)(2,1)} %w_ref.1, s32[]{:T(128)S(6)} %select_n.3), kind=kLoop, calls=%fused_computation.3 | loop fusion | bytes 1048580 | tf_op jit(solution)/shard_map/dynamic_slice | solution.py:224
  30.0 0.0 collective-permute-done.1.refs_1_
  30.0 0.0 collective-permute-done.2.refs_2_
  30.0 6.2 %all-to-all-done.1 = bf16[8,32,256]{2,1,0:T(8,128)(2,1)S(1)} async-done(((bf16[8,32,256]{2,1,0:T(8,128)(2,1)}), bf16[8,32,256]{2,1,0:T(8,128)(2,1)S(1)}, u32[]{:S(2)}, u32[]{:S(2)}) %all-to-all-start.1) | async-done | bytes 131104 | tf_op jit(solution)/shard_map/all_to_all | solution.py:223
  36.3 0.0 copy-done
  36.3 0.0 copy-done.1
  36.3 0.0 copy-done.3
  36.3 0.0 copy-done.2
  36.3 0.1 fusion.1
  36.4 6.5 %all_gather.3.gated_ref = bf16[1024,256]{1,0:T(8,128)(2,1)S(1)} all-gather(bf16[256,256]{1,0:T(8,128)(2,1)S(1)} %fusion.1), channel_id=1, replica_groups=mesh['ctx'=8,'tp'=4] {'tp'}, dimensions={0}, use_global_device_ids=true | all-gather | bytes 655360 | tf_op jit(solution)/shard_map/all_gather | solution.py:229
  42.9 1.6 %project.1 = bf16[1024,256]{1,0:T(8,128)(2,1)} custom-call(bf16[1024,256]{1,0:T(8,128)(2,1)S(1)} %all_gather.3.gated_ref, bf16[256,1024]{1,0:T(8,128)(2,1)S(1)} %constant_dynamic-slice_fusion.own_ref, bf16[256,1024]{1,0:T(8,128)(2,1)S(1)} %collective-permute-done.refs_0_, bf16[256,1024]{1,0:T(8,128)(2,1)S(1)} %collective-permute-done.1.refs_1_, ...), custom_call_target="tpu_custom_call" | custom-call | flops 536870912 | bytes 2621440 | tf_op jit(solution)/shard_map/project/pallas_call | solution.py:196
Async XLA Ops:
  0.0 36.3 %copy-start = (bf16[256,256]{1,0:T(8,128)(2,1)S(1)}, bf16[256,256]{1,0:T(8,128)(2,1)}, u32[]{:S(2)}) copy-start(bf16[256,256]{1,0:T(8,128)(2,1)} %value_ref.1) | copy-start | bytes 393220
  0.0 36.3 %copy-start.1 = (bf16[256,256]{1,0:T(8,128)(2,1)S(1)}, bf16[256,256]{1,0:T(8,128)(2,1)}, u32[]{:S(2)}) copy-start(bf16[256,256]{1,0:T(8,128)(2,1)} %key_ref.1) | copy-start | bytes 393220
  0.0 36.3 %copy-start.3 = (f32[256]{0:T(256)S(1)}, f32[256]{0:T(256)}, u32[]{:S(2)}) copy-start(f32[256]{0:T(256)} %param.10) | copy-start | bytes 3076
  0.0 36.3 %copy-start.2 = (bf16[256,256]{1,0:T(8,128)(2,1)S(1)}, bf16[256,256]{1,0:T(8,128)(2,1)}, u32[]{:S(2)}) copy-start(bf16[256,256]{1,0:T(8,128)(2,1)} %param.6) | copy-start | bytes 393220
  2.9 22.4 %collective-permute-start = (bf16[256,1024]{1,0:T(8,128)(2,1)}, bf16[256,1024]{1,0:T(8,128)(2,1)S(1)}, u32[]{:S(2)}, u32[]{:S(2)}) collective-permute-start(bf16[256,1024]{1,0:T(8,128)(2,1)} %get-tuple-element.17), channel_id=1, source_target_pairs={{0,2},{1,3},{2,0},{3,1},{4,6},{5,7},{6,4},{7,5},{8,10},{9,11},{10,... | collective-permute-start | bytes 1572872 | tf_op jit(solution)/shard_map/ppermute | solution.py:217
  5.9 14.4 %all-to-all-start = ((bf16[8,2,32,256]{3,2,1,0:T(8,128)(2,1)}), bf16[8,2,32,256]{3,2,1,0:T(8,128)(2,1)S(1)}, u32[]{:S(2)}, u32[]{:S(2)}) async-start(bf16[8,2,32,256]{3,2,1,0:T(8,128)(2,1)} %get-tuple-element.16), calls=%async_computation | async-start | bytes 524288 | tf_op jit(solution)/shard_map/all_to_all | solution.py:220
  11.7 18.3 %collective-permute-start.1 = (bf16[256,1024]{1,0:T(8,128)(2,1)}, bf16[256,1024]{1,0:T(8,128)(2,1)S(1)}, u32[]{:S(2)}, u32[]{:S(2)}) collective-permute-start(bf16[256,1024]{1,0:T(8,128)(2,1)} %get-tuple-element.20), channel_id=1, source_target_pairs={{0,3},{1,2},{2,1},{3,0},{4,7},{5,6},{6,5},{7,4},{8,11},{9,10},{10,... | collective-permute-start | bytes 1572872 | tf_op jit(solution)/shard_map/ppermute | solution.py:217
  11.8 18.3 %collective-permute-start.2 = (bf16[256,1024]{1,0:T(8,128)(2,1)}, bf16[256,1024]{1,0:T(8,128)(2,1)S(1)}, u32[]{:S(2)}, u32[]{:S(2)}) collective-permute-start(bf16[256,1024]{1,0:T(8,128)(2,1)} %get-tuple-element.21), channel_id=1, source_target_pairs={{0,1},{1,0},{2,3},{3,2},{4,5},{5,4},{6,7},{7,6},{8,9},{9,8},{10,11... | collective-permute-start | bytes 1572872 | tf_op jit(solution)/shard_map/ppermute | solution.py:217
  25.3 10.9 %all-to-all-start.1 = ((bf16[8,32,256]{2,1,0:T(8,128)(2,1)}), bf16[8,32,256]{2,1,0:T(8,128)(2,1)S(1)}, u32[]{:S(2)}, u32[]{:S(2)}) async-start(bf16[8,32,256]{2,1,0:T(8,128)(2,1)} %toeplitz_conv.1), calls=%async_computation.1 | async-start | bytes 262144 | tf_op jit(solution)/shard_map/all_to_all | solution.py:223

commit v3 on v2

v3 whole, which is shorter than its diff:
```python
import jax
import jax.numpy as jnp
from jax import lax
from jax.experimental import pallas as pl
from jax.experimental.pallas import tpu as pltpu
from jax.sharding import PartitionSpec as P

LANES = 128
PACK = 16
SUB = 16
PHASES = LANES // SUB
CORES = 2


def pitches(lines):
    pad = lines - PHASES
    return pad, (pad + lines) | 1, lines | 1


def conv_kernel(x_ref, bias_ref, y_ref, taps, rows, sums):
    blocks, _, chans, seq_dev = x_ref.shape
    halves = seq_dev // LANES
    lines = blocks * halves
    length = lines * LANES
    lane = lax.broadcasted_iota(jnp.int32, (chans, LANES), 1)

    taps[:, pl.ds(0, LANES)] = jnp.zeros((chans, LANES), jnp.float32)
    pad, row_pitch, sum_pitch = pitches(lines)
    for phase in range(PHASES):
        for chan in range(chans):
            rows[phase, pl.ds(chan * row_pitch, pad), :] = jnp.zeros((pad, LANES), jnp.float32)
    older = [[jnp.zeros((chans, LANES), jnp.float32)] * PHASES] * (PHASES - 1)
    for line in range(lines):
        block, half = divmod(line, halves)
        cut = pl.ds(half * LANES, LANES)
        taps[:, pl.ds(LANES + line * LANES, LANES)] = x_ref[block, 1, :, cut].astype(jnp.float32)
        fresh = x_ref[block, 0, :, cut].astype(jnp.float32)
        now = [[fresh] + [pltpu.roll(fresh, SUB * turn, axis=1) for turn in range(1, PHASES)]] + older
        older = now[: PHASES - 1]
        for phase in range(PHASES):
            made = now[0][-phase % PHASES]
            for step in range(1, PHASES):
                made = jnp.where(lane >= SUB * step, now[step][(step - phase) % PHASES], made)
            rows[phase, pl.ds(pad + line, chans, stride=row_pitch), :] = made

    def channel(chan, _):
        wide = jnp.broadcast_to(taps[pl.ds(chan, 1), :], (PACK, LANES + length))
        skew = pltpu.roll(wide, 0, 1, stride=1, stride_axis=0).astype(jnp.bfloat16)
        parts = []
        for part in range(SUB // PACK):
            parts.append(pltpu.roll(skew, part * PACK, 1) if part else skew)
        toeplitz = jnp.concatenate(
            [part[:, (line + 1) * LANES : (line + 2) * LANES] for line in range(lines) for part in parts], 0
        )
        base = chan * row_pitch + pad
        left = jnp.concatenate(
            [
                jnp.concatenate(
                    [
                        rows[phase, pl.ds(base - PHASES * step, lines), :].astype(jnp.bfloat16)
                        for step in range(lines // PHASES)
                    ],
                    1,
                )
                for phase in range(PHASES)
            ],
            0,
        )
        total = jnp.dot(left, toeplitz, preferred_element_type=jnp.float32)
        for phase in range(PHASES):
            sums[phase, pl.ds(chan * sum_pitch, lines), :] = total[phase * lines : (phase + 1) * lines]
        return 0

    lax.fori_loop(0, chans, channel, 0, unroll=16 if chans % 16 == 0 else 1)

    first = pl.multiple_of(lax.axis_index("ctx") * chans, chans)
    bias = jnp.broadcast_to(bias_ref[pl.ds(first, chans), :], (chans, LANES))
    older = [jnp.zeros((chans, LANES), jnp.float32)] * PHASES
    for line in range(lines):
        block, half = divmod(line, halves)
        now = [sums[phase, pl.ds(line, chans, stride=sum_pitch), :] for phase in range(PHASES)]
        cut = pl.ds(half * LANES, LANES)
        value = now[0] + bias * x_ref[block, 0, :, cut].astype(jnp.float32)
        for phase in range(1, PHASES):
            mixed = jnp.where(lane < LANES - SUB * phase, now[phase], older[phase])
            value = value + pltpu.roll(mixed, SUB * phase, axis=1)
        older = now
        for copy in range(y_ref.shape[1]):
            y_ref[block, copy, :, cut] = value.astype(jnp.bfloat16)


def convolve(pieces, bias, copies):
    blocks, _, chans, seq_dev = pieces.shape
    lines = blocks * seq_dev // LANES
    _, row_pitch, sum_pitch = pitches(lines)
    return pl.pallas_call(
        conv_kernel,
        out_shape=jax.ShapeDtypeStruct((blocks, copies, chans, seq_dev), jnp.bfloat16),
        in_specs=[pl.BlockSpec(memory_space=pltpu.VMEM)] * 2,
        out_specs=pl.BlockSpec(memory_space=pltpu.VMEM),
        scratch_shapes=[
            pltpu.VMEM((chans, LANES + lines * LANES), jnp.float32),
            pltpu.VMEM((PHASES, chans * row_pitch, LANES), jnp.float32),
            pltpu.VMEM((PHASES, chans * sum_pitch, LANES), jnp.float32),
        ],
        compiler_params=pltpu.CompilerParams(vmem_limit_bytes=16 * 2**20),
        cost_estimate=pl.CostEstimate(flops=1, bytes_accessed=1, transcendentals=0),
        name="toeplitz_conv",
    )(pieces, bias)


def partner(me, step, tp):
    chips, other = step
    return (me // CORES + chips) % (tp // CORES) * CORES + (me % CORES + other) % CORES


def source(me, step, tp):
    chips, other = step
    return (me // CORES + tp // CORES - chips) % (tp // CORES) * CORES + (me % CORES + CORES - other) % CORES


def exchanges(tp):
    steps = [(chips, other) for chips in range(tp // CORES) for other in range(CORES)][1:]
    early = (tp // CORES // 2, 0)
    return [early] + [step for step in reversed(steps) if step != early]


def prepare_kernel(key_ref, value_ref, taps_ref, w_ref, pieces_ref, *refs):
    shards, _, share, _ = pieces_ref.shape
    tp = lax.axis_size("tp")
    feats = w_ref.shape[1] // tp
    me = lax.axis_index("tp")
    plan = exchanges(tp)[: len(refs) - 5]
    cuts, (key, value, taps, in_sems, sems) = refs[: len(plan)], refs[len(plan) :]
    loads = []
    for place, (ref, held) in enumerate(((key_ref, key), (value_ref, value), (taps_ref, taps))):
        loads.append(pltpu.make_async_copy(ref, held, in_sems.at[place]))
        loads[-1].start()
    copies = []
    for place, step in enumerate(plan):
        column = pl.multiple_of(partner(me, step, tp) * feats, LANES)
        cut = w_ref.at[:, pl.ds(column, feats)]
        copies.append(pltpu.make_async_copy(cut, cuts[place], sems.at[place]))
        copies[-1].start()
    for load in loads:
        load.wait()
    for shard in range(shards):
        rows = pl.ds(shard * share, share)
        signal = key[rows, :].astype(jnp.float32) * value[rows, :].astype(jnp.float32)
        pieces_ref[shard, 0] = signal.astype(jnp.bfloat16)
        pieces_ref[shard, 1] = taps[rows, :].astype(jnp.bfloat16)
    for copy in copies:
        copy.wait()


def prepare(key_k, value_v, filter_taps, w_out, shards, tp):
    channels, seq_dev = key_k.shape
    feats = w_out.shape[1] // tp
    plan = exchanges(tp)[:1]
    vmem, hbm = pl.BlockSpec(memory_space=pltpu.VMEM), pl.BlockSpec(memory_space=pltpu.HBM)
    return pl.pallas_call(
        prepare_kernel,
        out_shape=[pltpu.VMEM((shards, 2, channels // shards, seq_dev), jnp.bfloat16)]
        + [pltpu.VMEM((channels, feats), jnp.bfloat16)] * len(plan),
        in_specs=[hbm, hbm, hbm, hbm],
        out_specs=[vmem] * (1 + len(plan)),
        scratch_shapes=[
            pltpu.VMEM(key_k.shape, key_k.dtype),
            pltpu.VMEM(value_v.shape, value_v.dtype),
            pltpu.VMEM(filter_taps.shape, filter_taps.dtype),
            pltpu.SemaphoreType.DMA((3,)),
            pltpu.SemaphoreType.DMA((len(plan),)),
        ],
        compiler_params=pltpu.CompilerParams(vmem_limit_bytes=8 * 2**20),
        cost_estimate=pl.CostEstimate(flops=channels * seq_dev, bytes_accessed=4 * w_out.size, transcendentals=0),
        name="prepare",
    )(*(pltpu.with_memory_space_constraint(x, pltpu.HBM) for x in (key_k, value_v, filter_taps, w_out)))


def gate_kernel(conv_ref, *refs):
    gates, out_ref = refs[:-1], refs[-1]
    blocks, chips, share, _ = conv_ref.shape
    channels = blocks * share
    row = lax.axis_index("tp") // CORES
    for step, gate_ref in enumerate(gates):
        other = (row + chips - step) % chips
        for block in range(blocks):
            rows = pl.ds(block * share, share)
            gated = gate_ref[rows, :].astype(jnp.float32) * conv_ref[block, other].astype(jnp.float32)
            out_ref[pl.ds(step * channels + block * share, share), :] = gated.astype(jnp.bfloat16)


def gate(convolved, gates):
    blocks, chips, share, seq_dev = convolved.shape
    return pl.pallas_call(
        gate_kernel,
        out_shape=pltpu.VMEM((chips * blocks * share, seq_dev), jnp.bfloat16),
        in_specs=[pl.BlockSpec(memory_space=pltpu.VMEM)] * (1 + chips),
        out_specs=pl.BlockSpec(memory_space=pltpu.VMEM),
        compiler_params=pltpu.CompilerParams(vmem_limit_bytes=8 * 2**20),
        name="gate",
    )(convolved, *(pltpu.with_memory_space_constraint(x, pltpu.VMEM) for x in gates))


def project_kernel(gated_ref, own_ref, *refs):
    weights, out_ref = (own_ref, *refs[:-1]), refs[-1]
    tp = lax.axis_size("tp")
    channels = own_ref.shape[0]
    core = lax.axis_index("tp") % CORES
    total = None
    for weight_ref, (chips, other) in zip(weights, [(0, 0)] + exchanges(tp)):
        place = (core + CORES - other) % CORES * (tp // CORES) + chips
        term = lax.dot_general(
            weight_ref[...],
            gated_ref[pl.ds(pl.multiple_of(place * channels, channels), channels), :],
            (((0,), (0,)), ((), ())),
            preferred_element_type=jnp.float32,
        )
        total = term if total is None else total + term
    out_ref[...] = total.astype(jnp.bfloat16)


def project(gathered, own, weights):
    channels, feats = own.shape
    rows, seq_dev = gathered.shape
    return pl.pallas_call(
        project_kernel,
        out_shape=jax.ShapeDtypeStruct((feats, seq_dev), jnp.bfloat16),
        in_specs=[pl.BlockSpec(memory_space=pltpu.VMEM)] * (2 + len(weights)),
        out_specs=pl.BlockSpec(memory_space=pltpu.VMEM),
        compiler_params=pltpu.CompilerParams(vmem_limit_bytes=24 * 2**20),
        cost_estimate=pl.CostEstimate(
            flops=2 * rows * feats * seq_dev, bytes_accessed=2 * rows * (feats + seq_dev), transcendentals=0
        ),
        name="project",
    )(gathered, own, *weights)


def body(gate_q, key_k, value_v, filter_taps, skip_bias, w_out):
    channels, seq_dev = key_k.shape
    shards = lax.axis_size("ctx")
    tp = lax.axis_size("tp")
    me = lax.axis_index("tp")
    chips = tp // CORES
    feats = w_out.shape[1] // tp

    def exchange(array, step):
        return lax.ppermute(array, "tp", [(i, partner(i, step, tp)) for i in range(tp)])

    pieces, *cuts = prepare(key_k, value_v, filter_taps, w_out, shards, tp)
    for step in exchanges(tp)[len(cuts) :]:
        cuts.append(lax.dynamic_slice_in_dim(w_out, partner(me, step, tp) * feats, feats, 1))
    weights = [exchange(cut, step) for cut, step in zip(cuts, exchanges(tp))]
    gates = [gate_q] + [exchange(gate_q, (step, 0)) for step in range(1, chips)]

    pieces = lax.all_to_all(pieces, "ctx", split_axis=0, concat_axis=0, tiled=True)
    convolved = convolve(pieces, skip_bias.reshape(channels, 1), chips)
    convolved, weights[0] = lax.optimization_barrier((convolved, weights[0]))
    convolved = lax.all_to_all(
        convolved.reshape(shards * chips, channels // shards, seq_dev),
        ("ctx", "tp"),
        split_axis=0,
        concat_axis=0,
        tiled=True,
        axis_index_groups=[
            [shard * tp + chip * CORES + core for shard in range(shards) for chip in range(chips)] for core in range(CORES)
        ],
    )
    own = lax.dynamic_slice_in_dim(w_out, me * feats, feats, 1)
    convolved, own, gates, weights = lax.optimization_barrier((convolved, own, gates, weights))
    gated_vals = gate(convolved.reshape(shards, chips, channels // shards, seq_dev), gates)
    gathered = lax.all_gather(
        gated_vals,
        "tp",
        axis=0,
        tiled=True,
        axis_index_groups=[[chip * CORES + core for core in range(CORES)] for chip in range(chips)],
    )
    return project(gathered, own, weights)


def solution(mesh):
    return jax.shard_map(
        body,
        mesh=mesh,
        in_specs=(P("tp", "ctx"), P("tp", "ctx"), P("tp", "ctx"), P("tp", "ctx"), P("tp"), P("tp", None)),
        out_specs=P("tp", "ctx"),
        check_vma=False,
    )
```

time: 44.9 us -> 39.9 us (0.89)
  blocking collectives: 6.51 us -> 2.18 us
  Pallas kernels: 9.43 us -> 6.72 us
  starting transfers between devices: 13.1 us -> 15.1 us
  local copies, waits for them, and re-layouts: 1.09 us -> 2.66 us
  waiting for transfers between devices: 14.3 us -> 12.8 us
    ppermute x3 -> x4, waiting for transfers between devices: 0.01 us -> 4.86 us  [exchange(): lax.ppermute(array, 'tp', [(i, partner(i, step, tp)) for i in range(tp)])]
    all_gather x1, blocking collectives: 6.51 us -> 2.18 us  [body(): lax.all_gather(gated_vals, 'tp', axis=0, tiled=True, axis_index_groups=[[...]
    all_to_all x1, waiting for transfers between devices: 6.24 us -> 2.58 us  [body(): lax.all_to_all(convolved.reshape(shards * chips, channels // shards, seq_...]
    pallas_call x2 -> x3, Pallas kernels: 7.84 us -> 5.14 us  [the longest x1 3.07 us: convolve(): pl.pallas_call(conv_kernel, out_shape=jax.ShapeDtypeStruct((blocks, copie...]
    all_to_all x1, waiting for transfers between devices: 8.02 us -> 5.35 us  [body(): lax.all_to_all(pieces, 'ctx', split_axis=0, concat_axis=0, tiled=True)]
    ppermute x3 -> x4, starting transfers between devices: 3.66 us -> 5.64 us  [exchange(): lax.ppermute(array, 'tp', [(i, partner(i, step, tp)) for i in range(tp)])]
    dynamic_slice x1, local copies, waits for them, and re-layouts: 1.08 us -> 2.52 us  [body(): lax.dynamic_slice_in_dim(w_out, partner(me, step, tp) * feats, feats, 1)]
  transfers between devices with their start and end apart: 5 -> 6, of which waited for: 2 -> 3; matrix products, arithmetic and copies ran while one was open for 2% -> 7% of each run, Pallas kernels for 11% -> 8%
where the time goes in v3:
time: 39.9 us; the launch traced here: 39.5 us
  starting transfers between devices  15.1 us (38%)
  waiting for transfers between devices  12.8 us (32%)
  Pallas kernels  6.72 us (17%)
  local copies, waits for them, and re-layouts  2.66 us (7%)
  blocking collectives  2.18 us (5%)
    all_to_all x1, starting transfers between devices, body(): lax.all_to_all(pieces, 'ctx', split_axis=0, concat_axis=0, tiled=True)  5.81 us
    ppermute x4, starting transfers between devices, exchange(): lax.ppermute(array, 'tp', [(i, partner(i, step, tp)) for i in range(tp)])  5.64 us
    all_to_all x1, waiting for transfers between devices, body(): lax.all_to_all(pieces, 'ctx', split_axis=0, concat_axis=0, tiled=True)  5.35 us
    ppermute x4, waiting for transfers between devices, exchange(): lax.ppermute(array, 'tp', [(i, partner(i, step, tp)) for i in range(tp)])  4.86 us
    all_to_all x1, starting transfers between devices, body(): lax.all_to_all(convolved.reshape(shards * chips, channels // shards, seq_...  3.69 us
    pallas_call x1, Pallas kernels, convolve(): pl.pallas_call(conv_kernel, out_shape=jax.ShapeDtypeStruct((blocks, copie...  3.07 us
    all_to_all x1, waiting for transfers between devices, body(): lax.all_to_all(convolved.reshape(shards * chips, channels // shards, seq_...  2.58 us
    dynamic_slice x1, local copies, waits for them, and re-layouts, body(): lax.dynamic_slice_in_dim(w_out, partner(me, step, tp) * feats, feats, 1)  2.52 us
  transfers between devices with their start and end apart: 6, of which 3 were waited for; matrix products, arithmetic and copies ran while one was open for 7% of the time, Pallas kernels for 8%

profile of v3, /device:TPU:0, one launch (start us, length us, event | category | flops | bytes accessed | tf_op | source)
XLA Modules:
  0.0 39.5 jit_solution(1615492432665370999)
XLA Ops:
  0.0 2.0 %prepare.1 = (bf16[8,2,32,256]{3,2,1,0:T(8,128)(2,1)}, bf16[256,1024]{1,0:T(8,128)(2,1)S(1)}) custom-call(bf16[256,256]{1,0:T(8,128)(2,1)} %key_ref.1, bf16[256,256]{1,0:T(8,128)(2,1)} %value_ref.1, f32[256,256]{1,0:T(8,128)} %taps_ref.1, bf16[256,4096]{1,0:T(8,128)(2,1)} %w_ref.1), custom_call_target="tpu_custom_call" | custom-call | flops 65536 | bytes 4194304 | tf_op jit(solution)/shard_map/prepare/pallas_call | solution.py:161
  2.0 0.0 copy-start.1
  2.0 3.0 %collective-permute-start = (bf16[256,1024]{1,0:T(8,128)(2,1)S(1)}, bf16[256,1024]{1,0:T(8,128)(2,1)S(1)}, u32[]{:S(2)}, u32[]{:S(2)}) collective-permute-start(bf16[256,1024]{1,0:T(8,128)(2,1)S(1)} %get-tuple-element.17), channel_id=1, source_target_pairs={{0,2},{1,3},{2,0},{3,1},{4,6},{5,7},{6,4},{7,5},{8,10},{9,11},{10,... | collective-permute-start | bytes 1572872 | tf_op jit(solution)/shard_map/ppermute | solution.py:248
  5.0 5.8 %all-to-all-start = ((bf16[8,2,32,256]{3,2,1,0:T(8,128)(2,1)}), bf16[8,2,32,256]{3,2,1,0:T(8,128)(2,1)S(1)}, u32[]{:S(2)}, u32[]{:S(2)}) async-start(bf16[8,2,32,256]{3,2,1,0:T(8,128)(2,1)} %get-tuple-element.16), calls=%async_computation | async-start | bytes 524288 | tf_op jit(solution)/shard_map/all_to_all | solution.py:256
  10.8 0.0 copy-start
  10.9 2.5 %constant_dynamic-slice_fusion = (bf16[256,1024]{1,0:T(8,128)(2,1)}, bf16[256,1024]{1,0:T(8,128)(2,1)S(1)}, bf16[256,1024]{1,0:T(8,128)(2,1)}) fusion(bf16[256,4096]{1,0:T(8,128)(2,1)} %w_ref.1, s32[]{:T(128)S(6)} %select_n.44, s32[]{:T(128)S(6)} %select_n.37, s32[]{:T(128)S(6)} %select_n.42), kind=kLoop, calls=%fused_computation | loop fusion | bytes 3145740 | tf_op jit(solution)/shard_map/dynamic_slice | solution.py:252
  13.4 0.0 collective-permute-start.3
  13.4 0.6 %collective-permute-start.2 = (bf16[256,1024]{1,0:T(8,128)(2,1)}, bf16[256,1024]{1,0:T(8,128)(2,1)S(1)}, u32[]{:S(2)}, u32[]{:S(2)}) collective-permute-start(bf16[256,1024]{1,0:T(8,128)(2,1)} %get-tuple-element.29), channel_id=1, source_target_pairs={{0,3},{1,2},{2,1},{3,0},{4,7},{5,6},{6,5},{7,4},{8,11},{9,10},{10,... | collective-permute-start | bytes 1572872 | tf_op jit(solution)/shard_map/ppermute | solution.py:248
  14.0 0.0 copy-done.1
  14.0 0.1 copy.7.bias_ref
  14.1 5.4 %all-to-all-done.x_ref = bf16[8,2,32,256]{3,2,1,0:T(8,128)(2,1)S(1)} async-done(((bf16[8,2,32,256]{3,2,1,0:T(8,128)(2,1)}), bf16[8,2,32,256]{3,2,1,0:T(8,128)(2,1)S(1)}, u32[]{:S(2)}, u32[]{:S(2)}) %all-to-all-start) | async-done | bytes 262176 | tf_op jit(solution)/shard_map/all_to_all | solution.py:256
  19.5 3.1 %toeplitz_conv.1 = bf16[8,2,32,256]{3,2,1,0:T(8,128)(2,1)} custom-call(bf16[8,2,32,256]{3,2,1,0:T(8,128)(2,1)S(1)} %all-to-all-done.x_ref, f32[256,1]{1,0:T(8,128)S(1)} %copy.7.bias_ref), custom_call_target="tpu_custom_call" | custom-call | flops 1 | bytes 1 | tf_op jit(solution)/shard_map/toeplitz_conv/pallas_call | solution.py:96
  22.6 0.0 collective-permute-done.refs_0_
  22.6 3.7 %all-to-all-start.1 = ((bf16[16,32,256]{2,1,0:T(8,128)(2,1)}), bf16[16,32,256]{2,1,0:T(8,128)(2,1)S(1)}, u32[]{:S(2)}, u32[]{:S(2)}) async-start(bf16[16,32,256]{2,1,0:T(8,128)(2,1)} %bitcast.1), calls=%async_computation.1 | async-start | bytes 524288 | tf_op jit(solution)/shard_map/all_to_all | solution.py:259
  26.3 0.0 copy-done
  26.3 2.0 %collective-permute-start.1 = (bf16[256,256]{1,0:T(8,128)(2,1)S(1)}, bf16[256,256]{1,0:T(8,128)(2,1)S(1)}, u32[]{:S(2)}, u32[]{:S(2)}) collective-permute-start(bf16[256,256]{1,0:T(8,128)(2,1)S(1)} %copy-done), channel_id=1, source_target_pairs={{0,2},{1,3},{2,0},{3,1},{4,6},{5,7},{6,4},{7,5},{8,10},{9,11},{10,... | collective-permute-start | bytes 393224 | tf_op jit(solution)/shard_map/ppermute | solution.py:248
  28.3 4.9 %collective-permute-done.1.refs_1_ = bf16[256,256]{1,0:T(8,128)(2,1)S(1)} collective-permute-done((bf16[256,256]{1,0:T(8,128)(2,1)S(1)}, bf16[256,256]{1,0:T(8,128)(2,1)S(1)}, u32[]{:S(2)}, u32[]{:S(2)}) %collective-permute-start.1) | collective-permute-done | bytes 131104 | tf_op jit(solution)/shard_map/ppermute | solution.py:248
  33.1 0.0 collective-permute-done.3.refs_2_
  33.1 0.0 collective-permute-done.2.refs_1_
  33.1 2.6 %all-to-all-done.1 = bf16[16,32,256]{2,1,0:T(8,128)(2,1)S(1)} async-done(((bf16[16,32,256]{2,1,0:T(8,128)(2,1)}), bf16[16,32,256]{2,1,0:T(8,128)(2,1)S(1)}, u32[]{:S(2)}, u32[]{:S(2)}) %all-to-all-start.1) | async-done | bytes 262176 | tf_op jit(solution)/shard_map/all_to_all | solution.py:259
  35.7 0.1 gate.1
  35.8 2.2 %all_gather.3.gated_ref = bf16[1024,256]{1,0:T(8,128)(2,1)S(1)} all-gather(bf16[512,256]{1,0:T(8,128)(2,1)S(1)} %gate.1), channel_id=1, replica_groups={{0,1},{2,3},{4,5},{6,7},{8,9},{10,11},{12,13},{14,15},{16,17},{18,19},{..., dimensions={0}, use_global_device_ids=true | all-gather | bytes 786432 | tf_op jit(solution)/shard_map/all_gather | solution.py:272
  38.0 1.6 %project.1 = bf16[1024,256]{1,0:T(8,128)(2,1)} custom-call(bf16[1024,256]{1,0:T(8,128)(2,1)S(1)} %all_gather.3.gated_ref, bf16[256,1024]{1,0:T(8,128)(2,1)S(1)} %get-tuple-element.23.own_ref, bf16[256,1024]{1,0:T(8,128)(2,1)S(1)} %collective-permute-done.refs_0_, bf16[256,1024]{1,0:T(8,128)(2,1)S(1)} %collective-permute-done.2.refs_1_, ...), custom_call_target="tpu_custom_call" | custom-call | flops 536870912 | bytes 2621440 | tf_op jit(solution)/shard_map/project/pallas_call | solution.py:226
Async XLA Ops:
  2.0 12.0 %copy-start.1 = (f32[256]{0:T(256)S(1)}, f32[256]{0:T(256)}, u32[]{:S(2)}) copy-start(f32[256]{0:T(256)} %param.10) | copy-start | bytes 3076
  2.0 20.6 %collective-permute-start = (bf16[256,1024]{1,0:T(8,128)(2,1)S(1)}, bf16[256,1024]{1,0:T(8,128)(2,1)S(1)}, u32[]{:S(2)}, u32[]{:S(2)}) collective-permute-start(bf16[256,1024]{1,0:T(8,128)(2,1)S(1)} %get-tuple-element.17), channel_id=1, source_target_pairs={{0,2},{1,3},{2,0},{3,1},{4,6},{5,7},{6,4},{7,5},{8,10},{9,11},{10,... | collective-permute-start | bytes 1572872 | tf_op jit(solution)/shard_map/ppermute | solution.py:248
  5.0 14.4 %all-to-all-start = ((bf16[8,2,32,256]{3,2,1,0:T(8,128)(2,1)}), bf16[8,2,32,256]{3,2,1,0:T(8,128)(2,1)S(1)}, u32[]{:S(2)}, u32[]{:S(2)}) async-start(bf16[8,2,32,256]{3,2,1,0:T(8,128)(2,1)} %get-tuple-element.16), calls=%async_computation | async-start | bytes 524288 | tf_op jit(solution)/shard_map/all_to_all | solution.py:256
  10.8 15.4 %copy-start = (bf16[256,256]{1,0:T(8,128)(2,1)S(1)}, bf16[256,256]{1,0:T(8,128)(2,1)}, u32[]{:S(2)}) copy-start(bf16[256,256]{1,0:T(8,128)(2,1)} %refs_0_) | copy-start | bytes 393220
  13.4 19.7 %collective-permute-start.3 = (bf16[256,1024]{1,0:T(8,128)(2,1)}, bf16[256,1024]{1,0:T(8,128)(2,1)S(1)}, u32[]{:S(2)}, u32[]{:S(2)}) collective-permute-start(bf16[256,1024]{1,0:T(8,128)(2,1)} %get-tuple-element.27), channel_id=1, source_target_pairs={{0,1},{1,0},{2,3},{3,2},{4,5},{5,4},{6,7},{7,6},{8,9},{9,8},{10,11... | collective-permute-start | bytes 1572872 | tf_op jit(solution)/shard_map/ppermute | solution.py:248
  13.4 19.7 %collective-permute-start.2 = (bf16[256,1024]{1,0:T(8,128)(2,1)}, bf16[256,1024]{1,0:T(8,128)(2,1)S(1)}, u32[]{:S(2)}, u32[]{:S(2)}) collective-permute-start(bf16[256,1024]{1,0:T(8,128)(2,1)} %get-tuple-element.29), channel_id=1, source_target_pairs={{0,3},{1,2},{2,1},{3,0},{4,7},{5,6},{6,5},{7,4},{8,11},{9,10},{10,... | collective-permute-start | bytes 1572872 | tf_op jit(solution)/shard_map/ppermute | solution.py:248
  22.6 13.1 %all-to-all-start.1 = ((bf16[16,32,256]{2,1,0:T(8,128)(2,1)}), bf16[16,32,256]{2,1,0:T(8,128)(2,1)S(1)}, u32[]{:S(2)}, u32[]{:S(2)}) async-start(bf16[16,32,256]{2,1,0:T(8,128)(2,1)} %bitcast.1), calls=%async_computation.1 | async-start | bytes 524288 | tf_op jit(solution)/shard_map/all_to_all | solution.py:259
  26.3 6.8 %collective-permute-start.1 = (bf16[256,256]{1,0:T(8,128)(2,1)S(1)}, bf16[256,256]{1,0:T(8,128)(2,1)S(1)}, u32[]{:S(2)}, u32[]{:S(2)}) collective-permute-start(bf16[256,256]{1,0:T(8,128)(2,1)S(1)} %copy-done), channel_id=1, source_target_pairs={{0,2},{1,3},{2,0},{3,1},{4,6},{5,7},{6,4},{7,5},{8,10},{9,11},{10,... | collective-permute-start | bytes 393224 | tf_op jit(solution)/shard_map/ppermute | solution.py:248

commit v4 on v3

--- a/solution.py
+++ b/solution.py
@@ -17,41 +17,42 @@
     return pad, (pad + lines) | 1, lines | 1
 
 
-def conv_kernel(x_ref, bias_ref, y_ref, taps, rows, sums):
+def conv_kernel(x_ref, bias_ref, y_ref, taps, rows, sums, result, sems):
     blocks, _, chans, seq_dev = x_ref.shape
     halves = seq_dev // LANES
     lines = blocks * halves
     length = lines * LANES
-    lane = lax.broadcasted_iota(jnp.int32, (chans, LANES), 1)
+    pad, row_pitch, sum_pitch = pitches(lines)
 
     taps[:, pl.ds(0, LANES)] = jnp.zeros((chans, LANES), jnp.float32)
-    pad, row_pitch, sum_pitch = pitches(lines)
     for phase in range(PHASES):
         for chan in range(chans):
             rows[phase, pl.ds(chan * row_pitch, pad), :] = jnp.zeros((pad, LANES), jnp.float32)
-    older = [[jnp.zeros((chans, LANES), jnp.float32)] * PHASES] * (PHASES - 1)
+    size = 8 if chans % 8 == 0 else chans
+    lane = lax.broadcasted_iota(jnp.int32, (size, LANES), 1)
+    bits = PHASES.bit_length() - 1
+    odd = [lane // (SUB << bit) % 2 == 1 for bit in range(bits)]
+    for begin in range(0, chans, size):
+        history = [[[jnp.zeros((size, LANES), jnp.float32)] * PHASES] * (1 << bit) for bit in range(bits)]
+        for line in range(lines):
+            block, half = divmod(line, halves)
+            fresh = x_ref[block, 0, pl.ds(begin, size), pl.ds(half * LANES, LANES)].astype(jnp.float32)
+            level = [fresh] + [pltpu.roll(fresh, SUB * turn, axis=1) for turn in range(1, PHASES)]
+            for bit in range(bits):
+                step = 1 << bit
+                past = history[bit][0]
+                history[bit] = history[bit][1:] + [level]
+                level = [jnp.where(odd[bit], past[(turn + step) % PHASES], level[turn]) for turn in range(PHASES)]
+            for phase in range(PHASES):
+                rows[phase, pl.ds(begin * row_pitch + pad + line, size, stride=row_pitch), :] = level[-phase % PHASES]
     for line in range(lines):
         block, half = divmod(line, halves)
-        cut = pl.ds(half * LANES, LANES)
-        taps[:, pl.ds(LANES + line * LANES, LANES)] = x_ref[block, 1, :, cut].astype(jnp.float32)
-        fresh = x_ref[block, 0, :, cut].astype(jnp.float32)
-        now = [[fresh] + [pltpu.roll(fresh, SUB * turn, axis=1) for turn in range(1, PHASES)]] + older
-        older = now[: PHASES - 1]
-        for phase in range(PHASES):
-            made = now[0][-phase % PHASES]
-            for step in range(1, PHASES):
-                made = jnp.where(lane >= SUB * step, now[step][(step - phase) % PHASES], made)
-            rows[phase, pl.ds(pad + line, chans, stride=row_pitch), :] = made
+        taps[:, pl.ds(LANES + line * LANES, LANES)] = x_ref[block, 1, :, pl.ds(half * LANES, LANES)].astype(jnp.float32)
 
     def channel(chan, _):
         wide = jnp.broadcast_to(taps[pl.ds(chan, 1), :], (PACK, LANES + length))
         skew = pltpu.roll(wide, 0, 1, stride=1, stride_axis=0).astype(jnp.bfloat16)
-        parts = []
-        for part in range(SUB // PACK):
-            parts.append(pltpu.roll(skew, part * PACK, 1) if part else skew)
-        toeplitz = jnp.concatenate(
-            [part[:, (line + 1) * LANES : (line + 2) * LANES] for line in range(lines) for part in parts], 0
-        )
+        toeplitz = jnp.concatenate([skew[:, (line + 1) * LANES : (line + 2) * LANES] for line in range(lines)], 0)
         base = chan * row_pitch + pad
         left = jnp.concatenate(
             [
@@ -71,22 +72,32 @@
             sums[phase, pl.ds(chan * sum_pitch, lines), :] = total[phase * lines : (phase + 1) * lines]
         return 0
 
-    lax.fori_loop(0, chans, channel, 0, unroll=16 if chans % 16 == 0 else 1)
+    lax.fori_loop(0, chans, channel, 0, unroll=True)
 
     first = pl.multiple_of(lax.axis_index("ctx") * chans, chans)
-    bias = jnp.broadcast_to(bias_ref[pl.ds(first, chans), :], (chans, LANES))
-    older = [jnp.zeros((chans, LANES), jnp.float32)] * PHASES
-    for line in range(lines):
-        block, half = divmod(line, halves)
-        now = [sums[phase, pl.ds(line, chans, stride=sum_pitch), :] for phase in range(PHASES)]
-        cut = pl.ds(half * LANES, LANES)
-        value = now[0] + bias * x_ref[block, 0, :, cut].astype(jnp.float32)
-        for phase in range(1, PHASES):
-            mixed = jnp.where(lane < LANES - SUB * phase, now[phase], older[phase])
-            value = value + pltpu.roll(mixed, SUB * phase, axis=1)
-        older = now
+    size = PACK if chans % PACK == 0 else chans
+    lane = lax.broadcasted_iota(jnp.int32, (size, LANES), 1)
+    copies = []
+    for begin in range(0, chans, size):
+        part = pl.ds(begin, size)
+        bias = jnp.broadcast_to(bias_ref[pl.ds(first + begin, size), :], (size, LANES))
+        older = [jnp.zeros((size, LANES), jnp.float32)] * PHASES
+        for line in range(lines):
+            block, half = divmod(line, halves)
+            cut = pl.ds(half * LANES, LANES)
+            now = [sums[phase, pl.ds(begin * sum_pitch + line, size, stride=sum_pitch), :] for phase in range(PHASES)]
+            value = now[0] + bias * x_ref[block, 0, part, cut].astype(jnp.float32)
+            for phase in range(1, PHASES):
+                mixed = jnp.where(lane < LANES - SUB * phase, now[phase], older[phase])
+                value = value + pltpu.roll(mixed, SUB * phase, axis=1)
+            older = now
+            result[block, part, cut] = value.astype(jnp.bfloat16)
         for copy in range(y_ref.shape[1]):
-            y_ref[block, copy, :, cut] = value.astype(jnp.bfloat16)
+            sem = sems.at[begin // size, copy]
+            copies.append(pltpu.make_async_copy(result.at[:, part, :], y_ref.at[:, copy, part, :], sem))
+            copies[-1].start()
+    for copy in copies:
+        copy.wait()
 
 
 def convolve(pieces, bias, copies):
@@ -97,11 +108,13 @@
         conv_kernel,
         out_shape=jax.ShapeDtypeStruct((blocks, copies, chans, seq_dev), jnp.bfloat16),
         in_specs=[pl.BlockSpec(memory_space=pltpu.VMEM)] * 2,
-        out_specs=pl.BlockSpec(memory_space=pltpu.VMEM),
+        out_specs=pl.BlockSpec(memory_space=pltpu.HBM),
         scratch_shapes=[
             pltpu.VMEM((chans, LANES + lines * LANES), jnp.float32),
             pltpu.VMEM((PHASES, chans * row_pitch, LANES), jnp.float32),
             pltpu.VMEM((PHASES, chans * sum_pitch, LANES), jnp.float32),
+            pltpu.VMEM((blocks, chans, seq_dev), jnp.bfloat16),
+            pltpu.SemaphoreType.DMA((pl.cdiv(chans, PACK), copies)),
         ],
         compiler_params=pltpu.CompilerParams(vmem_limit_bytes=16 * 2**20),
         cost_estimate=pl.CostEstimate(flops=1, bytes_accessed=1, transcendentals=0),

time: 39.9 us -> 39.1 us (0.980)
  Pallas kernels: 6.72 us -> 5.91 us
    pallas_call x1, Pallas kernels: 3.07 us -> 2.27 us  [convolve(): pl.pallas_call(conv_kernel, out_shape=jax.ShapeDtypeStruct((blocks, copie...]
    all_to_all x1, waiting for transfers between devices: 2.58 us -> 1.8 us  [body(): lax.all_to_all(convolved.reshape(shards * chips, channels // shards, seq_...]
    ppermute x4, waiting for transfers between devices: 4.86 us -> 5.64 us  [exchange(): lax.ppermute(array, 'tp', [(i, partner(i, step, tp)) for i in range(tp)])]
  transfers between devices with their start and end apart: 6 -> 6, of which waited for: 3 -> 3; matrix products, arithmetic and copies ran while one was open for 7% -> 7% of each run, Pallas kernels for 8% -> 6%
where the time goes in v4:
time: 39.1 us; the launch traced here: 38.8 us
  starting transfers between devices  15.1 us (39%)
  waiting for transfers between devices  12.8 us (33%)
  Pallas kernels  5.91 us (15%)
  local copies, waits for them, and re-layouts  2.66 us (7%)
  blocking collectives  2.18 us (6%)
    all_to_all x1, starting transfers between devices, body(): lax.all_to_all(pieces, 'ctx', split_axis=0, concat_axis=0, tiled=True)  5.81 us
    ppermute x4, waiting for transfers between devices, exchange(): lax.ppermute(array, 'tp', [(i, partner(i, step, tp)) for i in range(tp)])  5.64 us
    ppermute x4, starting transfers between devices, exchange(): lax.ppermute(array, 'tp', [(i, partner(i, step, tp)) for i in range(tp)])  5.64 us
    all_to_all x1, waiting for transfers between devices, body(): lax.all_to_all(pieces, 'ctx', split_axis=0, concat_axis=0, tiled=True)  5.35 us
    all_to_all x1, starting transfers between devices, body(): lax.all_to_all(convolved.reshape(shards * chips, channels // shards, seq_...  3.7 us
    dynamic_slice x1, local copies, waits for them, and re-layouts, body(): lax.dynamic_slice_in_dim(w_out, partner(me, step, tp) * feats, feats, 1)  2.52 us
    pallas_call x1, Pallas kernels, convolve(): pl.pallas_call(conv_kernel, out_shape=jax.ShapeDtypeStruct((blocks, copie...  2.27 us
    all_gather x1, blocking collectives, body(): lax.all_gather(gated_vals, 'tp', axis=0, tiled=True, axis_index_groups=[[...  2.18 us
  transfers between devices with their start and end apart: 6, of which 3 were waited for; matrix products, arithmetic and copies ran while one was open for 7% of the time, Pallas kernels for 6%

profile of v4, /device:TPU:0, one launch (start us, length us, event | category | flops | bytes accessed | tf_op | source)
XLA Modules:
  0.0 38.8 jit_solution(7193883923582383972)
XLA Ops:
  0.0 2.0 %prepare.1 = (bf16[8,2,32,256]{3,2,1,0:T(8,128)(2,1)}, bf16[256,1024]{1,0:T(8,128)(2,1)S(1)}) custom-call(bf16[256,256]{1,0:T(8,128)(2,1)} %key_ref.1, bf16[256,256]{1,0:T(8,128)(2,1)} %value_ref.1, f32[256,256]{1,0:T(8,128)} %taps_ref.1, bf16[256,4096]{1,0:T(8,128)(2,1)} %w_ref.1), custom_call_target="tpu_custom_call" | custom-call | flops 65536 | bytes 4194304 | tf_op jit(solution)/shard_map/prepare/pallas_call | solution.py:174
  2.0 0.0 copy-start.1
  2.0 3.0 %collective-permute-start = (bf16[256,1024]{1,0:T(8,128)(2,1)S(1)}, bf16[256,1024]{1,0:T(8,128)(2,1)S(1)}, u32[]{:S(2)}, u32[]{:S(2)}) collective-permute-start(bf16[256,1024]{1,0:T(8,128)(2,1)S(1)} %get-tuple-element.17), channel_id=1, source_target_pairs={{0,2},{1,3},{2,0},{3,1},{4,6},{5,7},{6,4},{7,5},{8,10},{9,11},{10,... | collective-permute-start | bytes 1572872 | tf_op jit(solution)/shard_map/ppermute | solution.py:261
  5.0 5.8 %all-to-all-start = ((bf16[8,2,32,256]{3,2,1,0:T(8,128)(2,1)}), bf16[8,2,32,256]{3,2,1,0:T(8,128)(2,1)S(1)}, u32[]{:S(2)}, u32[]{:S(2)}) async-start(bf16[8,2,32,256]{3,2,1,0:T(8,128)(2,1)} %get-tuple-element.16), calls=%async_computation | async-start | bytes 524288 | tf_op jit(solution)/shard_map/all_to_all | solution.py:269
  10.8 0.0 copy-start
  10.9 2.5 %constant_dynamic-slice_fusion = (bf16[256,1024]{1,0:T(8,128)(2,1)}, bf16[256,1024]{1,0:T(8,128)(2,1)S(1)}, bf16[256,1024]{1,0:T(8,128)(2,1)}) fusion(bf16[256,4096]{1,0:T(8,128)(2,1)} %w_ref.1, s32[]{:T(128)S(6)} %select_n.44, s32[]{:T(128)S(6)} %select_n.37, s32[]{:T(128)S(6)} %select_n.42), kind=kLoop, calls=%fused_computation | loop fusion | bytes 3145740 | tf_op jit(solution)/shard_map/dynamic_slice | solution.py:265
  13.4 0.0 collective-permute-start.3
  13.4 0.6 %collective-permute-start.2 = (bf16[256,1024]{1,0:T(8,128)(2,1)}, bf16[256,1024]{1,0:T(8,128)(2,1)S(1)}, u32[]{:S(2)}, u32[]{:S(2)}) collective-permute-start(bf16[256,1024]{1,0:T(8,128)(2,1)} %get-tuple-element.29), channel_id=1, source_target_pairs={{0,3},{1,2},{2,1},{3,0},{4,7},{5,6},{6,5},{7,4},{8,11},{9,10},{10,... | collective-permute-start | bytes 1572872 | tf_op jit(solution)/shard_map/ppermute | solution.py:261
  14.0 0.0 copy-done.1
  14.0 0.1 copy.7.bias_ref
  14.1 5.4 %all-to-all-done.x_ref = bf16[8,2,32,256]{3,2,1,0:T(8,128)(2,1)S(1)} async-done(((bf16[8,2,32,256]{3,2,1,0:T(8,128)(2,1)}), bf16[8,2,32,256]{3,2,1,0:T(8,128)(2,1)S(1)}, u32[]{:S(2)}, u32[]{:S(2)}) %all-to-all-start) | async-done | bytes 262176 | tf_op jit(solution)/shard_map/all_to_all | solution.py:269
  19.5 2.3 %toeplitz_conv.1 = bf16[8,2,32,256]{3,2,1,0:T(8,128)(2,1)} custom-call(bf16[8,2,32,256]{3,2,1,0:T(8,128)(2,1)S(1)} %all-to-all-done.x_ref, f32[256,1]{1,0:T(8,128)S(1)} %copy.7.bias_ref), custom_call_target="tpu_custom_call" | custom-call | flops 1 | bytes 1 | tf_op jit(solution)/shard_map/toeplitz_conv/pallas_call | solution.py:107
  21.8 0.0 collective-permute-done.refs_0_
  21.8 3.7 %all-to-all-start.1 = ((bf16[16,32,256]{2,1,0:T(8,128)(2,1)}), bf16[16,32,256]{2,1,0:T(8,128)(2,1)S(1)}, u32[]{:S(2)}, u32[]{:S(2)}) async-start(bf16[16,32,256]{2,1,0:T(8,128)(2,1)} %bitcast.1), calls=%async_computation.1 | async-start | bytes 524288 | tf_op jit(solution)/shard_map/all_to_all | solution.py:272
  25.5 0.0 copy-done
  25.5 2.0 %collective-permute-start.1 = (bf16[256,256]{1,0:T(8,128)(2,1)S(1)}, bf16[256,256]{1,0:T(8,128)(2,1)S(1)}, u32[]{:S(2)}, u32[]{:S(2)}) collective-permute-start(bf16[256,256]{1,0:T(8,128)(2,1)S(1)} %copy-done), channel_id=1, source_target_pairs={{0,2},{1,3},{2,0},{3,1},{4,6},{5,7},{6,4},{7,5},{8,10},{9,11},{10,... | collective-permute-start | bytes 393224 | tf_op jit(solution)/shard_map/ppermute | solution.py:261
  27.5 5.6 %collective-permute-done.1.refs_1_ = bf16[256,256]{1,0:T(8,128)(2,1)S(1)} collective-permute-done((bf16[256,256]{1,0:T(8,128)(2,1)S(1)}, bf16[256,256]{1,0:T(8,128)(2,1)S(1)}, u32[]{:S(2)}, u32[]{:S(2)}) %collective-permute-start.1) | collective-permute-done | bytes 131104 | tf_op jit(solution)/shard_map/ppermute | solution.py:261
  33.1 0.0 collective-permute-done.3.refs_2_
  33.1 0.0 collective-permute-done.2.refs_1_
  33.1 1.8 %all-to-all-done.1 = bf16[16,32,256]{2,1,0:T(8,128)(2,1)S(1)} async-done(((bf16[16,32,256]{2,1,0:T(8,128)(2,1)}), bf16[16,32,256]{2,1,0:T(8,128)(2,1)S(1)}, u32[]{:S(2)}, u32[]{:S(2)}) %all-to-all-start.1) | async-done | bytes 262176 | tf_op jit(solution)/shard_map/all_to_all | solution.py:272
  34.9 0.1 gate.1
  35.0 2.2 %all_gather.3.gated_ref = bf16[1024,256]{1,0:T(8,128)(2,1)S(1)} all-gather(bf16[512,256]{1,0:T(8,128)(2,1)S(1)} %gate.1), channel_id=1, replica_groups={{0,1},{2,3},{4,5},{6,7},{8,9},{10,11},{12,13},{14,15},{16,17},{18,19},{..., dimensions={0}, use_global_device_ids=true | all-gather | bytes 786432 | tf_op jit(solution)/shard_map/all_gather | solution.py:285
  37.2 1.6 %project.1 = bf16[1024,256]{1,0:T(8,128)(2,1)} custom-call(bf16[1024,256]{1,0:T(8,128)(2,1)S(1)} %all_gather.3.gated_ref, bf16[256,1024]{1,0:T(8,128)(2,1)S(1)} %get-tuple-element.23.own_ref, bf16[256,1024]{1,0:T(8,128)(2,1)S(1)} %collective-permute-done.refs_0_, bf16[256,1024]{1,0:T(8,128)(2,1)S(1)} %collective-permute-done.2.refs_1_, ...), custom_call_target="tpu_custom_call" | custom-call | flops 536870912 | bytes 2621440 | tf_op jit(solution)/shard_map/project/pallas_call | solution.py:239
Async XLA Ops:
  2.0 12.0 %copy-start.1 = (f32[256]{0:T(256)S(1)}, f32[256]{0:T(256)}, u32[]{:S(2)}) copy-start(f32[256]{0:T(256)} %param.10) | copy-start | bytes 3076
  2.0 19.8 %collective-permute-start = (bf16[256,1024]{1,0:T(8,128)(2,1)S(1)}, bf16[256,1024]{1,0:T(8,128)(2,1)S(1)}, u32[]{:S(2)}, u32[]{:S(2)}) collective-permute-start(bf16[256,1024]{1,0:T(8,128)(2,1)S(1)} %get-tuple-element.17), channel_id=1, source_target_pairs={{0,2},{1,3},{2,0},{3,1},{4,6},{5,7},{6,4},{7,5},{8,10},{9,11},{10,... | collective-permute-start | bytes 1572872 | tf_op jit(solution)/shard_map/ppermute | solution.py:261
  5.0 14.4 %all-to-all-start = ((bf16[8,2,32,256]{3,2,1,0:T(8,128)(2,1)}), bf16[8,2,32,256]{3,2,1,0:T(8,128)(2,1)S(1)}, u32[]{:S(2)}, u32[]{:S(2)}) async-start(bf16[8,2,32,256]{3,2,1,0:T(8,128)(2,1)} %get-tuple-element.16), calls=%async_computation | async-start | bytes 524288 | tf_op jit(solution)/shard_map/all_to_all | solution.py:269
  10.8 14.6 %copy-start = (bf16[256,256]{1,0:T(8,128)(2,1)S(1)}, bf16[256,256]{1,0:T(8,128)(2,1)}, u32[]{:S(2)}) copy-start(bf16[256,256]{1,0:T(8,128)(2,1)} %refs_0_) | copy-start | bytes 393220
  13.4 19.7 %collective-permute-start.3 = (bf16[256,1024]{1,0:T(8,128)(2,1)}, bf16[256,1024]{1,0:T(8,128)(2,1)S(1)}, u32[]{:S(2)}, u32[]{:S(2)}) collective-permute-start(bf16[256,1024]{1,0:T(8,128)(2,1)} %get-tuple-element.27), channel_id=1, source_target_pairs={{0,1},{1,0},{2,3},{3,2},{4,5},{5,4},{6,7},{7,6},{8,9},{9,8},{10,11... | collective-permute-start | bytes 1572872 | tf_op jit(solution)/shard_map/ppermute | solution.py:261
  13.4 19.7 %collective-permute-start.2 = (bf16[256,1024]{1,0:T(8,128)(2,1)}, bf16[256,1024]{1,0:T(8,128)(2,1)S(1)}, u32[]{:S(2)}, u32[]{:S(2)}) collective-permute-start(bf16[256,1024]{1,0:T(8,128)(2,1)} %get-tuple-element.29), channel_id=1, source_target_pairs={{0,3},{1,2},{2,1},{3,0},{4,7},{5,6},{6,5},{7,4},{8,11},{9,10},{10,... | collective-permute-start | bytes 1572872 | tf_op jit(solution)/shard_map/ppermute | solution.py:261
  21.8 13.1 %all-to-all-start.1 = ((bf16[16,32,256]{2,1,0:T(8,128)(2,1)}), bf16[16,32,256]{2,1,0:T(8,128)(2,1)S(1)}, u32[]{:S(2)}, u32[]{:S(2)}) async-start(bf16[16,32,256]{2,1,0:T(8,128)(2,1)} %bitcast.1), calls=%async_computation.1 | async-start | bytes 524288 | tf_op jit(solution)/shard_map/all_to_all | solution.py:272
  25.5 7.6 %collective-permute-start.1 = (bf16[256,256]{1,0:T(8,128)(2,1)S(1)}, bf16[256,256]{1,0:T(8,128)(2,1)S(1)}, u32[]{:S(2)}, u32[]{:S(2)}) collective-permute-start(bf16[256,256]{1,0:T(8,128)(2,1)S(1)} %copy-done), channel_id=1, source_target_pairs={{0,2},{1,3},{2,0},{3,1},{4,6},{5,7},{6,4},{7,5},{8,10},{9,11},{10,... | collective-permute-start | bytes 393224 | tf_op jit(solution)/shard_map/ppermute | solution.py:261

commit v5 on v4

--- a/solution.py
+++ b/solution.py
@@ -9,6 +9,7 @@
 PACK = 16
 SUB = 16
 PHASES = LANES // SUB
+PARTS = 4
 CORES = 2
 
 
@@ -215,38 +216,67 @@
     )(convolved, *(pltpu.with_memory_space_constraint(x, pltpu.VMEM) for x in gates))
 
 
-def project_kernel(gated_ref, own_ref, *refs):
-    weights, out_ref = (own_ref, *refs[:-1]), refs[-1]
-    tp = lax.axis_size("tp")
-    channels = own_ref.shape[0]
-    core = lax.axis_index("tp") % CORES
+def project_own_kernel(gated_ref, *refs):
+    *weights, sum_ref, turned_ref = refs
+    mine, others = weights[: len(weights) // CORES], weights[len(weights) // CORES :]
+    channels = weights[0].shape[0]
     total = None
-    for weight_ref, (chips, other) in zip(weights, [(0, 0)] + exchanges(tp)):
-        place = (core + CORES - other) % CORES * (tp // CORES) + chips
+    for place, weight_ref in enumerate(mine):
         term = lax.dot_general(
             weight_ref[...],
-            gated_ref[pl.ds(pl.multiple_of(place * channels, channels), channels), :],
+            gated_ref[pl.ds(place * channels, channels), :],
             (((0,), (0,)), ((), ())),
             preferred_element_type=jnp.float32,
         )
         total = term if total is None else total + term
-    out_ref[...] = total.astype(jnp.bfloat16)
-
-
-def project(gathered, own, weights):
-    channels, feats = own.shape
-    rows, seq_dev = gathered.shape
+    sum_ref[...] = total
+    for place, weight_ref in enumerate(others):
+        turned_ref[:, pl.ds(place * channels, channels)] = weight_ref[...].T
+
+
+def project_other_kernel(gated_ref, sum_ref, turned_ref, out_ref, held, sems):
+    parts = sems.shape[0]
+    count = out_ref.shape[0] // parts
+    copies = []
+    for part in range(parts):
+        rows = pl.ds(part * count, count)
+        term = jnp.dot(turned_ref[rows, :], gated_ref[...], preferred_element_type=jnp.float32)
+        held[rows, :] = (sum_ref[rows, :] + term).astype(jnp.bfloat16)
+        copies.append(pltpu.make_async_copy(held.at[rows, :], out_ref.at[rows, :], sems.at[part]))
+        copies[-1].start()
+    for copy in copies:
+        copy.wait()
+
+
+def project(gated_vals, others, weights):
+    channels, feats = weights[0].shape
+    rows, seq_dev = gated_vals.shape
+    vmem = pl.BlockSpec(memory_space=pltpu.VMEM)
+    cost = pl.CostEstimate(
+        flops=2 * rows * feats * seq_dev, bytes_accessed=2 * rows * (feats + seq_dev), transcendentals=0
+    )
+    so_far, turned = pl.pallas_call(
+        project_own_kernel,
+        out_shape=[
+            jax.ShapeDtypeStruct((feats, seq_dev), jnp.float32),
+            jax.ShapeDtypeStruct((feats, rows), jnp.bfloat16),
+        ],
+        in_specs=[vmem] * (1 + len(weights)),
+        out_specs=[vmem] * 2,
+        compiler_params=pltpu.CompilerParams(vmem_limit_bytes=16 * 2**20),
+        cost_estimate=cost,
+        name="project_own",
+    )(gated_vals, *weights)
     return pl.pallas_call(
-        project_kernel,
+        project_other_kernel,
         out_shape=jax.ShapeDtypeStruct((feats, seq_dev), jnp.bfloat16),
-        in_specs=[pl.BlockSpec(memory_space=pltpu.VMEM)] * (2 + len(weights)),
-        out_specs=pl.BlockSpec(memory_space=pltpu.VMEM),
-        compiler_params=pltpu.CompilerParams(vmem_limit_bytes=24 * 2**20),
-        cost_estimate=pl.CostEstimate(
-            flops=2 * rows * feats * seq_dev, bytes_accessed=2 * rows * (feats + seq_dev), transcendentals=0
-        ),
-        name="project",
-    )(gathered, own, *weights)
+        in_specs=[vmem] * 3,
+        out_specs=pl.BlockSpec(memory_space=pltpu.HBM),
+        scratch_shapes=[pltpu.VMEM((feats, seq_dev), jnp.bfloat16), pltpu.SemaphoreType.DMA((PARTS,))],
+        compiler_params=pltpu.CompilerParams(vmem_limit_bytes=16 * 2**20),
+        cost_estimate=cost,
+        name="project_other",
+    )(others, so_far, turned)
 
 
 def body(gate_q, key_k, value_v, filter_taps, skip_bias, w_out):
@@ -282,14 +312,10 @@
     own = lax.dynamic_slice_in_dim(w_out, me * feats, feats, 1)
     convolved, own, gates, weights = lax.optimization_barrier((convolved, own, gates, weights))
     gated_vals = gate(convolved.reshape(shards, chips, channels // shards, seq_dev), gates)
-    gathered = lax.all_gather(
-        gated_vals,
-        "tp",
-        axis=0,
-        tiled=True,
-        axis_index_groups=[[chip * CORES + core for core in range(CORES)] for chip in range(chips)],
-    )
-    return project(gathered, own, weights)
+    others = exchange(gated_vals, (0, 1))
+    blocks = dict(zip([(0, 0)] + exchanges(tp), [own, *weights]))
+    ordered = [blocks[chip, core] for core in range(CORES) for chip in range(chips)]
+    return project(gated_vals, others, ordered)
 
 
 def solution(mesh):

time: 39.1 us -> 38.1 us (0.974)
  blocking collectives: 2.18 us -> 0 us
  waiting for transfers between devices: 12.8 us -> 13.7 us
    all_gather x1 -> x0, blocking collectives: 2.18 us -> none  [body(): lax.all_gather(gated_vals, 'tp', axis=0, tiled=True, axis_index_groups=[[...]
    ppermute x4 -> x5, waiting for transfers between devices: 5.64 us -> 6.55 us  [exchange(): lax.ppermute(array, 'tp', [(i, partner(i, step, tp)) for i in range(tp)])]
    pallas_call x1 -> x2, Pallas kernels: 1.58 us -> 1.78 us  [the longest x1 1.17 us: project(): pl.pallas_call(project_other_kernel, out_shape=jax.ShapeDtypeStruct((feat...]
    ppermute x4 -> x5, starting transfers between devices: 5.64 us -> 5.71 us  [exchange(): lax.ppermute(array, 'tp', [(i, partner(i, step, tp)) for i in range(tp)])]
  transfers between devices with their start and end apart: 6 -> 7, of which waited for: 3 -> 4; matrix products, arithmetic and copies ran while one was open for 7% -> 7% of each run, Pallas kernels for 6% -> 8%
where the time goes in v5:
time: 38.1 us; the launch traced here: 37.8 us
  starting transfers between devices  15.2 us (40%)
  waiting for transfers between devices  13.7 us (36%)
  Pallas kernels  6.12 us (16%)
  local copies, waits for them, and re-layouts  2.67 us (7%)
    ppermute x5, waiting for transfers between devices, exchange(): lax.ppermute(array, 'tp', [(i, partner(i, step, tp)) for i in range(tp)])  6.55 us
    all_to_all x1, starting transfers between devices, body(): lax.all_to_all(pieces, 'ctx', split_axis=0, concat_axis=0, tiled=True)  5.81 us
    ppermute x5, starting transfers between devices, exchange(): lax.ppermute(array, 'tp', [(i, partner(i, step, tp)) for i in range(tp)])  5.71 us
    all_to_all x1, waiting for transfers between devices, body(): lax.all_to_all(pieces, 'ctx', split_axis=0, concat_axis=0, tiled=True)  5.34 us
    all_to_all x1, starting transfers between devices, body(): lax.all_to_all(convolved.reshape(shards * chips, channels // shards, seq_...  3.7 us
    dynamic_slice x1, local copies, waits for them, and re-layouts, body(): lax.dynamic_slice_in_dim(w_out, partner(me, step, tp) * feats, feats, 1)  2.53 us
    pallas_call x1, Pallas kernels, convolve(): pl.pallas_call(conv_kernel, out_shape=jax.ShapeDtypeStruct((blocks, copie...  2.27 us
    pallas_call x1, Pallas kernels, prepare(): pl.pallas_call(prepare_kernel, out_shape=[pltpu.VMEM((shards, 2, channels...  1.99 us
  transfers between devices with their start and end apart: 7, of which 4 were waited for; matrix products, arithmetic and copies ran while one was open for 7% of the time, Pallas kernels for 8%

profile of v5, /device:TPU:0, one launch (start us, length us, event | category | flops | bytes accessed | tf_op | source)
XLA Modules:
  0.0 37.8 jit_solution(172557973458699028)
XLA Ops:
  0.0 2.0 %prepare.1 = (bf16[8,2,32,256]{3,2,1,0:T(8,128)(2,1)}, bf16[256,1024]{1,0:T(8,128)(2,1)S(1)}) custom-call(bf16[256,256]{1,0:T(8,128)(2,1)} %key_ref.1, bf16[256,256]{1,0:T(8,128)(2,1)} %value_ref.1, f32[256,256]{1,0:T(8,128)} %taps_ref.1, bf16[256,4096]{1,0:T(8,128)(2,1)} %w_ref.1), custom_call_target="tpu_custom_call" | custom-call | flops 65536 | bytes 4194304 | tf_op jit(solution)/shard_map/prepare/pallas_call | solution.py:175
  2.0 0.0 copy-start.1
  2.0 3.0 %collective-permute-start = (bf16[256,1024]{1,0:T(8,128)(2,1)S(1)}, bf16[256,1024]{1,0:T(8,128)(2,1)S(1)}, u32[]{:S(2)}, u32[]{:S(2)}) collective-permute-start(bf16[256,1024]{1,0:T(8,128)(2,1)S(1)} %get-tuple-element.19), channel_id=1, source_target_pairs={{0,2},{1,3},{2,0},{3,1},{4,6},{5,7},{6,4},{7,5},{8,10},{9,11},{10,... | collective-permute-start | bytes 1572872 | tf_op jit(solution)/shard_map/ppermute | solution.py:291
  5.0 5.8 %all-to-all-start = ((bf16[8,2,32,256]{3,2,1,0:T(8,128)(2,1)}), bf16[8,2,32,256]{3,2,1,0:T(8,128)(2,1)S(1)}, u32[]{:S(2)}, u32[]{:S(2)}) async-start(bf16[8,2,32,256]{3,2,1,0:T(8,128)(2,1)} %get-tuple-element.18), calls=%async_computation | async-start | bytes 524288 | tf_op jit(solution)/shard_map/all_to_all | solution.py:299
  10.9 0.0 copy-start
  10.9 2.5 %constant_dynamic-slice_fusion = (bf16[256,1024]{1,0:T(8,128)(2,1)}, bf16[256,1024]{1,0:T(8,128)(2,1)S(1)}, bf16[256,1024]{1,0:T(8,128)(2,1)}) fusion(bf16[256,4096]{1,0:T(8,128)(2,1)} %w_ref.1, s32[]{:T(128)S(6)} %select_n.44, s32[]{:T(128)S(6)} %select_n.37, s32[]{:T(128)S(6)} %select_n.42), kind=kLoop, calls=%fused_computation | loop fusion | bytes 3145740 | tf_op jit(solution)/shard_map/dynamic_slice | solution.py:295
  13.4 0.0 collective-permute-start.3
  13.4 0.6 %collective-permute-start.2 = (bf16[256,1024]{1,0:T(8,128)(2,1)}, bf16[256,1024]{1,0:T(8,128)(2,1)S(1)}, u32[]{:S(2)}, u32[]{:S(2)}) collective-permute-start(bf16[256,1024]{1,0:T(8,128)(2,1)} %get-tuple-element.33), channel_id=1, source_target_pairs={{0,3},{1,2},{2,1},{3,0},{4,7},{5,6},{6,5},{7,4},{8,11},{9,10},{10,... | collective-permute-start | bytes 1572872 | tf_op jit(solution)/shard_map/ppermute | solution.py:291
  14.0 0.0 copy-done.1
  14.0 0.1 copy.7.bias_ref
  14.1 5.3 %all-to-all-done.x_ref = bf16[8,2,32,256]{3,2,1,0:T(8,128)(2,1)S(1)} async-done(((bf16[8,2,32,256]{3,2,1,0:T(8,128)(2,1)}), bf16[8,2,32,256]{3,2,1,0:T(8,128)(2,1)S(1)}, u32[]{:S(2)}, u32[]{:S(2)}) %all-to-all-start) | async-done | bytes 262176 | tf_op jit(solution)/shard_map/all_to_all | solution.py:299
  19.5 2.3 %toeplitz_conv.1 = bf16[8,2,32,256]{3,2,1,0:T(8,128)(2,1)} custom-call(bf16[8,2,32,256]{3,2,1,0:T(8,128)(2,1)S(1)} %all-to-all-done.x_ref, f32[256,1]{1,0:T(8,128)S(1)} %copy.7.bias_ref), custom_call_target="tpu_custom_call" | custom-call | flops 1 | bytes 1 | tf_op jit(solution)/shard_map/toeplitz_conv/pallas_call | solution.py:108
  21.8 0.0 collective-permute-done.refs_1_
  21.8 3.7 %all-to-all-start.1 = ((bf16[16,32,256]{2,1,0:T(8,128)(2,1)}), bf16[16,32,256]{2,1,0:T(8,128)(2,1)S(1)}, u32[]{:S(2)}, u32[]{:S(2)}) async-start(bf16[16,32,256]{2,1,0:T(8,128)(2,1)} %bitcast.1), calls=%async_computation.1 | async-start | bytes 524288 | tf_op jit(solution)/shard_map/all_to_all | solution.py:302
  25.5 0.0 copy-done
  25.5 2.0 %collective-permute-start.1 = (bf16[256,256]{1,0:T(8,128)(2,1)S(1)}, bf16[256,256]{1,0:T(8,128)(2,1)S(1)}, u32[]{:S(2)}, u32[]{:S(2)}) collective-permute-start(bf16[256,256]{1,0:T(8,128)(2,1)S(1)} %copy-done), channel_id=1, source_target_pairs={{0,2},{1,3},{2,0},{3,1},{4,6},{5,7},{6,4},{7,5},{8,10},{9,11},{10,... | collective-permute-start | bytes 393224 | tf_op jit(solution)/shard_map/ppermute | solution.py:291
  27.5 5.6 %collective-permute-done.1.refs_1_ = bf16[256,256]{1,0:T(8,128)(2,1)S(1)} collective-permute-done((bf16[256,256]{1,0:T(8,128)(2,1)S(1)}, bf16[256,256]{1,0:T(8,128)(2,1)S(1)}, u32[]{:S(2)}, u32[]{:S(2)}) %collective-permute-start.1) | collective-permute-done | bytes 131104 | tf_op jit(solution)/shard_map/ppermute | solution.py:291
  33.1 0.0 collective-permute-done.3.refs_2_
  33.1 0.0 collective-permute-done.2.refs_3_
  33.1 1.8 %all-to-all-done.1 = bf16[16,32,256]{2,1,0:T(8,128)(2,1)S(1)} async-done(((bf16[16,32,256]{2,1,0:T(8,128)(2,1)}), bf16[16,32,256]{2,1,0:T(8,128)(2,1)S(1)}, u32[]{:S(2)}, u32[]{:S(2)}) %all-to-all-start.1) | async-done | bytes 262176 | tf_op jit(solution)/shard_map/all_to_all | solution.py:302
  34.9 0.1 gate.1.gated_ref
  35.0 0.1 collective-permute-start.4
  35.1 0.6 %project_own.1 = (f32[1024,256]{1,0:T(8,128)S(1)}, bf16[1024,512]{1,0:T(8,128)(2,1)S(1)}) custom-call(bf16[512,256]{1,0:T(8,128)(2,1)S(1)} %gate.1.gated_ref, bf16[256,1024]{1,0:T(8,128)(2,1)S(1)} %get-tuple-element.25.refs_0_, bf16[256,1024]{1,0:T(8,128)(2,1)S(1)} %collective-permute-done.refs_1_, bf16[256,1024]{1,0:T(8,128)(2,1)S(1)} %collective-permute-done.3.refs_2_, ...), custom_call_target="tpu_custom_call" | custom-call | flops 268435456 | bytes 1310720 | tf_op jit(solution)/shard_map/project_own/pallas_call | solution.py:258
  35.7 0.9 %collective-permute-done.4.gated_ref = bf16[512,256]{1,0:T(8,128)(2,1)S(1)} collective-permute-done((bf16[512,256]{1,0:T(8,128)(2,1)S(1)}, bf16[512,256]{1,0:T(8,128)(2,1)S(1)}, u32[]{:S(2)}, u32[]{:S(2)}) %collective-permute-start.4) | collective-permute-done | bytes 262176 | tf_op jit(solution)/shard_map/ppermute | solution.py:291
  36.6 1.2 %project_other.1 = bf16[1024,256]{1,0:T(8,128)(2,1)} custom-call(bf16[512,256]{1,0:T(8,128)(2,1)S(1)} %collective-permute-done.4.gated_ref, f32[1024,256]{1,0:T(8,128)S(1)} %get-tuple-element.29.sum_ref, bf16[1024,512]{1,0:T(8,128)(2,1)S(1)} %get-tuple-element.30.turned_ref), custom_call_target="tpu_custom_call" | custom-call | flops 268435456 | bytes 1310720 | tf_op jit(solution)/shard_map/project_other/pallas_call | solution.py:270
Async XLA Ops:
  2.0 12.0 %copy-start.1 = (f32[256]{0:T(256)S(1)}, f32[256]{0:T(256)}, u32[]{:S(2)}) copy-start(f32[256]{0:T(256)} %param.10) | copy-start | bytes 3076
  2.0 19.8 %collective-permute-start = (bf16[256,1024]{1,0:T(8,128)(2,1)S(1)}, bf16[256,1024]{1,0:T(8,128)(2,1)S(1)}, u32[]{:S(2)}, u32[]{:S(2)}) collective-permute-start(bf16[256,1024]{1,0:T(8,128)(2,1)S(1)} %get-tuple-element.19), channel_id=1, source_target_pairs={{0,2},{1,3},{2,0},{3,1},{4,6},{5,7},{6,4},{7,5},{8,10},{9,11},{10,... | collective-permute-start | bytes 1572872 | tf_op jit(solution)/shard_map/ppermute | solution.py:291
  5.0 14.4 %all-to-all-start = ((bf16[8,2,32,256]{3,2,1,0:T(8,128)(2,1)}), bf16[8,2,32,256]{3,2,1,0:T(8,128)(2,1)S(1)}, u32[]{:S(2)}, u32[]{:S(2)}) async-start(bf16[8,2,32,256]{3,2,1,0:T(8,128)(2,1)} %get-tuple-element.18), calls=%async_computation | async-start | bytes 524288 | tf_op jit(solution)/shard_map/all_to_all | solution.py:299
  10.9 14.6 %copy-start = (bf16[256,256]{1,0:T(8,128)(2,1)S(1)}, bf16[256,256]{1,0:T(8,128)(2,1)}, u32[]{:S(2)}) copy-start(bf16[256,256]{1,0:T(8,128)(2,1)} %refs_0_) | copy-start | bytes 393220
  13.4 19.7 %collective-permute-start.3 = (bf16[256,1024]{1,0:T(8,128)(2,1)}, bf16[256,1024]{1,0:T(8,128)(2,1)S(1)}, u32[]{:S(2)}, u32[]{:S(2)}) collective-permute-start(bf16[256,1024]{1,0:T(8,128)(2,1)} %get-tuple-element.31), channel_id=1, source_target_pairs={{0,1},{1,0},{2,3},{3,2},{4,5},{5,4},{6,7},{7,6},{8,9},{9,8},{10,11... | collective-permute-start | bytes 1572872 | tf_op jit(solution)/shard_map/ppermute | solution.py:291
  13.4 19.7 %collective-permute-start.2 = (bf16[256,1024]{1,0:T(8,128)(2,1)}, bf16[256,1024]{1,0:T(8,128)(2,1)S(1)}, u32[]{:S(2)}, u32[]{:S(2)}) collective-permute-start(bf16[256,1024]{1,0:T(8,128)(2,1)} %get-tuple-element.33), channel_id=1, source_target_pairs={{0,3},{1,2},{2,1},{3,0},{4,7},{5,6},{6,5},{7,4},{8,11},{9,10},{10,... | collective-permute-start | bytes 1572872 | tf_op jit(solution)/shard_map/ppermute | solution.py:291
  21.8 13.1 %all-to-all-start.1 = ((bf16[16,32,256]{2,1,0:T(8,128)(2,1)}), bf16[16,32,256]{2,1,0:T(8,128)(2,1)S(1)}, u32[]{:S(2)}, u32[]{:S(2)}) async-start(bf16[16,32,256]{2,1,0:T(8,128)(2,1)} %bitcast.1), calls=%async_computation.1 | async-start | bytes 524288 | tf_op jit(solution)/shard_map/all_to_all | solution.py:302
  25.5 7.6 %collective-permute-start.1 = (bf16[256,256]{1,0:T(8,128)(2,1)S(1)}, bf16[256,256]{1,0:T(8,128)(2,1)S(1)}, u32[]{:S(2)}, u32[]{:S(2)}) collective-permute-start(bf16[256,256]{1,0:T(8,128)(2,1)S(1)} %copy-done), channel_id=1, source_target_pairs={{0,2},{1,3},{2,0},{3,1},{4,6},{5,7},{6,4},{7,5},{8,10},{9,11},{10,... | collective-permute-start | bytes 393224 | tf_op jit(solution)/shard_map/ppermute | solution.py:291
  35.0 1.6 %collective-permute-start.4 = (bf16[512,256]{1,0:T(8,128)(2,1)S(1)}, bf16[512,256]{1,0:T(8,128)(2,1)S(1)}, u32[]{:S(2)}, u32[]{:S(2)}) collective-permute-start(bf16[512,256]{1,0:T(8,128)(2,1)S(1)} %gate.1.gated_ref), channel_id=1, source_target_pairs={{0,1},{1,0},{2,3},{3,2},{4,5},{5,4},{6,7},{7,6},{8,9},{9,8},{10,11... | collective-permute-start | bytes 786440 | tf_op jit(solution)/shard_map/ppermute | solution.py:291

commit v6 on v5

--- a/solution.py
+++ b/solution.py
@@ -13,6 +13,11 @@
 CORES = 2
 
 
+def ctx_order(shards):
+    middle = shards // 2
+    return [middle] + [shard for shard in range(shards) if shard != middle]
+
+
 def pitches(lines):
     pad = lines - PHASES
     return pad, (pad + lines) | 1, lines | 1
@@ -21,6 +26,7 @@
 def conv_kernel(x_ref, bias_ref, y_ref, taps, rows, sums, result, sems):
     blocks, _, chans, seq_dev = x_ref.shape
     halves = seq_dev // LANES
+    place = ctx_order(blocks).index
     lines = blocks * halves
     length = lines * LANES
     pad, row_pitch, sum_pitch = pitches(lines)
@@ -37,7 +43,7 @@
         history = [[[jnp.zeros((size, LANES), jnp.float32)] * PHASES] * (1 << bit) for bit in range(bits)]
         for line in range(lines):
             block, half = divmod(line, halves)
-            fresh = x_ref[block, 0, pl.ds(begin, size), pl.ds(half * LANES, LANES)].astype(jnp.float32)
+            fresh = x_ref[place(block), 0, pl.ds(begin, size), pl.ds(half * LANES, LANES)].astype(jnp.float32)
             level = [fresh] + [pltpu.roll(fresh, SUB * turn, axis=1) for turn in range(1, PHASES)]
             for bit in range(bits):
                 step = 1 << bit
@@ -48,7 +54,7 @@
                 rows[phase, pl.ds(begin * row_pitch + pad + line, size, stride=row_pitch), :] = level[-phase % PHASES]
     for line in range(lines):
         block, half = divmod(line, halves)
-        taps[:, pl.ds(LANES + line * LANES, LANES)] = x_ref[block, 1, :, pl.ds(half * LANES, LANES)].astype(jnp.float32)
+        taps[:, pl.ds(LANES + line * LANES, LANES)] = x_ref[place(block), 1, :, pl.ds(half * LANES, LANES)].astype(jnp.float32)
 
     def channel(chan, _):
         wide = jnp.broadcast_to(taps[pl.ds(chan, 1), :], (PACK, LANES + length))
@@ -87,12 +93,12 @@
             block, half = divmod(line, halves)
             cut = pl.ds(half * LANES, LANES)
             now = [sums[phase, pl.ds(begin * sum_pitch + line, size, stride=sum_pitch), :] for phase in range(PHASES)]
-            value = now[0] + bias * x_ref[block, 0, part, cut].astype(jnp.float32)
+            value = now[0] + bias * x_ref[place(block), 0, part, cut].astype(jnp.float32)
             for phase in range(1, PHASES):
                 mixed = jnp.where(lane < LANES - SUB * phase, now[phase], older[phase])
                 value = value + pltpu.roll(mixed, SUB * phase, axis=1)
             older = now
-            result[block, part, cut] = value.astype(jnp.bfloat16)
+            result[place(block), part, cut] = value.astype(jnp.bfloat16)
         for copy in range(y_ref.shape[1]):
             sem = sems.at[begin // size, copy]
             copies.append(pltpu.make_async_copy(result.at[:, part, :], y_ref.at[:, copy, part, :], sem))
@@ -158,11 +164,11 @@
         copies[-1].start()
     for load in loads:
         load.wait()
-    for shard in range(shards):
+    for place, shard in enumerate(ctx_order(shards)):
         rows = pl.ds(shard * share, share)
         signal = key[rows, :].astype(jnp.float32) * value[rows, :].astype(jnp.float32)
-        pieces_ref[shard, 0] = signal.astype(jnp.bfloat16)
-        pieces_ref[shard, 1] = taps[rows, :].astype(jnp.bfloat16)
+        pieces_ref[place, 0] = signal.astype(jnp.bfloat16)
+        pieces_ref[place, 1] = taps[rows, :].astype(jnp.bfloat16)
     for copy in copies:
         copy.wait()
 
@@ -198,9 +204,9 @@
     row = lax.axis_index("tp") // CORES
     for step, gate_ref in enumerate(gates):
         other = (row + chips - step) % chips
-        for block in range(blocks):
+        for place, block in enumerate(ctx_order(blocks)):
             rows = pl.ds(block * share, share)
-            gated = gate_ref[rows, :].astype(jnp.float32) * conv_ref[block, other].astype(jnp.float32)
+            gated = gate_ref[rows, :].astype(jnp.float32) * conv_ref[place, chips - 1 - other].astype(jnp.float32)
             out_ref[pl.ds(step * channels + block * share, share), :] = gated.astype(jnp.bfloat16)
 
 
@@ -296,7 +302,8 @@
     weights = [exchange(cut, step) for cut, step in zip(cuts, exchanges(tp))]
     gates = [gate_q] + [exchange(gate_q, (step, 0)) for step in range(1, chips)]
 
-    pieces = lax.all_to_all(pieces, "ctx", split_axis=0, concat_axis=0, tiled=True)
+    order = ctx_order(shards)
+    pieces = lax.all_to_all(pieces, "ctx", split_axis=0, concat_axis=0, tiled=True, axis_index_groups=[order])
     convolved = convolve(pieces, skip_bias.reshape(channels, 1), chips)
     convolved, weights[0] = lax.optimization_barrier((convolved, weights[0]))
     convolved = lax.all_to_all(
@@ -306,7 +313,7 @@
         concat_axis=0,
         tiled=True,
         axis_index_groups=[
-            [shard * tp + chip * CORES + core for shard in range(shards) for chip in range(chips)] for core in range(CORES)
+            [shard * tp + chip * CORES + core for shard in order for chip in reversed(range(chips))] for core in range(CORES)
         ],
     )
     own = lax.dynamic_slice_in_dim(w_out, me * feats, feats, 1)

time: 38.1 us -> 37.2 us (0.976)
  waiting for transfers between devices: 13.7 us -> 12.2 us
  starting transfers between devices: 15.2 us -> 15.8 us
    all_to_all x1, waiting for transfers between devices: 1.8 us -> 0.01 us  [body(): lax.all_to_all(convolved.reshape(shards * chips, channels // shards, seq_...]
    ppermute x5, waiting for transfers between devices: 6.55 us -> 8.31 us  [exchange(): lax.ppermute(array, 'tp', [(i, partner(i, step, tp)) for i in range(tp)])]
    all_to_all x1, waiting for transfers between devices: 5.34 us -> 3.85 us  [body(): lax.all_to_all(pieces, 'ctx', split_axis=0, concat_axis=0, tiled=True, ax...]
    all_to_all x1, starting transfers between devices: 3.7 us -> 5.12 us  [body(): lax.all_to_all(convolved.reshape(shards * chips, channels // shards, seq_...]
    ppermute x5, starting transfers between devices: 5.71 us -> 4.35 us  [exchange(): lax.ppermute(array, 'tp', [(i, partner(i, step, tp)) for i in range(tp)])]
    all_to_all x1, starting transfers between devices: 5.81 us -> 6.36 us  [body(): lax.all_to_all(pieces, 'ctx', split_axis=0, concat_axis=0, tiled=True, ax...]
  transfers between devices with their start and end apart: 7 -> 7, of which waited for: 4 -> 3; matrix products, arithmetic and copies ran while one was open for 7% -> 7% of each run, Pallas kernels for 8% -> 8%
where the time goes in v6:
time: 37.2 us; the launch traced here: 36.9 us
  starting transfers between devices  15.8 us (42%)
  waiting for transfers between devices  12.2 us (33%)
  Pallas kernels  6.13 us (16%)
  local copies, waits for them, and re-layouts  2.66 us (7%)
    ppermute x5, waiting for transfers between devices, exchange(): lax.ppermute(array, 'tp', [(i, partner(i, step, tp)) for i in range(tp)])  8.31 us
    all_to_all x1, starting transfers between devices, body(): lax.all_to_all(pieces, 'ctx', split_axis=0, concat_axis=0, tiled=True, ax...  6.36 us
    all_to_all x1, starting transfers between devices, body(): lax.all_to_all(convolved.reshape(shards * chips, channels // shards, seq_...  5.12 us
    ppermute x5, starting transfers between devices, exchange(): lax.ppermute(array, 'tp', [(i, partner(i, step, tp)) for i in range(tp)])  4.35 us
    all_to_all x1, waiting for transfers between devices, body(): lax.all_to_all(pieces, 'ctx', split_axis=0, concat_axis=0, tiled=True, ax...  3.85 us
    dynamic_slice x1, local copies, waits for them, and re-layouts, body(): lax.dynamic_slice_in_dim(w_out, partner(me, step, tp) * feats, feats, 1)  2.52 us
    pallas_call x1, Pallas kernels, convolve(): pl.pallas_call(conv_kernel, out_shape=jax.ShapeDtypeStruct((blocks, copie...  2.27 us
    pallas_call x1, Pallas kernels, prepare(): pl.pallas_call(prepare_kernel, out_shape=[pltpu.VMEM((shards, 2, channels...  1.99 us
  transfers between devices with their start and end apart: 7, of which 3 were waited for; matrix products, arithmetic and copies ran while one was open for 7% of the time, Pallas kernels for 8%

profile of v6, /device:TPU:0, one launch (start us, length us, event | category | flops | bytes accessed | tf_op | source)
XLA Modules:
  0.0 36.9 jit_solution(9201744099262056071)
XLA Ops:
  0.0 2.0 %prepare.1 = (bf16[8,2,32,256]{3,2,1,0:T(8,128)(2,1)}, bf16[256,1024]{1,0:T(8,128)(2,1)S(1)}) custom-call(bf16[256,256]{1,0:T(8,128)(2,1)} %key_ref.1, bf16[256,256]{1,0:T(8,128)(2,1)} %value_ref.1, f32[256,256]{1,0:T(8,128)} %taps_ref.1, bf16[256,4096]{1,0:T(8,128)(2,1)} %w_ref.1), custom_call_target="tpu_custom_call" | custom-call | flops 65536 | bytes 4194304 | tf_op jit(solution)/shard_map/prepare/pallas_call | solution.py:181
  2.0 0.0 copy-start.1
  2.0 3.0 %collective-permute-start = (bf16[256,1024]{1,0:T(8,128)(2,1)S(1)}, bf16[256,1024]{1,0:T(8,128)(2,1)S(1)}, u32[]{:S(2)}, u32[]{:S(2)}) collective-permute-start(bf16[256,1024]{1,0:T(8,128)(2,1)S(1)} %get-tuple-element.19), channel_id=1, source_target_pairs={{0,2},{1,3},{2,0},{3,1},{4,6},{5,7},{6,4},{7,5},{8,10},{9,11},{10,... | collective-permute-start | bytes 1572872 | tf_op jit(solution)/shard_map/ppermute | solution.py:297
  5.0 6.4 %all-to-all-start = ((bf16[8,2,32,256]{3,2,1,0:T(8,128)(2,1)}), bf16[8,2,32,256]{3,2,1,0:T(8,128)(2,1)S(1)}, u32[]{:S(2)}, u32[]{:S(2)}) async-start(bf16[8,2,32,256]{3,2,1,0:T(8,128)(2,1)} %get-tuple-element.18), calls=%async_computation | async-start | bytes 524288 | tf_op jit(solution)/shard_map/all_to_all | solution.py:306
  11.4 0.0 copy-start
  11.4 2.5 %constant_dynamic-slice_fusion = (bf16[256,1024]{1,0:T(8,128)(2,1)}, bf16[256,1024]{1,0:T(8,128)(2,1)S(1)}, bf16[256,1024]{1,0:T(8,128)(2,1)}) fusion(bf16[256,4096]{1,0:T(8,128)(2,1)} %w_ref.1, s32[]{:T(128)S(6)} %select_n.44, s32[]{:T(128)S(6)} %select_n.37, s32[]{:T(128)S(6)} %select_n.42), kind=kLoop, calls=%fused_computation | loop fusion | bytes 3145740 | tf_op jit(solution)/shard_map/dynamic_slice | solution.py:301
  13.9 0.0 collective-permute-start.3
  13.9 0.6 %collective-permute-start.2 = (bf16[256,1024]{1,0:T(8,128)(2,1)}, bf16[256,1024]{1,0:T(8,128)(2,1)S(1)}, u32[]{:S(2)}, u32[]{:S(2)}) collective-permute-start(bf16[256,1024]{1,0:T(8,128)(2,1)} %get-tuple-element.33), channel_id=1, source_target_pairs={{0,3},{1,2},{2,1},{3,0},{4,7},{5,6},{6,5},{7,4},{8,11},{9,10},{10,... | collective-permute-start | bytes 1572872 | tf_op jit(solution)/shard_map/ppermute | solution.py:297
  14.6 0.0 copy-done.1
  14.6 0.1 copy.7.bias_ref
  14.7 3.8 %all-to-all-done.x_ref = bf16[8,2,32,256]{3,2,1,0:T(8,128)(2,1)S(1)} async-done(((bf16[8,2,32,256]{3,2,1,0:T(8,128)(2,1)}), bf16[8,2,32,256]{3,2,1,0:T(8,128)(2,1)S(1)}, u32[]{:S(2)}, u32[]{:S(2)}) %all-to-all-start) | async-done | bytes 262176 | tf_op jit(solution)/shard_map/all_to_all | solution.py:306
  18.5 2.3 %toeplitz_conv.1 = bf16[8,2,32,256]{3,2,1,0:T(8,128)(2,1)} custom-call(bf16[8,2,32,256]{3,2,1,0:T(8,128)(2,1)S(1)} %all-to-all-done.x_ref, f32[256,1]{1,0:T(8,128)S(1)} %copy.7.bias_ref), custom_call_target="tpu_custom_call" | custom-call | flops 1 | bytes 1 | tf_op jit(solution)/shard_map/toeplitz_conv/pallas_call | solution.py:114
  20.8 0.0 collective-permute-done.refs_1_
  20.8 5.1 %all-to-all-start.1 = ((bf16[16,32,256]{2,1,0:T(8,128)(2,1)}), bf16[16,32,256]{2,1,0:T(8,128)(2,1)S(1)}, u32[]{:S(2)}, u32[]{:S(2)}) async-start(bf16[16,32,256]{2,1,0:T(8,128)(2,1)} %bitcast.1), calls=%async_computation.1 | async-start | bytes 524288 | tf_op jit(solution)/shard_map/all_to_all | solution.py:309
  26.0 0.0 copy-done
  26.0 0.6 %collective-permute-start.1 = (bf16[256,256]{1,0:T(8,128)(2,1)S(1)}, bf16[256,256]{1,0:T(8,128)(2,1)S(1)}, u32[]{:S(2)}, u32[]{:S(2)}) collective-permute-start(bf16[256,256]{1,0:T(8,128)(2,1)S(1)} %copy-done), channel_id=1, source_target_pairs={{0,2},{1,3},{2,0},{3,1},{4,6},{5,7},{6,4},{7,5},{8,10},{9,11},{10,... | collective-permute-start | bytes 393224 | tf_op jit(solution)/shard_map/ppermute | solution.py:297
  26.6 7.4 %collective-permute-done.1.refs_1_ = bf16[256,256]{1,0:T(8,128)(2,1)S(1)} collective-permute-done((bf16[256,256]{1,0:T(8,128)(2,1)S(1)}, bf16[256,256]{1,0:T(8,128)(2,1)S(1)}, u32[]{:S(2)}, u32[]{:S(2)}) %collective-permute-start.1) | collective-permute-done | bytes 131104 | tf_op jit(solution)/shard_map/ppermute | solution.py:297
  34.0 0.0 collective-permute-done.3.refs_2_
  34.0 0.0 collective-permute-done.2.refs_3_
  34.0 0.0 all-to-all-done.1
  34.0 0.1 gate.1.gated_ref
  34.1 0.1 collective-permute-start.4
  34.2 0.6 %project_own.1 = (f32[1024,256]{1,0:T(8,128)S(1)}, bf16[1024,512]{1,0:T(8,128)(2,1)S(1)}) custom-call(bf16[512,256]{1,0:T(8,128)(2,1)S(1)} %gate.1.gated_ref, bf16[256,1024]{1,0:T(8,128)(2,1)S(1)} %get-tuple-element.25.refs_0_, bf16[256,1024]{1,0:T(8,128)(2,1)S(1)} %collective-permute-done.refs_1_, bf16[256,1024]{1,0:T(8,128)(2,1)S(1)} %collective-permute-done.3.refs_2_, ...), custom_call_target="tpu_custom_call" | custom-call | flops 268435456 | bytes 1310720 | tf_op jit(solution)/shard_map/project_own/pallas_call | solution.py:264
  34.8 0.9 %collective-permute-done.4.gated_ref = bf16[512,256]{1,0:T(8,128)(2,1)S(1)} collective-permute-done((bf16[512,256]{1,0:T(8,128)(2,1)S(1)}, bf16[512,256]{1,0:T(8,128)(2,1)S(1)}, u32[]{:S(2)}, u32[]{:S(2)}) %collective-permute-start.4) | collective-permute-done | bytes 262176 | tf_op jit(solution)/shard_map/ppermute | solution.py:297
  35.7 1.2 %project_other.1 = bf16[1024,256]{1,0:T(8,128)(2,1)} custom-call(bf16[512,256]{1,0:T(8,128)(2,1)S(1)} %collective-permute-done.4.gated_ref, f32[1024,256]{1,0:T(8,128)S(1)} %get-tuple-element.29.sum_ref, bf16[1024,512]{1,0:T(8,128)(2,1)S(1)} %get-tuple-element.30.turned_ref), custom_call_target="tpu_custom_call" | custom-call | flops 268435456 | bytes 1310720 | tf_op jit(solution)/shard_map/project_other/pallas_call | solution.py:276
Async XLA Ops:
  2.0 12.6 %copy-start.1 = (f32[256]{0:T(256)S(1)}, f32[256]{0:T(256)}, u32[]{:S(2)}) copy-start(f32[256]{0:T(256)} %param.10) | copy-start | bytes 3076
  2.0 18.8 %collective-permute-start = (bf16[256,1024]{1,0:T(8,128)(2,1)S(1)}, bf16[256,1024]{1,0:T(8,128)(2,1)S(1)}, u32[]{:S(2)}, u32[]{:S(2)}) collective-permute-start(bf16[256,1024]{1,0:T(8,128)(2,1)S(1)} %get-tuple-element.19), channel_id=1, source_target_pairs={{0,2},{1,3},{2,0},{3,1},{4,6},{5,7},{6,4},{7,5},{8,10},{9,11},{10,... | collective-permute-start | bytes 1572872 | tf_op jit(solution)/shard_map/ppermute | solution.py:297
  5.0 13.5 %all-to-all-start = ((bf16[8,2,32,256]{3,2,1,0:T(8,128)(2,1)}), bf16[8,2,32,256]{3,2,1,0:T(8,128)(2,1)S(1)}, u32[]{:S(2)}, u32[]{:S(2)}) async-start(bf16[8,2,32,256]{3,2,1,0:T(8,128)(2,1)} %get-tuple-element.18), calls=%async_computation | async-start | bytes 524288 | tf_op jit(solution)/shard_map/all_to_all | solution.py:306
  11.4 14.5 %copy-start = (bf16[256,256]{1,0:T(8,128)(2,1)S(1)}, bf16[256,256]{1,0:T(8,128)(2,1)}, u32[]{:S(2)}) copy-start(bf16[256,256]{1,0:T(8,128)(2,1)} %refs_0_) | copy-start | bytes 393220
  13.9 20.1 %collective-permute-start.3 = (bf16[256,1024]{1,0:T(8,128)(2,1)}, bf16[256,1024]{1,0:T(8,128)(2,1)S(1)}, u32[]{:S(2)}, u32[]{:S(2)}) collective-permute-start(bf16[256,1024]{1,0:T(8,128)(2,1)} %get-tuple-element.31), channel_id=1, source_target_pairs={{0,1},{1,0},{2,3},{3,2},{4,5},{5,4},{6,7},{7,6},{8,9},{9,8},{10,11... | collective-permute-start | bytes 1572872 | tf_op jit(solution)/shard_map/ppermute | solution.py:297
  13.9 20.1 %collective-permute-start.2 = (bf16[256,1024]{1,0:T(8,128)(2,1)}, bf16[256,1024]{1,0:T(8,128)(2,1)S(1)}, u32[]{:S(2)}, u32[]{:S(2)}) collective-permute-start(bf16[256,1024]{1,0:T(8,128)(2,1)} %get-tuple-element.33), channel_id=1, source_target_pairs={{0,3},{1,2},{2,1},{3,0},{4,7},{5,6},{6,5},{7,4},{8,11},{9,10},{10,... | collective-permute-start | bytes 1572872 | tf_op jit(solution)/shard_map/ppermute | solution.py:297
  20.8 13.2 %all-to-all-start.1 = ((bf16[16,32,256]{2,1,0:T(8,128)(2,1)}), bf16[16,32,256]{2,1,0:T(8,128)(2,1)S(1)}, u32[]{:S(2)}, u32[]{:S(2)}) async-start(bf16[16,32,256]{2,1,0:T(8,128)(2,1)} %bitcast.1), calls=%async_computation.1 | async-start | bytes 524288 | tf_op jit(solution)/shard_map/all_to_all | solution.py:309
  26.0 8.0 %collective-permute-start.1 = (bf16[256,256]{1,0:T(8,128)(2,1)S(1)}, bf16[256,256]{1,0:T(8,128)(2,1)S(1)}, u32[]{:S(2)}, u32[]{:S(2)}) collective-permute-start(bf16[256,256]{1,0:T(8,128)(2,1)S(1)} %copy-done), channel_id=1, source_target_pairs={{0,2},{1,3},{2,0},{3,1},{4,6},{5,7},{6,4},{7,5},{8,10},{9,11},{10,... | collective-permute-start | bytes 393224 | tf_op jit(solution)/shard_map/ppermute | solution.py:297
  34.1 1.6 %collective-permute-start.4 = (bf16[512,256]{1,0:T(8,128)(2,1)S(1)}, bf16[512,256]{1,0:T(8,128)(2,1)S(1)}, u32[]{:S(2)}, u32[]{:S(2)}) collective-permute-start(bf16[512,256]{1,0:T(8,128)(2,1)S(1)} %gate.1.gated_ref), channel_id=1, source_target_pairs={{0,1},{1,0},{2,3},{3,2},{4,5},{5,4},{6,7},{7,6},{8,9},{9,8},{10,11... | collective-permute-start | bytes 786440 | tf_op jit(solution)/shard_map/ppermute | solution.py:297

commit v7 on v6

--- a/solution.py
+++ b/solution.py
@@ -302,6 +302,8 @@
     weights = [exchange(cut, step) for cut, step in zip(cuts, exchanges(tp))]
     gates = [gate_q] + [exchange(gate_q, (step, 0)) for step in range(1, chips)]
 
+    pieces, arrived = lax.optimization_barrier((pieces, gates[1:]))
+    gates = [gate_q, *arrived]
     order = ctx_order(shards)
     pieces = lax.all_to_all(pieces, "ctx", split_axis=0, concat_axis=0, tiled=True, axis_index_groups=[order])
     convolved = convolve(pieces, skip_bias.reshape(channels, 1), chips)
@@ -317,7 +319,7 @@
         ],
     )
     own = lax.dynamic_slice_in_dim(w_out, me * feats, feats, 1)
-    convolved, own, gates, weights = lax.optimization_barrier((convolved, own, gates, weights))
+    convolved, own, weights = lax.optimization_barrier((convolved, own, weights))
     gated_vals = gate(convolved.reshape(shards, chips, channels // shards, seq_dev), gates)
     others = exchange(gated_vals, (0, 1))
     blocks = dict(zip([(0, 0)] + exchanges(tp), [own, *weights]))

time: 37.2 us -> 36.9 us (level)
  waiting for transfers between devices: 12.2 us -> 10.3 us
  starting transfers between devices: 15.8 us -> 17.3 us
    all_to_all x1, waiting for transfers between devices: 3.85 us -> 1.52 us  [body(): lax.all_to_all(pieces, 'ctx', split_axis=0, concat_axis=0, tiled=True, ax...]
    ppermute x5, starting transfers between devices: 4.35 us -> 5.46 us  [exchange(): lax.ppermute(array, 'tp', [(i, partner(i, step, tp)) for i in range(tp)])]
    all_to_all x1, waiting for transfers between devices: 0.01 us -> 0.91 us  [body(): lax.all_to_all(convolved.reshape(shards * chips, channels // shards, seq_...]
    all_to_all x1, starting transfers between devices: 5.12 us -> 5.61 us  [body(): lax.all_to_all(convolved.reshape(shards * chips, channels // shards, seq_...]
    ppermute x5, waiting for transfers between devices: 8.31 us -> 7.9 us  [exchange(): lax.ppermute(array, 'tp', [(i, partner(i, step, tp)) for i in range(tp)])]
  transfers between devices with their start and end apart: 7 -> 7, of which waited for: 3 -> 5; matrix products, arithmetic and copies ran while one was open for 7% -> 7% of each run, Pallas kernels for 8% -> 13%
where the time goes in v7:
time: 36.9 us; the launch traced here: 36.5 us
  starting transfers between devices  17.3 us (47%)
  waiting for transfers between devices  10.3 us (28%)
  Pallas kernels  6.12 us (17%)
  local copies, waits for them, and re-layouts  2.66 us (7%)
    ppermute x5, waiting for transfers between devices, exchange(): lax.ppermute(array, 'tp', [(i, partner(i, step, tp)) for i in range(tp)])  7.9 us
    all_to_all x1, starting transfers between devices, body(): lax.all_to_all(pieces, 'ctx', split_axis=0, concat_axis=0, tiled=True, ax...  6.25 us
    all_to_all x1, starting transfers between devices, body(): lax.all_to_all(convolved.reshape(shards * chips, channels // shards, seq_...  5.61 us
    ppermute x5, starting transfers between devices, exchange(): lax.ppermute(array, 'tp', [(i, partner(i, step, tp)) for i in range(tp)])  5.46 us
    dynamic_slice x1, local copies, waits for them, and re-layouts, body(): lax.dynamic_slice_in_dim(w_out, partner(me, step, tp) * feats, feats, 1)  2.52 us
    pallas_call x1, Pallas kernels, convolve(): pl.pallas_call(conv_kernel, out_shape=jax.ShapeDtypeStruct((blocks, copie...  2.27 us
    pallas_call x1, Pallas kernels, prepare(): pl.pallas_call(prepare_kernel, out_shape=[pltpu.VMEM((shards, 2, channels...  1.99 us
    all_to_all x1, waiting for transfers between devices, body(): lax.all_to_all(pieces, 'ctx', split_axis=0, concat_axis=0, tiled=True, ax...  1.52 us
  transfers between devices with their start and end apart: 7, of which 5 were waited for; matrix products, arithmetic and copies ran while one was open for 7% of the time, Pallas kernels for 13%

profile of v7, /device:TPU:0, one launch (start us, length us, event | category | flops | bytes accessed | tf_op | source)
XLA Modules:
  0.0 36.5 jit_solution(13104598268626190070)
XLA Ops:
  0.0 3.0 %collective-permute-start = (bf16[256,256]{1,0:T(8,128)(2,1)}, bf16[256,256]{1,0:T(8,128)(2,1)S(1)}, u32[]{:S(2)}, u32[]{:S(2)}) collective-permute-start(bf16[256,256]{1,0:T(8,128)(2,1)} %refs_0_.1), channel_id=1, source_target_pairs={{0,2},{1,3},{2,0},{3,1},{4,6},{5,7},{6,4},{7,5},{8,10},{9,11},{10,... | collective-permute-start | bytes 393224 | tf_op jit(solution)/shard_map/ppermute | solution.py:297
  3.0 2.0 %prepare.1 = (bf16[8,2,32,256]{3,2,1,0:T(8,128)(2,1)}, bf16[256,1024]{1,0:T(8,128)(2,1)S(1)}) custom-call(bf16[256,256]{1,0:T(8,128)(2,1)} %key_ref.1, bf16[256,256]{1,0:T(8,128)(2,1)} %value_ref.1, f32[256,256]{1,0:T(8,128)} %taps_ref.1, bf16[256,4096]{1,0:T(8,128)(2,1)} %w_ref.1), custom_call_target="tpu_custom_call" | custom-call | flops 65536 | bytes 4194304 | tf_op jit(solution)/shard_map/prepare/pallas_call | solution.py:181
  5.0 0.0 copy-start.1
  5.0 0.1 collective-permute-start.1
  5.1 2.0 %collective-permute-done.refs_1_ = bf16[256,256]{1,0:T(8,128)(2,1)S(1)} collective-permute-done((bf16[256,256]{1,0:T(8,128)(2,1)}, bf16[256,256]{1,0:T(8,128)(2,1)S(1)}, u32[]{:S(2)}, u32[]{:S(2)}) %collective-permute-start) | collective-permute-done | bytes 131104 | tf_op jit(solution)/shard_map/ppermute | solution.py:297
  7.0 6.2 %all-to-all-start = ((bf16[8,2,32,256]{3,2,1,0:T(8,128)(2,1)}), bf16[8,2,32,256]{3,2,1,0:T(8,128)(2,1)S(1)}, u32[]{:S(2)}, u32[]{:S(2)}) async-start(bf16[8,2,32,256]{3,2,1,0:T(8,128)(2,1)} %get-tuple-element.19), calls=%async_computation | async-start | bytes 524288 | tf_op jit(solution)/shard_map/all_to_all | solution.py:308
  13.3 0.0 copy-start
  13.3 2.5 %constant_dynamic-slice_fusion = (bf16[256,1024]{1,0:T(8,128)(2,1)}, bf16[256,1024]{1,0:T(8,128)(2,1)S(1)}, bf16[256,1024]{1,0:T(8,128)(2,1)}) fusion(bf16[256,4096]{1,0:T(8,128)(2,1)} %w_ref.1, s32[]{:T(128)S(6)} %select_n.44, s32[]{:T(128)S(6)} %select_n.37, s32[]{:T(128)S(6)} %select_n.42), kind=kLoop, calls=%fused_computation | loop fusion | bytes 3145740 | tf_op jit(solution)/shard_map/dynamic_slice | solution.py:301
  15.8 0.0 collective-permute-start.3
  15.8 2.4 %collective-permute-start.2 = (bf16[256,1024]{1,0:T(8,128)(2,1)}, bf16[256,1024]{1,0:T(8,128)(2,1)S(1)}, u32[]{:S(2)}, u32[]{:S(2)}) collective-permute-start(bf16[256,1024]{1,0:T(8,128)(2,1)} %get-tuple-element.33), channel_id=1, source_target_pairs={{0,3},{1,2},{2,1},{3,0},{4,7},{5,6},{6,5},{7,4},{8,11},{9,10},{10,... | collective-permute-start | bytes 1572872 | tf_op jit(solution)/shard_map/ppermute | solution.py:297
  18.1 0.0 copy-done.1
  18.1 0.1 copy.7.bias_ref
  18.3 1.5 %all-to-all-done.x_ref = bf16[8,2,32,256]{3,2,1,0:T(8,128)(2,1)S(1)} async-done(((bf16[8,2,32,256]{3,2,1,0:T(8,128)(2,1)}), bf16[8,2,32,256]{3,2,1,0:T(8,128)(2,1)S(1)}, u32[]{:S(2)}, u32[]{:S(2)}) %all-to-all-start) | async-done | bytes 262176 | tf_op jit(solution)/shard_map/all_to_all | solution.py:308
  19.8 2.3 %toeplitz_conv.1 = bf16[8,2,32,256]{3,2,1,0:T(8,128)(2,1)} custom-call(bf16[8,2,32,256]{3,2,1,0:T(8,128)(2,1)S(1)} %all-to-all-done.x_ref, f32[256,1]{1,0:T(8,128)S(1)} %copy.7.bias_ref), custom_call_target="tpu_custom_call" | custom-call | flops 1 | bytes 1 | tf_op jit(solution)/shard_map/toeplitz_conv/pallas_call | solution.py:114
  22.1 0.0 collective-permute-done.1.refs_1_
  22.1 5.6 %all-to-all-start.1 = ((bf16[16,32,256]{2,1,0:T(8,128)(2,1)}), bf16[16,32,256]{2,1,0:T(8,128)(2,1)S(1)}, u32[]{:S(2)}, u32[]{:S(2)}) async-start(bf16[16,32,256]{2,1,0:T(8,128)(2,1)} %bitcast.1), calls=%async_computation.1 | async-start | bytes 524288 | tf_op jit(solution)/shard_map/all_to_all | solution.py:311
  27.7 0.0 collective-permute-done.3.refs_2_
  27.7 5.0 %collective-permute-done.2.refs_3_ = bf16[256,1024]{1,0:T(8,128)(2,1)S(1)} collective-permute-done((bf16[256,1024]{1,0:T(8,128)(2,1)}, bf16[256,1024]{1,0:T(8,128)(2,1)S(1)}, u32[]{:S(2)}, u32[]{:S(2)}) %collective-permute-start.2) | collective-permute-done | bytes 524320 | tf_op jit(solution)/shard_map/ppermute | solution.py:297
  32.7 0.9 %all-to-all-done.1 = bf16[16,32,256]{2,1,0:T(8,128)(2,1)S(1)} async-done(((bf16[16,32,256]{2,1,0:T(8,128)(2,1)}), bf16[16,32,256]{2,1,0:T(8,128)(2,1)S(1)}, u32[]{:S(2)}, u32[]{:S(2)}) %all-to-all-start.1) | async-done | bytes 262176 | tf_op jit(solution)/shard_map/all_to_all | solution.py:311
  33.7 0.0 copy-done
  33.7 0.1 gate.1.gated_ref
  33.7 0.1 collective-permute-start.4
  33.8 0.6 %project_own.1 = (f32[1024,256]{1,0:T(8,128)S(1)}, bf16[1024,512]{1,0:T(8,128)(2,1)S(1)}) custom-call(bf16[512,256]{1,0:T(8,128)(2,1)S(1)} %gate.1.gated_ref, bf16[256,1024]{1,0:T(8,128)(2,1)S(1)} %get-tuple-element.25.refs_0_, bf16[256,1024]{1,0:T(8,128)(2,1)S(1)} %collective-permute-done.1.refs_1_, bf16[256,1024]{1,0:T(8,128)(2,1)S(1)} %collective-permute-done.3.refs_2_, ...), custom_call_target="tpu_custom_call" | custom-call | flops 268435456 | bytes 1310720 | tf_op jit(solution)/shard_map/project_own/pallas_call | solution.py:264
  34.4 0.9 %collective-permute-done.4.gated_ref = bf16[512,256]{1,0:T(8,128)(2,1)S(1)} collective-permute-done((bf16[512,256]{1,0:T(8,128)(2,1)S(1)}, bf16[512,256]{1,0:T(8,128)(2,1)S(1)}, u32[]{:S(2)}, u32[]{:S(2)}) %collective-permute-start.4) | collective-permute-done | bytes 262176 | tf_op jit(solution)/shard_map/ppermute | solution.py:297
  35.3 1.2 %project_other.1 = bf16[1024,256]{1,0:T(8,128)(2,1)} custom-call(bf16[512,256]{1,0:T(8,128)(2,1)S(1)} %collective-permute-done.4.gated_ref, f32[1024,256]{1,0:T(8,128)S(1)} %get-tuple-element.29.sum_ref, bf16[1024,512]{1,0:T(8,128)(2,1)S(1)} %get-tuple-element.30.turned_ref), custom_call_target="tpu_custom_call" | custom-call | flops 268435456 | bytes 1310720 | tf_op jit(solution)/shard_map/project_other/pallas_call | solution.py:276
Async XLA Ops:
  0.0 7.0 %collective-permute-start = (bf16[256,256]{1,0:T(8,128)(2,1)}, bf16[256,256]{1,0:T(8,128)(2,1)S(1)}, u32[]{:S(2)}, u32[]{:S(2)}) collective-permute-start(bf16[256,256]{1,0:T(8,128)(2,1)} %refs_0_.1), channel_id=1, source_target_pairs={{0,2},{1,3},{2,0},{3,1},{4,6},{5,7},{6,4},{7,5},{8,10},{9,11},{10,... | collective-permute-start | bytes 393224 | tf_op jit(solution)/shard_map/ppermute | solution.py:297
  5.0 13.2 %copy-start.1 = (f32[256]{0:T(256)S(1)}, f32[256]{0:T(256)}, u32[]{:S(2)}) copy-start(f32[256]{0:T(256)} %param.10) | copy-start | bytes 3076
  5.0 17.1 %collective-permute-start.1 = (bf16[256,1024]{1,0:T(8,128)(2,1)S(1)}, bf16[256,1024]{1,0:T(8,128)(2,1)S(1)}, u32[]{:S(2)}, u32[]{:S(2)}) collective-permute-start(bf16[256,1024]{1,0:T(8,128)(2,1)S(1)} %get-tuple-element.20), channel_id=1, source_target_pairs={{0,2},{1,3},{2,0},{3,1},{4,6},{5,7},{6,4},{7,5},{8,10},{9,11},{10,... | collective-permute-start | bytes 1572872 | tf_op jit(solution)/shard_map/ppermute | solution.py:297
  7.0 12.8 %all-to-all-start = ((bf16[8,2,32,256]{3,2,1,0:T(8,128)(2,1)}), bf16[8,2,32,256]{3,2,1,0:T(8,128)(2,1)S(1)}, u32[]{:S(2)}, u32[]{:S(2)}) async-start(bf16[8,2,32,256]{3,2,1,0:T(8,128)(2,1)} %get-tuple-element.19), calls=%async_computation | async-start | bytes 524288 | tf_op jit(solution)/shard_map/all_to_all | solution.py:308
  13.3 20.4 %copy-start = (bf16[256,256]{1,0:T(8,128)(2,1)S(1)}, bf16[256,256]{1,0:T(8,128)(2,1)}, u32[]{:S(2)}) copy-start(bf16[256,256]{1,0:T(8,128)(2,1)} %refs_0_.1) | copy-start | bytes 393220
  15.8 11.9 %collective-permute-start.3 = (bf16[256,1024]{1,0:T(8,128)(2,1)}, bf16[256,1024]{1,0:T(8,128)(2,1)S(1)}, u32[]{:S(2)}, u32[]{:S(2)}) collective-permute-start(bf16[256,1024]{1,0:T(8,128)(2,1)} %get-tuple-element.31), channel_id=1, source_target_pairs={{0,1},{1,0},{2,3},{3,2},{4,5},{5,4},{6,7},{7,6},{8,9},{9,8},{10,11... | collective-permute-start | bytes 1572872 | tf_op jit(solution)/shard_map/ppermute | solution.py:297
  15.8 17.0 %collective-permute-start.2 = (bf16[256,1024]{1,0:T(8,128)(2,1)}, bf16[256,1024]{1,0:T(8,128)(2,1)S(1)}, u32[]{:S(2)}, u32[]{:S(2)}) collective-permute-start(bf16[256,1024]{1,0:T(8,128)(2,1)} %get-tuple-element.33), channel_id=1, source_target_pairs={{0,3},{1,2},{2,1},{3,0},{4,7},{5,6},{6,5},{7,4},{8,11},{9,10},{10,... | collective-permute-start | bytes 1572872 | tf_op jit(solution)/shard_map/ppermute | solution.py:297
  22.1 11.6 %all-to-all-start.1 = ((bf16[16,32,256]{2,1,0:T(8,128)(2,1)}), bf16[16,32,256]{2,1,0:T(8,128)(2,1)S(1)}, u32[]{:S(2)}, u32[]{:S(2)}) async-start(bf16[16,32,256]{2,1,0:T(8,128)(2,1)} %bitcast.1), calls=%async_computation.1 | async-start | bytes 524288 | tf_op jit(solution)/shard_map/all_to_all | solution.py:311
  33.7 1.6 %collective-permute-start.4 = (bf16[512,256]{1,0:T(8,128)(2,1)S(1)}, bf16[512,256]{1,0:T(8,128)(2,1)S(1)}, u32[]{:S(2)}, u32[]{:S(2)}) collective-permute-start(bf16[512,256]{1,0:T(8,128)(2,1)S(1)} %gate.1.gated_ref), channel_id=1, source_target_pairs={{0,1},{1,0},{2,3},{3,2},{4,5},{5,4},{6,7},{7,6},{8,9},{9,8},{10,11... | collective-permute-start | bytes 786440 | tf_op jit(solution)/shard_map/ppermute | solution.py:297

commit v8 on v7

--- a/solution.py
+++ b/solution.py
@@ -23,7 +23,7 @@
     return pad, (pad + lines) | 1, lines | 1
 
 
-def conv_kernel(x_ref, bias_ref, y_ref, taps, rows, sums, result, sems):
+def conv_kernel(x_ref, bias_ref, y_ref, taps, rows, sums):
     blocks, _, chans, seq_dev = x_ref.shape
     halves = seq_dev // LANES
     place = ctx_order(blocks).index
@@ -84,7 +84,6 @@
     first = pl.multiple_of(lax.axis_index("ctx") * chans, chans)
     size = PACK if chans % PACK == 0 else chans
     lane = lax.broadcasted_iota(jnp.int32, (size, LANES), 1)
-    copies = []
     for begin in range(0, chans, size):
         part = pl.ds(begin, size)
         bias = jnp.broadcast_to(bias_ref[pl.ds(first + begin, size), :], (size, LANES))
@@ -98,13 +97,8 @@
                 mixed = jnp.where(lane < LANES - SUB * phase, now[phase], older[phase])
                 value = value + pltpu.roll(mixed, SUB * phase, axis=1)
             older = now
-            result[place(block), part, cut] = value.astype(jnp.bfloat16)
-        for copy in range(y_ref.shape[1]):
-            sem = sems.at[begin // size, copy]
-            copies.append(pltpu.make_async_copy(result.at[:, part, :], y_ref.at[:, copy, part, :], sem))
-            copies[-1].start()
-    for copy in copies:
-        copy.wait()
+            for copy in range(y_ref.shape[1]):
+                y_ref[place(block), copy, part, cut] = value.astype(jnp.bfloat16)
 
 
 def convolve(pieces, bias, copies):
@@ -115,13 +109,11 @@
         conv_kernel,
         out_shape=jax.ShapeDtypeStruct((blocks, copies, chans, seq_dev), jnp.bfloat16),
         in_specs=[pl.BlockSpec(memory_space=pltpu.VMEM)] * 2,
-        out_specs=pl.BlockSpec(memory_space=pltpu.HBM),
+        out_specs=pl.BlockSpec(memory_space=pltpu.VMEM),
         scratch_shapes=[
             pltpu.VMEM((chans, LANES + lines * LANES), jnp.float32),
             pltpu.VMEM((PHASES, chans * row_pitch, LANES), jnp.float32),
             pltpu.VMEM((PHASES, chans * sum_pitch, LANES), jnp.float32),
-            pltpu.VMEM((blocks, chans, seq_dev), jnp.bfloat16),
-            pltpu.SemaphoreType.DMA((pl.cdiv(chans, PACK), copies)),
         ],
         compiler_params=pltpu.CompilerParams(vmem_limit_bytes=16 * 2**20),
         cost_estimate=pl.CostEstimate(flops=1, bytes_accessed=1, transcendentals=0),
@@ -307,7 +299,8 @@
     order = ctx_order(shards)
     pieces = lax.all_to_all(pieces, "ctx", split_axis=0, concat_axis=0, tiled=True, axis_index_groups=[order])
     convolved = convolve(pieces, skip_bias.reshape(channels, 1), chips)
-    convolved, weights[0] = lax.optimization_barrier((convolved, weights[0]))
+    own = lax.dynamic_slice_in_dim(w_out, me * feats, feats, 1)
+    convolved, own, weights[0] = lax.optimization_barrier((convolved, own, weights[0]))
     convolved = lax.all_to_all(
         convolved.reshape(shards * chips, channels // shards, seq_dev),
         ("ctx", "tp"),
@@ -318,9 +311,8 @@
             [shard * tp + chip * CORES + core for shard in order for chip in reversed(range(chips))] for core in range(CORES)
         ],
     )
-    own = lax.dynamic_slice_in_dim(w_out, me * feats, feats, 1)
-    convolved, own, weights = lax.optimization_barrier((convolved, own, weights))
     gated_vals = gate(convolved.reshape(shards, chips, channels // shards, seq_dev), gates)
+    gated_vals, weights = lax.optimization_barrier((gated_vals, weights))
     others = exchange(gated_vals, (0, 1))
     blocks = dict(zip([(0, 0)] + exchanges(tp), [own, *weights]))
     ordered = [blocks[chip, core] for core in range(CORES) for chip in range(chips)]

time: 36.9 us -> 36.8 us (level)
  blocking collectives: 0 us -> 12.3 us
  waiting for transfers between devices: 10.3 us -> 4.39 us
  starting transfers between devices: 17.3 us -> 11.7 us
  Pallas kernels: 6.12 us -> 5.4 us
    all_to_all x0 -> x1, blocking collectives: none -> 12.3 us  [body(): lax.all_to_all(convolved.reshape(shards * chips, channels // shards, seq_...]
    all_to_all x1 -> x0, starting transfers between devices: 5.61 us -> none  [body(): lax.all_to_all(convolved.reshape(shards * chips, channels // shards, seq_...]
    ppermute x5, waiting for transfers between devices: 7.9 us -> 2.87 us  [exchange(): lax.ppermute(array, 'tp', [(i, partner(i, step, tp)) for i in range(tp)])]
    all_to_all x1 -> x0, waiting for transfers between devices: 0.91 us -> none  [body(): lax.all_to_all(convolved.reshape(shards * chips, channels // shards, seq_...]
    pallas_call x1, Pallas kernels: 2.27 us -> 1.56 us  [convolve(): pl.pallas_call(conv_kernel, out_shape=jax.ShapeDtypeStruct((blocks, copie...]
  transfers between devices with their start and end apart: 7 -> 6, of which waited for: 5 -> 3; matrix products, arithmetic and copies ran while one was open for 7% -> 7% of each run, Pallas kernels for 13% -> 12%
where the time goes in v8:
time: 36.8 us; the launch traced here: 36.5 us
  blocking collectives  12.3 us (33%)
  starting transfers between devices  11.7 us (32%)
  Pallas kernels  5.4 us (15%)
  waiting for transfers between devices  4.39 us (12%)
  local copies, waits for them, and re-layouts  2.65 us (7%)
    all_to_all x1, blocking collectives, body(): lax.all_to_all(convolved.reshape(shards * chips, channels // shards, seq_...  12.3 us
    all_to_all x1, starting transfers between devices, body(): lax.all_to_all(pieces, 'ctx', split_axis=0, concat_axis=0, tiled=True, ax...  6.25 us
    ppermute x5, starting transfers between devices, exchange(): lax.ppermute(array, 'tp', [(i, partner(i, step, tp)) for i in range(tp)])  5.47 us
    ppermute x5, waiting for transfers between devices, exchange(): lax.ppermute(array, 'tp', [(i, partner(i, step, tp)) for i in range(tp)])  2.87 us
    dynamic_slice x1, local copies, waits for them, and re-layouts, body(): lax.dynamic_slice_in_dim(w_out, partner(me, step, tp) * feats, feats, 1)  2.51 us
    pallas_call x1, Pallas kernels, prepare(): pl.pallas_call(prepare_kernel, out_shape=[pltpu.VMEM((shards, 2, channels...  1.99 us
    pallas_call x1, Pallas kernels, convolve(): pl.pallas_call(conv_kernel, out_shape=jax.ShapeDtypeStruct((blocks, copie...  1.56 us
    all_to_all x1, waiting for transfers between devices, body(): lax.all_to_all(pieces, 'ctx', split_axis=0, concat_axis=0, tiled=True, ax...  1.53 us
  transfers between devices with their start and end apart: 6, of which 3 were waited for; matrix products, arithmetic and copies ran while one was open for 7% of the time, Pallas kernels for 12%

profile of v8, /device:TPU:0, one launch (start us, length us, event | category | flops | bytes accessed | tf_op | source)
XLA Modules:
  0.0 36.5 jit_solution(17865253058776687131)
XLA Ops:
  0.0 3.0 %collective-permute-start = (bf16[256,256]{1,0:T(8,128)(2,1)}, bf16[256,256]{1,0:T(8,128)(2,1)S(1)}, u32[]{:S(2)}, u32[]{:S(2)}) collective-permute-start(bf16[256,256]{1,0:T(8,128)(2,1)} %refs_0_.1), channel_id=1, source_target_pairs={{0,2},{1,3},{2,0},{3,1},{4,6},{5,7},{6,4},{7,5},{8,10},{9,11},{10,... | collective-permute-start | bytes 393224 | tf_op jit(solution)/shard_map/ppermute | solution.py:289
  3.0 2.0 %prepare.1 = (bf16[8,2,32,256]{3,2,1,0:T(8,128)(2,1)}, bf16[256,1024]{1,0:T(8,128)(2,1)S(1)}) custom-call(bf16[256,256]{1,0:T(8,128)(2,1)} %key_ref.1, bf16[256,256]{1,0:T(8,128)(2,1)} %value_ref.1, f32[256,256]{1,0:T(8,128)} %taps_ref.1, bf16[256,4096]{1,0:T(8,128)(2,1)} %w_ref.1), custom_call_target="tpu_custom_call" | custom-call | flops 65536 | bytes 4194304 | tf_op jit(solution)/shard_map/prepare/pallas_call | solution.py:173
  5.0 0.0 copy-start.1
  5.0 0.1 collective-permute-start.1
  5.1 2.0 %collective-permute-done.refs_1_ = bf16[256,256]{1,0:T(8,128)(2,1)S(1)} collective-permute-done((bf16[256,256]{1,0:T(8,128)(2,1)}, bf16[256,256]{1,0:T(8,128)(2,1)S(1)}, u32[]{:S(2)}, u32[]{:S(2)}) %collective-permute-start) | collective-permute-done | bytes 131104 | tf_op jit(solution)/shard_map/ppermute | solution.py:289
  7.0 6.2 %all-to-all-start = ((bf16[8,2,32,256]{3,2,1,0:T(8,128)(2,1)}), bf16[8,2,32,256]{3,2,1,0:T(8,128)(2,1)S(1)}, u32[]{:S(2)}, u32[]{:S(2)}) async-start(bf16[8,2,32,256]{3,2,1,0:T(8,128)(2,1)} %get-tuple-element.19), calls=%async_computation | async-start | bytes 524288 | tf_op jit(solution)/shard_map/all_to_all | solution.py:300
  13.3 0.0 copy-start
  13.3 2.5 %constant_dynamic-slice_fusion = (bf16[256,1024]{1,0:T(8,128)(2,1)}, bf16[256,1024]{1,0:T(8,128)(2,1)S(1)}, bf16[256,1024]{1,0:T(8,128)(2,1)}) fusion(bf16[256,4096]{1,0:T(8,128)(2,1)} %w_ref.1, s32[]{:T(128)S(6)} %select_n.44, s32[]{:T(128)S(6)} %select_n.37, s32[]{:T(128)S(6)} %select_n.42), kind=kLoop, calls=%fused_computation | loop fusion | bytes 3145740 | tf_op jit(solution)/shard_map/dynamic_slice | solution.py:293
  15.8 0.0 collective-permute-start.3
  15.8 2.4 %collective-permute-start.2 = (bf16[256,1024]{1,0:T(8,128)(2,1)}, bf16[256,1024]{1,0:T(8,128)(2,1)S(1)}, u32[]{:S(2)}, u32[]{:S(2)}) collective-permute-start(bf16[256,1024]{1,0:T(8,128)(2,1)} %get-tuple-element.33), channel_id=1, source_target_pairs={{0,3},{1,2},{2,1},{3,0},{4,7},{5,6},{6,5},{7,4},{8,11},{9,10},{10,... | collective-permute-start | bytes 1572872 | tf_op jit(solution)/shard_map/ppermute | solution.py:289
  18.1 0.0 copy-done.1
  18.1 0.1 copy.7.bias_ref
  18.3 1.5 %all-to-all-done.x_ref = bf16[8,2,32,256]{3,2,1,0:T(8,128)(2,1)S(1)} async-done(((bf16[8,2,32,256]{3,2,1,0:T(8,128)(2,1)}), bf16[8,2,32,256]{3,2,1,0:T(8,128)(2,1)S(1)}, u32[]{:S(2)}, u32[]{:S(2)}) %all-to-all-start) | async-done | bytes 262176 | tf_op jit(solution)/shard_map/all_to_all | solution.py:300
  19.8 1.6 %toeplitz_conv.1 = bf16[8,2,32,256]{3,2,1,0:T(8,128)(2,1)S(1)} custom-call(bf16[8,2,32,256]{3,2,1,0:T(8,128)(2,1)S(1)} %all-to-all-done.x_ref, f32[256,1]{1,0:T(8,128)S(1)} %copy.7.bias_ref), custom_call_target="tpu_custom_call" | custom-call | flops 1 | bytes 1 | tf_op jit(solution)/shard_map/toeplitz_conv/pallas_call | solution.py:108
  21.4 0.0 collective-permute-done.1.refs_1_
  21.4 12.3 %all_to_all.10 = bf16[16,32,256]{2,1,0:T(8,128)(2,1)S(1)} all-to-all(bf16[16,32,256]{2,1,0:T(8,128)(2,1)S(1)} %bitcast.4), channel_id=1, replica_groups={{18,16,2,0,6,4,10,8,14,12,22,20,26,24,30,28},{19,17,3,1,7,5,11,9,15,13,..., dimensions={0} | all-to-all | bytes 524288 | tf_op jit(solution)/shard_map/all_to_all | solution.py:304
  33.6 0.0 copy-done
  33.6 0.1 gate.1.gated_ref
  33.7 0.0 collective-permute-done.3.refs_2_
  33.7 0.0 collective-permute-done.2.refs_3_
  33.7 0.1 collective-permute-start.4
  33.8 0.6 %project_own.1 = (f32[1024,256]{1,0:T(8,128)S(1)}, bf16[1024,512]{1,0:T(8,128)(2,1)S(1)}) custom-call(bf16[512,256]{1,0:T(8,128)(2,1)S(1)} %gate.1.gated_ref, bf16[256,1024]{1,0:T(8,128)(2,1)S(1)} %get-tuple-element.25.refs_0_, bf16[256,1024]{1,0:T(8,128)(2,1)S(1)} %collective-permute-done.1.refs_1_, bf16[256,1024]{1,0:T(8,128)(2,1)S(1)} %collective-permute-done.3.refs_2_, ...), custom_call_target="tpu_custom_call" | custom-call | flops 268435456 | bytes 1310720 | tf_op jit(solution)/shard_map/project_own/pallas_call | solution.py:256
  34.4 0.9 %collective-permute-done.4.gated_ref = bf16[512,256]{1,0:T(8,128)(2,1)S(1)} collective-permute-done((bf16[512,256]{1,0:T(8,128)(2,1)S(1)}, bf16[512,256]{1,0:T(8,128)(2,1)S(1)}, u32[]{:S(2)}, u32[]{:S(2)}) %collective-permute-start.4) | collective-permute-done | bytes 262176 | tf_op jit(solution)/shard_map/ppermute | solution.py:289
  35.3 1.2 %project_other.1 = bf16[1024,256]{1,0:T(8,128)(2,1)} custom-call(bf16[512,256]{1,0:T(8,128)(2,1)S(1)} %collective-permute-done.4.gated_ref, f32[1024,256]{1,0:T(8,128)S(1)} %get-tuple-element.29.sum_ref, bf16[1024,512]{1,0:T(8,128)(2,1)S(1)} %get-tuple-element.30.turned_ref), custom_call_target="tpu_custom_call" | custom-call | flops 268435456 | bytes 1310720 | tf_op jit(solution)/shard_map/project_other/pallas_call | solution.py:268
Async XLA Ops:
  0.0 7.0 %collective-permute-start = (bf16[256,256]{1,0:T(8,128)(2,1)}, bf16[256,256]{1,0:T(8,128)(2,1)S(1)}, u32[]{:S(2)}, u32[]{:S(2)}) collective-permute-start(bf16[256,256]{1,0:T(8,128)(2,1)} %refs_0_.1), channel_id=1, source_target_pairs={{0,2},{1,3},{2,0},{3,1},{4,6},{5,7},{6,4},{7,5},{8,10},{9,11},{10,... | collective-permute-start | bytes 393224 | tf_op jit(solution)/shard_map/ppermute | solution.py:289
  5.0 13.2 %copy-start.1 = (f32[256]{0:T(256)S(1)}, f32[256]{0:T(256)}, u32[]{:S(2)}) copy-start(f32[256]{0:T(256)} %param.10) | copy-start | bytes 3076
  5.0 16.4 %collective-permute-start.1 = (bf16[256,1024]{1,0:T(8,128)(2,1)S(1)}, bf16[256,1024]{1,0:T(8,128)(2,1)S(1)}, u32[]{:S(2)}, u32[]{:S(2)}) collective-permute-start(bf16[256,1024]{1,0:T(8,128)(2,1)S(1)} %get-tuple-element.20), channel_id=1, source_target_pairs={{0,2},{1,3},{2,0},{3,1},{4,6},{5,7},{6,4},{7,5},{8,10},{9,11},{10,... | collective-permute-start | bytes 1572872 | tf_op jit(solution)/shard_map/ppermute | solution.py:289
  7.0 12.8 %all-to-all-start = ((bf16[8,2,32,256]{3,2,1,0:T(8,128)(2,1)}), bf16[8,2,32,256]{3,2,1,0:T(8,128)(2,1)S(1)}, u32[]{:S(2)}, u32[]{:S(2)}) async-start(bf16[8,2,32,256]{3,2,1,0:T(8,128)(2,1)} %get-tuple-element.19), calls=%async_computation | async-start | bytes 524288 | tf_op jit(solution)/shard_map/all_to_all | solution.py:300
  13.3 20.4 %copy-start = (bf16[256,256]{1,0:T(8,128)(2,1)S(1)}, bf16[256,256]{1,0:T(8,128)(2,1)}, u32[]{:S(2)}) copy-start(bf16[256,256]{1,0:T(8,128)(2,1)} %refs_0_.1) | copy-start | bytes 393220
  15.8 17.9 %collective-permute-start.3 = (bf16[256,1024]{1,0:T(8,128)(2,1)}, bf16[256,1024]{1,0:T(8,128)(2,1)S(1)}, u32[]{:S(2)}, u32[]{:S(2)}) collective-permute-start(bf16[256,1024]{1,0:T(8,128)(2,1)} %get-tuple-element.31), channel_id=1, source_target_pairs={{0,1},{1,0},{2,3},{3,2},{4,5},{5,4},{6,7},{7,6},{8,9},{9,8},{10,11... | collective-permute-start | bytes 1572872 | tf_op jit(solution)/shard_map/ppermute | solution.py:289
  15.8 18.0 %collective-permute-start.2 = (bf16[256,1024]{1,0:T(8,128)(2,1)}, bf16[256,1024]{1,0:T(8,128)(2,1)S(1)}, u32[]{:S(2)}, u32[]{:S(2)}) collective-permute-start(bf16[256,1024]{1,0:T(8,128)(2,1)} %get-tuple-element.33), channel_id=1, source_target_pairs={{0,3},{1,2},{2,1},{3,0},{4,7},{5,6},{6,5},{7,4},{8,11},{9,10},{10,... | collective-permute-start | bytes 1572872 | tf_op jit(solution)/shard_map/ppermute | solution.py:289
  33.7 1.6 %collective-permute-start.4 = (bf16[512,256]{1,0:T(8,128)(2,1)S(1)}, bf16[512,256]{1,0:T(8,128)(2,1)S(1)}, u32[]{:S(2)}, u32[]{:S(2)}) collective-permute-start(bf16[512,256]{1,0:T(8,128)(2,1)S(1)} %gate.1.gated_ref), channel_id=1, source_target_pairs={{0,1},{1,0},{2,3},{3,2},{4,5},{5,4},{6,7},{7,6},{8,9},{9,8},{10,11... | collective-permute-start | bytes 786440 | tf_op jit(solution)/shard_map/ppermute | solution.py:289

commit v9 on v8

--- a/solution.py
+++ b/solution.py
@@ -134,7 +134,7 @@
 def exchanges(tp):
     steps = [(chips, other) for chips in range(tp // CORES) for other in range(CORES)][1:]
     early = (tp // CORES // 2, 0)
-    return [early] + [step for step in reversed(steps) if step != early]
+    return [early] + [step for step in steps if step != early]
 
 
 def prepare_kernel(key_ref, value_ref, taps_ref, w_ref, pieces_ref, *refs):

time: 36.8 us -> 36.2 us (0.984)
  blocking collectives: 12.3 us -> 11.6 us
    all_to_all x1, blocking collectives: 12.3 us -> 11.6 us  [body(): lax.all_to_all(convolved.reshape(shards * chips, channels // shards, seq_...]
where the time goes in v9:
time: 36.2 us; the launch traced here: 35.9 us
  starting transfers between devices  11.7 us (32%)
  blocking collectives  11.6 us (32%)
  Pallas kernels  5.4 us (15%)
  waiting for transfers between devices  4.39 us (12%)
  local copies, waits for them, and re-layouts  2.65 us (7%)
    all_to_all x1, blocking collectives, body(): lax.all_to_all(convolved.reshape(shards * chips, channels // shards, seq_...  11.6 us
    all_to_all x1, starting transfers between devices, body(): lax.all_to_all(pieces, 'ctx', split_axis=0, concat_axis=0, tiled=True, ax...  6.25 us
    ppermute x5, starting transfers between devices, exchange(): lax.ppermute(array, 'tp', [(i, partner(i, step, tp)) for i in range(tp)])  5.47 us
    ppermute x5, waiting for transfers between devices, exchange(): lax.ppermute(array, 'tp', [(i, partner(i, step, tp)) for i in range(tp)])  2.87 us
    dynamic_slice x1, local copies, waits for them, and re-layouts, body(): lax.dynamic_slice_in_dim(w_out, partner(me, step, tp) * feats, feats, 1)  2.51 us
    pallas_call x1, Pallas kernels, prepare(): pl.pallas_call(prepare_kernel, out_shape=[pltpu.VMEM((shards, 2, channels...  1.99 us
    pallas_call x1, Pallas kernels, convolve(): pl.pallas_call(conv_kernel, out_shape=jax.ShapeDtypeStruct((blocks, copie...  1.56 us
    all_to_all x1, waiting for transfers between devices, body(): lax.all_to_all(pieces, 'ctx', split_axis=0, concat_axis=0, tiled=True, ax...  1.53 us
  transfers between devices with their start and end apart: 6, of which 3 were waited for; matrix products, arithmetic and copies ran while one was open for 7% of the time, Pallas kernels for 12%

profile of v9, /device:TPU:0, one launch (start us, length us, event | category | flops | bytes accessed | tf_op | source)
XLA Modules:
  0.0 35.9 jit_solution(18057947920510993790)
XLA Ops:
  0.0 3.0 %collective-permute-start = (bf16[256,256]{1,0:T(8,128)(2,1)}, bf16[256,256]{1,0:T(8,128)(2,1)S(1)}, u32[]{:S(2)}, u32[]{:S(2)}) collective-permute-start(bf16[256,256]{1,0:T(8,128)(2,1)} %refs_0_.1), channel_id=1, source_target_pairs={{0,2},{1,3},{2,0},{3,1},{4,6},{5,7},{6,4},{7,5},{8,10},{9,11},{10,... | collective-permute-start | bytes 393224 | tf_op jit(solution)/shard_map/ppermute | solution.py:289
  3.0 2.0 %prepare.1 = (bf16[8,2,32,256]{3,2,1,0:T(8,128)(2,1)}, bf16[256,1024]{1,0:T(8,128)(2,1)S(1)}) custom-call(bf16[256,256]{1,0:T(8,128)(2,1)} %key_ref.1, bf16[256,256]{1,0:T(8,128)(2,1)} %value_ref.1, f32[256,256]{1,0:T(8,128)} %taps_ref.1, bf16[256,4096]{1,0:T(8,128)(2,1)} %w_ref.1), custom_call_target="tpu_custom_call" | custom-call | flops 65536 | bytes 4194304 | tf_op jit(solution)/shard_map/prepare/pallas_call | solution.py:173
  5.0 0.0 copy-start.1
  5.0 0.1 collective-permute-start.1
  5.1 2.0 %collective-permute-done.refs_1_ = bf16[256,256]{1,0:T(8,128)(2,1)S(1)} collective-permute-done((bf16[256,256]{1,0:T(8,128)(2,1)}, bf16[256,256]{1,0:T(8,128)(2,1)S(1)}, u32[]{:S(2)}, u32[]{:S(2)}) %collective-permute-start) | collective-permute-done | bytes 131104 | tf_op jit(solution)/shard_map/ppermute | solution.py:289
  7.0 6.2 %all-to-all-start = ((bf16[8,2,32,256]{3,2,1,0:T(8,128)(2,1)}), bf16[8,2,32,256]{3,2,1,0:T(8,128)(2,1)S(1)}, u32[]{:S(2)}, u32[]{:S(2)}) async-start(bf16[8,2,32,256]{3,2,1,0:T(8,128)(2,1)} %get-tuple-element.19), calls=%async_computation | async-start | bytes 524288 | tf_op jit(solution)/shard_map/all_to_all | solution.py:300
  13.3 0.0 copy-start
  13.3 2.5 %constant_dynamic-slice_fusion = (bf16[256,1024]{1,0:T(8,128)(2,1)}, bf16[256,1024]{1,0:T(8,128)(2,1)S(1)}, bf16[256,1024]{1,0:T(8,128)(2,1)}) fusion(bf16[256,4096]{1,0:T(8,128)(2,1)} %w_ref.1, s32[]{:T(128)S(6)} %select_n.44, s32[]{:T(128)S(6)} %select_n.37, s32[]{:T(128)S(6)} %select_n.42), kind=kLoop, calls=%fused_computation | loop fusion | bytes 3145740 | tf_op jit(solution)/shard_map/dynamic_slice | solution.py:293
  15.8 0.0 collective-permute-start.3
  15.8 2.4 %collective-permute-start.2 = (bf16[256,1024]{1,0:T(8,128)(2,1)}, bf16[256,1024]{1,0:T(8,128)(2,1)S(1)}, u32[]{:S(2)}, u32[]{:S(2)}) collective-permute-start(bf16[256,1024]{1,0:T(8,128)(2,1)} %get-tuple-element.33), channel_id=1, source_target_pairs={{0,1},{1,0},{2,3},{3,2},{4,5},{5,4},{6,7},{7,6},{8,9},{9,8},{10,11... | collective-permute-start | bytes 1572872 | tf_op jit(solution)/shard_map/ppermute | solution.py:289
  18.1 0.0 copy-done.1
  18.1 0.1 copy.7.bias_ref
  18.3 1.5 %all-to-all-done.x_ref = bf16[8,2,32,256]{3,2,1,0:T(8,128)(2,1)S(1)} async-done(((bf16[8,2,32,256]{3,2,1,0:T(8,128)(2,1)}), bf16[8,2,32,256]{3,2,1,0:T(8,128)(2,1)S(1)}, u32[]{:S(2)}, u32[]{:S(2)}) %all-to-all-start) | async-done | bytes 262176 | tf_op jit(solution)/shard_map/all_to_all | solution.py:300
  19.8 1.6 %toeplitz_conv.1 = bf16[8,2,32,256]{3,2,1,0:T(8,128)(2,1)S(1)} custom-call(bf16[8,2,32,256]{3,2,1,0:T(8,128)(2,1)S(1)} %all-to-all-done.x_ref, f32[256,1]{1,0:T(8,128)S(1)} %copy.7.bias_ref), custom_call_target="tpu_custom_call" | custom-call | flops 1 | bytes 1 | tf_op jit(solution)/shard_map/toeplitz_conv/pallas_call | solution.py:108
  21.4 0.0 collective-permute-done.1.refs_1_
  21.4 11.6 %all_to_all.10 = bf16[16,32,256]{2,1,0:T(8,128)(2,1)S(1)} all-to-all(bf16[16,32,256]{2,1,0:T(8,128)(2,1)S(1)} %bitcast.4), channel_id=1, replica_groups={{18,16,2,0,6,4,10,8,14,12,22,20,26,24,30,28},{19,17,3,1,7,5,11,9,15,13,..., dimensions={0} | all-to-all | bytes 524288 | tf_op jit(solution)/shard_map/all_to_all | solution.py:304
  33.0 0.0 copy-done
  33.0 0.1 gate.1.gated_ref
  33.1 0.0 collective-permute-done.3.refs_3_
  33.1 0.0 collective-permute-done.2.refs_2_
  33.1 0.1 collective-permute-start.4
  33.2 0.6 %project_own.1 = (f32[1024,256]{1,0:T(8,128)S(1)}, bf16[1024,512]{1,0:T(8,128)(2,1)S(1)}) custom-call(bf16[512,256]{1,0:T(8,128)(2,1)S(1)} %gate.1.gated_ref, bf16[256,1024]{1,0:T(8,128)(2,1)S(1)} %get-tuple-element.25.refs_0_, bf16[256,1024]{1,0:T(8,128)(2,1)S(1)} %collective-permute-done.1.refs_1_, bf16[256,1024]{1,0:T(8,128)(2,1)S(1)} %collective-permute-done.2.refs_2_, ...), custom_call_target="tpu_custom_call" | custom-call | flops 268435456 | bytes 1310720 | tf_op jit(solution)/shard_map/project_own/pallas_call | solution.py:256
  33.8 0.9 %collective-permute-done.4.gated_ref = bf16[512,256]{1,0:T(8,128)(2,1)S(1)} collective-permute-done((bf16[512,256]{1,0:T(8,128)(2,1)S(1)}, bf16[512,256]{1,0:T(8,128)(2,1)S(1)}, u32[]{:S(2)}, u32[]{:S(2)}) %collective-permute-start.4) | collective-permute-done | bytes 262176 | tf_op jit(solution)/shard_map/ppermute | solution.py:289
  34.7 1.2 %project_other.1 = bf16[1024,256]{1,0:T(8,128)(2,1)} custom-call(bf16[512,256]{1,0:T(8,128)(2,1)S(1)} %collective-permute-done.4.gated_ref, f32[1024,256]{1,0:T(8,128)S(1)} %get-tuple-element.29.sum_ref, bf16[1024,512]{1,0:T(8,128)(2,1)S(1)} %get-tuple-element.30.turned_ref), custom_call_target="tpu_custom_call" | custom-call | flops 268435456 | bytes 1310720 | tf_op jit(solution)/shard_map/project_other/pallas_call | solution.py:268
Async XLA Ops:
  0.0 7.0 %collective-permute-start = (bf16[256,256]{1,0:T(8,128)(2,1)}, bf16[256,256]{1,0:T(8,128)(2,1)S(1)}, u32[]{:S(2)}, u32[]{:S(2)}) collective-permute-start(bf16[256,256]{1,0:T(8,128)(2,1)} %refs_0_.1), channel_id=1, source_target_pairs={{0,2},{1,3},{2,0},{3,1},{4,6},{5,7},{6,4},{7,5},{8,10},{9,11},{10,... | collective-permute-start | bytes 393224 | tf_op jit(solution)/shard_map/ppermute | solution.py:289
  5.0 13.2 %copy-start.1 = (f32[256]{0:T(256)S(1)}, f32[256]{0:T(256)}, u32[]{:S(2)}) copy-start(f32[256]{0:T(256)} %param.10) | copy-start | bytes 3076
  5.0 16.4 %collective-permute-start.1 = (bf16[256,1024]{1,0:T(8,128)(2,1)S(1)}, bf16[256,1024]{1,0:T(8,128)(2,1)S(1)}, u32[]{:S(2)}, u32[]{:S(2)}) collective-permute-start(bf16[256,1024]{1,0:T(8,128)(2,1)S(1)} %get-tuple-element.20), channel_id=1, source_target_pairs={{0,2},{1,3},{2,0},{3,1},{4,6},{5,7},{6,4},{7,5},{8,10},{9,11},{10,... | collective-permute-start | bytes 1572872 | tf_op jit(solution)/shard_map/ppermute | solution.py:289
  7.0 12.8 %all-to-all-start = ((bf16[8,2,32,256]{3,2,1,0:T(8,128)(2,1)}), bf16[8,2,32,256]{3,2,1,0:T(8,128)(2,1)S(1)}, u32[]{:S(2)}, u32[]{:S(2)}) async-start(bf16[8,2,32,256]{3,2,1,0:T(8,128)(2,1)} %get-tuple-element.19), calls=%async_computation | async-start | bytes 524288 | tf_op jit(solution)/shard_map/all_to_all | solution.py:300
  13.3 19.8 %copy-start = (bf16[256,256]{1,0:T(8,128)(2,1)S(1)}, bf16[256,256]{1,0:T(8,128)(2,1)}, u32[]{:S(2)}) copy-start(bf16[256,256]{1,0:T(8,128)(2,1)} %refs_0_.1) | copy-start | bytes 393220
  15.8 17.3 %collective-permute-start.3 = (bf16[256,1024]{1,0:T(8,128)(2,1)}, bf16[256,1024]{1,0:T(8,128)(2,1)S(1)}, u32[]{:S(2)}, u32[]{:S(2)}) collective-permute-start(bf16[256,1024]{1,0:T(8,128)(2,1)} %get-tuple-element.31), channel_id=1, source_target_pairs={{0,3},{1,2},{2,1},{3,0},{4,7},{5,6},{6,5},{7,4},{8,11},{9,10},{10,... | collective-permute-start | bytes 1572872 | tf_op jit(solution)/shard_map/ppermute | solution.py:289
  15.8 17.3 %collective-permute-start.2 = (bf16[256,1024]{1,0:T(8,128)(2,1)}, bf16[256,1024]{1,0:T(8,128)(2,1)S(1)}, u32[]{:S(2)}, u32[]{:S(2)}) collective-permute-start(bf16[256,1024]{1,0:T(8,128)(2,1)} %get-tuple-element.33), channel_id=1, source_target_pairs={{0,1},{1,0},{2,3},{3,2},{4,5},{5,4},{6,7},{7,6},{8,9},{9,8},{10,11... | collective-permute-start | bytes 1572872 | tf_op jit(solution)/shard_map/ppermute | solution.py:289
  33.1 1.6 %collective-permute-start.4 = (bf16[512,256]{1,0:T(8,128)(2,1)S(1)}, bf16[512,256]{1,0:T(8,128)(2,1)S(1)}, u32[]{:S(2)}, u32[]{:S(2)}) collective-permute-start(bf16[512,256]{1,0:T(8,128)(2,1)S(1)} %gate.1.gated_ref), channel_id=1, source_target_pairs={{0,1},{1,0},{2,3},{3,2},{4,5},{5,4},{6,7},{7,6},{8,9},{9,8},{10,11... | collective-permute-start | bytes 786440 | tf_op jit(solution)/shard_map/ppermute | solution.py:289

commit v10 on v9

--- a/solution.py
+++ b/solution.py
@@ -15,7 +15,8 @@
 
 def ctx_order(shards):
     middle = shards // 2
-    return [middle] + [shard for shard in range(shards) if shard != middle]
+    others = [shard for shard in range(shards) if shard != middle]
+    return [middle] + sorted(others, key=lambda shard: -abs(shard - middle))
 
 
 def pitches(lines):

time: 36.2 us -> 36.2 us (level)
  no operation moved by 1% of the time
where the time goes in v10:
time: 36.2 us; the launch traced here: 35.9 us
  blocking collectives  11.9 us (33%)
  starting transfers between devices  11.7 us (32%)
  Pallas kernels  5.4 us (15%)
  waiting for transfers between devices  4.09 us (11%)
  local copies, waits for them, and re-layouts  2.65 us (7%)
    all_to_all x1, blocking collectives, body(): lax.all_to_all(convolved.reshape(shards * chips, channels // shards, seq_...  11.9 us
    all_to_all x1, starting transfers between devices, body(): lax.all_to_all(pieces, 'ctx', split_axis=0, concat_axis=0, tiled=True, ax...  6.25 us
    ppermute x5, starting transfers between devices, exchange(): lax.ppermute(array, 'tp', [(i, partner(i, step, tp)) for i in range(tp)])  5.47 us
    ppermute x5, waiting for transfers between devices, exchange(): lax.ppermute(array, 'tp', [(i, partner(i, step, tp)) for i in range(tp)])  2.87 us
    dynamic_slice x1, local copies, waits for them, and re-layouts, body(): lax.dynamic_slice_in_dim(w_out, partner(me, step, tp) * feats, feats, 1)  2.51 us
    pallas_call x1, Pallas kernels, prepare(): pl.pallas_call(prepare_kernel, out_shape=[pltpu.VMEM((shards, 2, channels...  1.99 us
    pallas_call x1, Pallas kernels, convolve(): pl.pallas_call(conv_kernel, out_shape=jax.ShapeDtypeStruct((blocks, copie...  1.56 us
    all_to_all x1, waiting for transfers between devices, body(): lax.all_to_all(pieces, 'ctx', split_axis=0, concat_axis=0, tiled=True, ax...  1.22 us
  transfers between devices with their start and end apart: 6, of which 3 were waited for; matrix products, arithmetic and copies ran while one was open for 7% of the time, Pallas kernels for 12%

profile of v10, /device:TPU:0, one launch (start us, length us, event | category | flops | bytes accessed | tf_op | source)
XLA Modules:
  0.0 35.9 jit_solution(1364020301099247622)
XLA Ops:
  0.0 3.0 %collective-permute-start = (bf16[256,256]{1,0:T(8,128)(2,1)}, bf16[256,256]{1,0:T(8,128)(2,1)S(1)}, u32[]{:S(2)}, u32[]{:S(2)}) collective-permute-start(bf16[256,256]{1,0:T(8,128)(2,1)} %refs_0_.1), channel_id=1, source_target_pairs={{0,2},{1,3},{2,0},{3,1},{4,6},{5,7},{6,4},{7,5},{8,10},{9,11},{10,... | collective-permute-start | bytes 393224 | tf_op jit(solution)/shard_map/ppermute | solution.py:290
  3.0 2.0 %prepare.1 = (bf16[8,2,32,256]{3,2,1,0:T(8,128)(2,1)}, bf16[256,1024]{1,0:T(8,128)(2,1)S(1)}) custom-call(bf16[256,256]{1,0:T(8,128)(2,1)} %key_ref.1, bf16[256,256]{1,0:T(8,128)(2,1)} %value_ref.1, f32[256,256]{1,0:T(8,128)} %taps_ref.1, bf16[256,4096]{1,0:T(8,128)(2,1)} %w_ref.1), custom_call_target="tpu_custom_call" | custom-call | flops 65536 | bytes 4194304 | tf_op jit(solution)/shard_map/prepare/pallas_call | solution.py:174
  5.0 0.0 copy-start.1
  5.0 0.1 collective-permute-start.1
  5.1 2.0 %collective-permute-done.refs_1_ = bf16[256,256]{1,0:T(8,128)(2,1)S(1)} collective-permute-done((bf16[256,256]{1,0:T(8,128)(2,1)}, bf16[256,256]{1,0:T(8,128)(2,1)S(1)}, u32[]{:S(2)}, u32[]{:S(2)}) %collective-permute-start) | collective-permute-done | bytes 131104 | tf_op jit(solution)/shard_map/ppermute | solution.py:290
  7.0 6.2 %all-to-all-start = ((bf16[8,2,32,256]{3,2,1,0:T(8,128)(2,1)}), bf16[8,2,32,256]{3,2,1,0:T(8,128)(2,1)S(1)}, u32[]{:S(2)}, u32[]{:S(2)}) async-start(bf16[8,2,32,256]{3,2,1,0:T(8,128)(2,1)} %get-tuple-element.19), calls=%async_computation | async-start | bytes 524288 | tf_op jit(solution)/shard_map/all_to_all | solution.py:301
  13.3 0.0 copy-start
  13.3 2.5 %constant_dynamic-slice_fusion = (bf16[256,1024]{1,0:T(8,128)(2,1)}, bf16[256,1024]{1,0:T(8,128)(2,1)S(1)}, bf16[256,1024]{1,0:T(8,128)(2,1)}) fusion(bf16[256,4096]{1,0:T(8,128)(2,1)} %w_ref.1, s32[]{:T(128)S(6)} %select_n.44, s32[]{:T(128)S(6)} %select_n.37, s32[]{:T(128)S(6)} %select_n.42), kind=kLoop, calls=%fused_computation | loop fusion | bytes 3145740 | tf_op jit(solution)/shard_map/dynamic_slice | solution.py:294
  15.8 0.0 collective-permute-start.3
  15.8 2.4 %collective-permute-start.2 = (bf16[256,1024]{1,0:T(8,128)(2,1)}, bf16[256,1024]{1,0:T(8,128)(2,1)S(1)}, u32[]{:S(2)}, u32[]{:S(2)}) collective-permute-start(bf16[256,1024]{1,0:T(8,128)(2,1)} %get-tuple-element.33), channel_id=1, source_target_pairs={{0,1},{1,0},{2,3},{3,2},{4,5},{5,4},{6,7},{7,6},{8,9},{9,8},{10,11... | collective-permute-start | bytes 1572872 | tf_op jit(solution)/shard_map/ppermute | solution.py:290
  18.1 0.0 copy-done.1
  18.1 0.1 copy.7.bias_ref
  18.3 1.2 %all-to-all-done.x_ref = bf16[8,2,32,256]{3,2,1,0:T(8,128)(2,1)S(1)} async-done(((bf16[8,2,32,256]{3,2,1,0:T(8,128)(2,1)}), bf16[8,2,32,256]{3,2,1,0:T(8,128)(2,1)S(1)}, u32[]{:S(2)}, u32[]{:S(2)}) %all-to-all-start) | async-done | bytes 262176 | tf_op jit(solution)/shard_map/all_to_all | solution.py:301
  19.5 1.6 %toeplitz_conv.1 = bf16[8,2,32,256]{3,2,1,0:T(8,128)(2,1)S(1)} custom-call(bf16[8,2,32,256]{3,2,1,0:T(8,128)(2,1)S(1)} %all-to-all-done.x_ref, f32[256,1]{1,0:T(8,128)S(1)} %copy.7.bias_ref), custom_call_target="tpu_custom_call" | custom-call | flops 1 | bytes 1 | tf_op jit(solution)/shard_map/toeplitz_conv/pallas_call | solution.py:109
  21.1 0.0 collective-permute-done.1.refs_1_
  21.1 11.9 %all_to_all.10 = bf16[16,32,256]{2,1,0:T(8,128)(2,1)S(1)} all-to-all(bf16[16,32,256]{2,1,0:T(8,128)(2,1)S(1)} %bitcast.4), channel_id=1, replica_groups={{18,16,2,0,6,4,30,28,10,8,26,24,14,12,22,20},{19,17,3,1,7,5,31,29,11,9,..., dimensions={0} | all-to-all | bytes 524288 | tf_op jit(solution)/shard_map/all_to_all | solution.py:305
  33.0 0.0 copy-done
  33.0 0.1 gate.1.gated_ref
  33.1 0.0 collective-permute-done.3.refs_3_
  33.1 0.0 collective-permute-done.2.refs_2_
  33.1 0.1 collective-permute-start.4
  33.2 0.6 %project_own.1 = (f32[1024,256]{1,0:T(8,128)S(1)}, bf16[1024,512]{1,0:T(8,128)(2,1)S(1)}) custom-call(bf16[512,256]{1,0:T(8,128)(2,1)S(1)} %gate.1.gated_ref, bf16[256,1024]{1,0:T(8,128)(2,1)S(1)} %get-tuple-element.25.refs_0_, bf16[256,1024]{1,0:T(8,128)(2,1)S(1)} %collective-permute-done.1.refs_1_, bf16[256,1024]{1,0:T(8,128)(2,1)S(1)} %collective-permute-done.2.refs_2_, ...), custom_call_target="tpu_custom_call" | custom-call | flops 268435456 | bytes 1310720 | tf_op jit(solution)/shard_map/project_own/pallas_call | solution.py:257
  33.8 0.9 %collective-permute-done.4.gated_ref = bf16[512,256]{1,0:T(8,128)(2,1)S(1)} collective-permute-done((bf16[512,256]{1,0:T(8,128)(2,1)S(1)}, bf16[512,256]{1,0:T(8,128)(2,1)S(1)}, u32[]{:S(2)}, u32[]{:S(2)}) %collective-permute-start.4) | collective-permute-done | bytes 262176 | tf_op jit(solution)/shard_map/ppermute | solution.py:290
  34.7 1.2 %project_other.1 = bf16[1024,256]{1,0:T(8,128)(2,1)} custom-call(bf16[512,256]{1,0:T(8,128)(2,1)S(1)} %collective-permute-done.4.gated_ref, f32[1024,256]{1,0:T(8,128)S(1)} %get-tuple-element.29.sum_ref, bf16[1024,512]{1,0:T(8,128)(2,1)S(1)} %get-tuple-element.30.turned_ref), custom_call_target="tpu_custom_call" | custom-call | flops 268435456 | bytes 1310720 | tf_op jit(solution)/shard_map/project_other/pallas_call | solution.py:269
Async XLA Ops:
  0.0 7.0 %collective-permute-start = (bf16[256,256]{1,0:T(8,128)(2,1)}, bf16[256,256]{1,0:T(8,128)(2,1)S(1)}, u32[]{:S(2)}, u32[]{:S(2)}) collective-permute-start(bf16[256,256]{1,0:T(8,128)(2,1)} %refs_0_.1), channel_id=1, source_target_pairs={{0,2},{1,3},{2,0},{3,1},{4,6},{5,7},{6,4},{7,5},{8,10},{9,11},{10,... | collective-permute-start | bytes 393224 | tf_op jit(solution)/shard_map/ppermute | solution.py:290
  5.0 13.2 %copy-start.1 = (f32[256]{0:T(256)S(1)}, f32[256]{0:T(256)}, u32[]{:S(2)}) copy-start(f32[256]{0:T(256)} %param.10) | copy-start | bytes 3076
  5.0 16.1 %collective-permute-start.1 = (bf16[256,1024]{1,0:T(8,128)(2,1)S(1)}, bf16[256,1024]{1,0:T(8,128)(2,1)S(1)}, u32[]{:S(2)}, u32[]{:S(2)}) collective-permute-start(bf16[256,1024]{1,0:T(8,128)(2,1)S(1)} %get-tuple-element.20), channel_id=1, source_target_pairs={{0,2},{1,3},{2,0},{3,1},{4,6},{5,7},{6,4},{7,5},{8,10},{9,11},{10,... | collective-permute-start | bytes 1572872 | tf_op jit(solution)/shard_map/ppermute | solution.py:290
  7.0 12.5 %all-to-all-start = ((bf16[8,2,32,256]{3,2,1,0:T(8,128)(2,1)}), bf16[8,2,32,256]{3,2,1,0:T(8,128)(2,1)S(1)}, u32[]{:S(2)}, u32[]{:S(2)}) async-start(bf16[8,2,32,256]{3,2,1,0:T(8,128)(2,1)} %get-tuple-element.19), calls=%async_computation | async-start | bytes 524288 | tf_op jit(solution)/shard_map/all_to_all | solution.py:301
  13.3 19.8 %copy-start = (bf16[256,256]{1,0:T(8,128)(2,1)S(1)}, bf16[256,256]{1,0:T(8,128)(2,1)}, u32[]{:S(2)}) copy-start(bf16[256,256]{1,0:T(8,128)(2,1)} %refs_0_.1) | copy-start | bytes 393220
  15.8 17.3 %collective-permute-start.3 = (bf16[256,1024]{1,0:T(8,128)(2,1)}, bf16[256,1024]{1,0:T(8,128)(2,1)S(1)}, u32[]{:S(2)}, u32[]{:S(2)}) collective-permute-start(bf16[256,1024]{1,0:T(8,128)(2,1)} %get-tuple-element.31), channel_id=1, source_target_pairs={{0,3},{1,2},{2,1},{3,0},{4,7},{5,6},{6,5},{7,4},{8,11},{9,10},{10,... | collective-permute-start | bytes 1572872 | tf_op jit(solution)/shard_map/ppermute | solution.py:290
  15.8 17.3 %collective-permute-start.2 = (bf16[256,1024]{1,0:T(8,128)(2,1)}, bf16[256,1024]{1,0:T(8,128)(2,1)S(1)}, u32[]{:S(2)}, u32[]{:S(2)}) collective-permute-start(bf16[256,1024]{1,0:T(8,128)(2,1)} %get-tuple-element.33), channel_id=1, source_target_pairs={{0,1},{1,0},{2,3},{3,2},{4,5},{5,4},{6,7},{7,6},{8,9},{9,8},{10,11... | collective-permute-start | bytes 1572872 | tf_op jit(solution)/shard_map/ppermute | solution.py:290
  33.1 1.6 %collective-permute-start.4 = (bf16[512,256]{1,0:T(8,128)(2,1)S(1)}, bf16[512,256]{1,0:T(8,128)(2,1)S(1)}, u32[]{:S(2)}, u32[]{:S(2)}) collective-permute-start(bf16[512,256]{1,0:T(8,128)(2,1)S(1)} %gate.1.gated_ref), channel_id=1, source_target_pairs={{0,1},{1,0},{2,3},{3,2},{4,5},{5,4},{6,7},{7,6},{8,9},{9,8},{10,11... | collective-permute-start | bytes 786440 | tf_op jit(solution)/shard_map/ppermute | solution.py:290
